TPU v7x, 32 devices: a whole 2x2x4 slice. The times are simulated.
32 devices in a mesh: dp: 8 (over z, y), block: 4 (over x, core).
Axes of the slice: x: 2, y: 2, z: 4, core: 2. Of those that a mesh axis runs over, the one named last changes fastest.
Arguments:
- block_in: bfloat16 [8, 1024, 1024], P('dp', 'block'), may hold values from -6 to 6
- doc_starts: int32 [8, 4], P('dp'), may hold values from 0 to 1023, as said below
- norm1_gain: float32 [1024], replicated, may hold values from 0.5 to 1.5
- norm1_bias: float32 [1024], replicated, may hold values from -1.25 to 1.25
- w_in: bfloat16 [1024, 3072], P(None, 'dp'), may hold values from -0.1875 to 0.1875
- b_in: float32 [3072], replicated, may hold values from -1.25 to 1.25
- short_taps: float32 [3, 3072], replicated, may hold values from -3 to 3
- short_bias: float32 [3072], replicated, may hold values from -1.25 to 1.25
- filter_w1: float32 [33, 64], replicated, may hold values from -1 to 1
- filter_b1: float32 [64], replicated, may hold values from -6 to 6
- filter_w2: float32 [64, 64], replicated, may hold values from -0.75 to 0.75
- filter_b2: float32 [64], replicated, may hold values from -6 to 6
- filter_w3: float32 [64, 1024], replicated, may hold values from -0.0234375 to 0.0234375
- filter_decay: float32 [1024], replicated, may hold values from 0.5 to 25
- conv_bias: float32 [1024], replicated, may hold values from -6 to 6
- w_out: bfloat16 [1024, 1024], P(None, 'dp'), may hold values from -0.1875 to 0.1875
- b_out: float32 [1024], replicated, may hold values from -1.25 to 1.25
- norm2_gain: float32 [1024], replicated, may hold values from 0.5 to 1.5
- norm2_bias: float32 [1024], replicated, may hold values from -1.25 to 1.25
- w_up: bfloat16 [1024, 4096], P(None, 'dp'), may hold values from -0.1875 to 0.1875
- b_up: float32 [4096], replicated, may hold values from -1.25 to 1.25
- w_down: bfloat16 [4096, 1024], P(None, 'dp'), may hold values from -0.09375 to 0.09375
- b_down: float32 [1024], replicated, may hold values from -1.25 to 1.25
- cotangent: bfloat16 [8, 1024, 1024], P('dp', 'block'), may hold values from -6 to 6
Outputs:
- block_out: bfloat16 [8, 1024, 1024], P('dp', 'block')
- grad_in: float32 [8, 1024, 1024], P('dp', 'block')
- grad_norm1_gain: float32 [1024], replicated
- grad_norm1_bias: float32 [1024], replicated
- grad_w_in: float32 [1024, 3072], P(None, 'dp')
- grad_b_in: float32 [3072], replicated
- grad_short_taps: float32 [3, 3072], replicated
- grad_short_bias: float32 [3072], replicated
- grad_filter_w1: float32 [33, 64], replicated
- grad_filter_b1: float32 [64], replicated
- grad_filter_w2: float32 [64, 64], replicated
- grad_filter_b2: float32 [64], replicated
- grad_filter_w3: float32 [64, 1024], replicated
- grad_filter_decay: float32 [1024], replicated
- grad_conv_bias: float32 [1024], replicated
- grad_w_out: float32 [1024, 1024], P(None, 'dp')
- grad_b_out: float32 [1024], replicated
- grad_norm2_gain: float32 [1024], replicated
- grad_norm2_bias: float32 [1024], replicated
- grad_w_up: float32 [1024, 4096], P(None, 'dp')
- grad_b_up: float32 [4096], replicated
- grad_w_down: float32 [4096, 1024], P(None, 'dp')
- grad_b_down: float32 [1024], replicated
Inputs may be any that keep to these rules, and one draw needn't show every extreme that they name: `doc_starts`: in each row the starts rise strictly from 0; one document begins within the first 256 positions and ends within the last 256.
All inputs are finite; a program needn't handle non-finite values.
Results may differ from a plain program's by a relative error of at most 0.0096.
Values may be sent and summed in bfloat16 or wider, within the bound.
No kernel may reach another device: no remote copies, remote signals or barrier semaphores. Data moves between devices by JAX's collectives and lax.ppermute only.
A program may use at most 448 MiB of HBM per device.

v0:
```python
import math

import jax
import jax.numpy as jnp
from jax import lax
from jax.sharding import PartitionSpec as P

EPSILON = 1e-05
MOD_SHIFT = 0.05
HIGHEST = lax.Precision.HIGHEST


def from_behind(value, axis, steps):
    count = lax.axis_size(axis)
    initial, last = (max(0, -steps), min(count, count - steps))
    return lax.ppermute(value, axis, [(source, source + steps) for source in range(initial, last)])


def dot_high(left, right):
    return jnp.dot(left, right, precision=HIGHEST, preferred_element_type=jnp.float32)


def dot_first(left, right):
    return lax.dot_general(
        left, right, (((0,), (0,)), ((), ())), preferred_element_type=jnp.float32
    )


def dot_last(left, right):
    return lax.dot_general(
        left, right, (((1,), (1,)), ((), ())), preferred_element_type=jnp.float32
    )


def layer_norm(values, gain, bias):
    mean = jnp.mean(values, axis=-1, keepdims=True)
    centered = values - mean
    variance = jnp.mean(centered * centered, axis=-1, keepdims=True)
    return centered * lax.rsqrt(variance + EPSILON) * gain + bias


def exact_gelu(values):
    return jax.nn.gelu(values, approximate=False)


def position_table(length, emb_dim):
    bands = (emb_dim - 1) // 2
    sample = jnp.arange(length).astype(jnp.float32)
    times = sample / (length - 1)
    frequency = jnp.linspace(0.0001, bands - 1, bands).astype(jnp.float32)
    angle = 2.0 * math.pi * sample[:, None] * frequency[None, :] / length
    return (jnp.concatenate([times[:, None], jnp.cos(angle), -jnp.sin(angle)], axis=1), times)


def long_filter(length, first_w, first_b, second_w, second_b, third_w, rates):
    table, times = position_table(length, first_w.shape[0])
    first = jnp.sin(dot_high(table, first_w) + first_b)
    second = jnp.sin(dot_high(first, second_w) + second_b)
    return dot_high(second, third_w) * (jnp.exp(-times[:, None] * rates[None, :]) + MOD_SHIFT)


def segment_ids(doc_starts, length):
    positions = jnp.arange(length, dtype=jnp.int32)
    return jnp.sum((doc_starts[..., None, :] <= positions[:, None]).astype(jnp.int32), axis=-1) - 1


def transform_tables(block_len):
    span = 2 * block_len
    frequency = jnp.arange(block_len, dtype=jnp.int32)
    sample = jnp.arange(block_len, dtype=jnp.int32)
    is_zero = (frequency == 0)[:, None]
    turns = frequency[:, None] * sample[None, :] % span
    angle = 2.0 * math.pi * turns.astype(jnp.float32) / span
    alternate = jnp.where(sample % 2 == 0, 1.0, -1.0).astype(jnp.float32)
    real_rows = jnp.cos(angle)
    imag_rows = jnp.where(is_zero, alternate[None, :], -jnp.sin(angle))
    forward_table = jnp.concatenate([real_rows, imag_rows], axis=0)
    outputs = sample + block_len
    out_turns = outputs[:, None] * frequency[None, :] % span
    out_angle = 2.0 * math.pi * out_turns.astype(jnp.float32) / span
    out_alternate = jnp.where(outputs % 2 == 0, 1.0, -1.0).astype(jnp.float32)
    zero_col = (frequency == 0)[None, :]
    real_cols = jnp.where(zero_col, 1.0, 2.0) * jnp.cos(out_angle) / span
    imag_cols = jnp.where(zero_col, out_alternate[:, None] / span, -2.0 * jnp.sin(out_angle) / span)
    inverse_table = jnp.concatenate([real_cols, imag_cols], axis=1)
    parity = jnp.where(frequency % 2 == 0, 1.0, -1.0).astype(jnp.float32)
    nyquist_sign = 1.0
    sign = jnp.concatenate([parity, jnp.where(frequency == 0, nyquist_sign, parity)])
    edge = (frequency == 0).astype(jnp.float32)[:, None]
    return (forward_table, inverse_table, sign, edge)


def spectral_product(left, right, edge):
    half = left.shape[-2] // 2
    left_re, left_im = (left[..., :half, :], left[..., half:, :])
    right_re, right_im = (right[..., :half, :], right[..., half:, :])
    inside = 1.0 - edge
    out_re = left_re * right_re - inside * left_im * right_im
    out_im = inside * (left_re * right_im + left_im * right_re) + edge * left_im * right_im
    return jnp.concatenate([out_re, out_im], axis=-2)


def spectral_back(grad, other, edge):
    half = grad.shape[-2] // 2
    grad_re, grad_im = (grad[..., :half, :], grad[..., half:, :])
    other_re, other_im = (other[..., :half, :], other[..., half:, :])
    inside = 1.0 - edge
    back_re = grad_re * other_re + inside * grad_im * other_im
    back_im = inside * (grad_im * other_re - grad_re * other_im) + edge * grad_im * other_im
    return jnp.concatenate([back_re, back_im], axis=-2)


def local(
    block_in,
    doc_starts,
    norm1_gain,
    norm1_bias,
    w_in,
    b_in,
    short_taps,
    short_bias,
    filter_w1,
    filter_b1,
    filter_w2,
    filter_b2,
    filter_w3,
    filter_decay,
    conv_bias,
    w_out,
    b_out,
    norm2_gain,
    norm2_bias,
    w_up,
    b_up,
    w_down,
    b_down,
    cotangent,
):
    rows, block_len, width = block_in.shape
    blocks = lax.axis_size("block")
    place = lax.axis_index("block")
    length = block_len * blocks
    span = 2 * block_len
    tokens = rows * block_len
    num_docs = doc_starts.shape[1]
    full_in, full_out, full_up, full_down = (
        lax.all_gather(w_in, "dp", axis=1, tiled=True),
        lax.all_gather(w_out, "dp", axis=1, tiled=True),
        lax.all_gather(w_up, "dp", axis=1, tiled=True),
        lax.all_gather(w_down, "dp", axis=1, tiled=True),
    )
    forward_table, inverse_table, sign, edge = transform_tables(block_len)
    segment = segment_ids(doc_starts, length)
    keep_one_all = jnp.concatenate(
        [jnp.zeros((rows, 1), jnp.bool_), segment[:, 1:] == segment[:, :-1]], axis=1
    )
    keep_two_all = jnp.concatenate(
        [jnp.zeros((rows, 2), jnp.bool_), segment[:, 2:] == segment[:, :-2]], axis=1
    )
    offset = place * block_len
    local_segment = lax.dynamic_slice_in_dim(segment, offset, block_len, 1)
    keep_one = lax.dynamic_slice_in_dim(keep_one_all, offset, block_len, 1).astype(jnp.float32)[
        ..., None
    ]
    keep_two = lax.dynamic_slice_in_dim(keep_two_all, offset, block_len, 1).astype(jnp.float32)[
        ..., None
    ]
    heads = segment[:, ::block_len]
    tails = segment[:, block_len - 1 :: block_len]
    head_here = lax.dynamic_index_in_dim(heads, place, 1, keepdims=False)
    tail_here = lax.dynamic_index_in_dim(tails, place, 1, keepdims=False)
    doc_ids = jnp.arange(num_docs, dtype=jnp.int32)
    doc_mask = (local_segment[:, None, :] == doc_ids[None, :, None]).astype(jnp.float32)[..., None]
    head_pick = (doc_ids[None, :] == head_here[:, None]).astype(jnp.float32)[:, :, None, None]
    tail_pick = (doc_ids[None, :] == tail_here[:, None]).astype(jnp.float32)[:, :, None, None]
    inputs = block_in.astype(jnp.float32).reshape(tokens, width)
    normed, norm1_back = jax.vjp(layer_norm, inputs, norm1_gain, norm1_bias)
    normed_low = normed.astype(jnp.bfloat16)
    proj = (jnp.dot(normed_low, full_in, preferred_element_type=jnp.float32) + b_in).reshape(
        rows, block_len, 3 * width
    )
    rim_rows = from_behind(proj[:, block_len - 2 :], "block", 1)
    extended = jnp.concatenate([rim_rows, proj], axis=1)
    prev_one = extended[:, 1 : block_len + 1]
    prev_two = extended[:, :block_len]
    short = (
        short_bias
        + short_taps[0] * proj
        + short_taps[1] * prev_one * keep_one
        + short_taps[2] * prev_two * keep_two
    )
    gate_part = short[..., :width]
    mult = short[..., width : 2 * width]
    value = short[..., 2 * width :]
    inner = value * mult

    def filter_spectra(params):
        kernel = long_filter(
            length, params[0], params[1], params[2], params[3], params[4], params[5]
        )
        pieces = kernel.reshape(blocks, block_len, width)
        halves = jnp.einsum(
            "fn,jnw->jfw",
            forward_table,
            pieces,
            precision=HIGHEST,
            preferred_element_type=jnp.float32,
        )
        earlier = jnp.concatenate([jnp.zeros_like(halves[:1]), halves[:-1]], axis=0)
        return earlier + sign[None, :, None] * halves

    spectra, filter_back = jax.vjp(
        filter_spectra, (filter_w1, filter_b1, filter_w2, filter_b2, filter_w3, filter_decay)
    )
    zero_lag = spectra[0]
    masked = doc_mask * inner[:, None]
    own_spec = jnp.einsum(
        "fn,rdnw->rdfw",
        forward_table,
        masked,
        precision=HIGHEST,
        preferred_element_type=jnp.float32,
    )
    tail_spec = jnp.sum(tail_pick * own_spec, axis=1)
    local_prod = spectral_product(own_spec, zero_lag, edge)

    def cross_term(carry, spec, source):
        lag = jnp.clip(place - source, 0, blocks - 1)
        tail_there = lax.dynamic_index_in_dim(tails, source, 1, keepdims=False)
        factor = ((source < place) & (tail_there == head_here)).astype(jnp.float32)[:, None, None]
        kernel_spec = lax.dynamic_index_in_dim(spectra, lag, 0, keepdims=False)
        return carry + factor * spectral_product(spec, kernel_spec, edge)

    start_cross = jnp.zeros((rows, span, width), jnp.float32)
    piece = lax.all_gather(tail_spec[None], "block", axis=0, tiled=True)

    def advance(number, accum):
        item = lax.dynamic_index_in_dim(piece, number, 0, keepdims=False)
        return cross_term(accum, item, number)

    cross = lax.fori_loop(0, piece.shape[0], advance, start_cross)
    totals = local_prod + head_pick * cross[:, None]
    conv_docs = jnp.einsum(
        "tf,rdfw->rdtw",
        inverse_table,
        totals,
        precision=HIGHEST,
        preferred_element_type=jnp.float32,
    )
    mixed = jnp.sum(doc_mask * conv_docs, axis=1) + conv_bias * inner
    gated_low = (gate_part * mixed).astype(jnp.bfloat16).reshape(tokens, width)
    branch = jnp.dot(gated_low, full_out, preferred_element_type=jnp.float32) + b_out
    resid = inputs + branch
    normed2, norm2_back = jax.vjp(layer_norm, resid, norm2_gain, norm2_bias)
    normed2_low = normed2.astype(jnp.bfloat16)
    hidden = jnp.dot(normed2_low, full_up, preferred_element_type=jnp.float32) + b_up
    act, gelu_back = jax.vjp(exact_gelu, hidden)
    act_low = act.astype(jnp.bfloat16)
    output = resid + jnp.dot(act_low, full_down, preferred_element_type=jnp.float32) + b_down
    block_out = output.astype(jnp.bfloat16).reshape(rows, block_len, width)
    cot_flat = cotangent.reshape(tokens, width)
    grad_down = dot_first(act_low, cot_flat)
    grad_b_down = jnp.sum(cot_flat.astype(jnp.float32), axis=0)
    grad_act = dot_last(cot_flat, full_down)
    grad_hidden = gelu_back(grad_act)[0].astype(jnp.bfloat16)
    grad_up = dot_first(normed2_low, grad_hidden)
    grad_b_up = jnp.sum(grad_hidden.astype(jnp.float32), axis=0)
    grad_normed2 = dot_last(grad_hidden, full_up)
    resid_part, grad_gain_two, grad_bias_two = norm2_back(grad_normed2)
    grad_resid = cot_flat.astype(jnp.float32) + resid_part
    grad_branch = grad_resid.astype(jnp.bfloat16)
    grad_out = dot_first(gated_low, grad_branch)
    grad_b_out = jnp.sum(grad_branch.astype(jnp.float32), axis=0)
    grad_gated = dot_last(grad_branch, full_out).reshape(rows, block_len, width)
    grad_gate_part = grad_gated * mixed
    grad_mixed = grad_gated * gate_part
    grad_conv_bias = jnp.sum(grad_mixed * inner, axis=(0, 1))
    doc_grad = doc_mask * grad_mixed[:, None]
    grad_totals = jnp.einsum(
        "tf,rdtw->rdfw",
        inverse_table,
        doc_grad,
        precision=HIGHEST,
        preferred_element_type=jnp.float32,
    )
    grad_own = spectral_back(grad_totals, zero_lag, edge)
    lag_zero = jnp.sum(spectral_back(grad_totals, own_spec, edge), axis=(0, 1))

    def back_term(carry, spec, source):
        grad_tail, grad_lags = carry
        lag = jnp.clip(source - place, 0, blocks - 1)
        head_there = lax.dynamic_index_in_dim(heads, source, 1, keepdims=False)
        factor = ((source > place) & (head_there == tail_here)).astype(jnp.float32)[:, None, None]
        kernel_spec = lax.dynamic_index_in_dim(spectra, lag, 0, keepdims=False)
        scaled = factor * spec
        grad_tail = grad_tail + spectral_back(scaled, kernel_spec, edge)
        current = lax.dynamic_index_in_dim(grad_lags, lag, 0, keepdims=False)
        renewed = current + jnp.sum(spectral_back(scaled, tail_spec, edge), axis=0)
        grad_lags = lax.dynamic_update_index_in_dim(grad_lags, renewed, lag, 0)
        return (grad_tail, grad_lags)

    start_back = (
        jnp.zeros((rows, span, width), jnp.float32),
        jnp.zeros((blocks, span, width), jnp.float32),
    )
    head_grad = jnp.sum(head_pick * grad_totals, axis=1)
    fold_piece = lax.all_gather(head_grad[None], "block", axis=0, tiled=True)

    def advance(number, accum):
        item = lax.dynamic_index_in_dim(fold_piece, number, 0, keepdims=False)
        return back_term(accum, item, number)

    grad_tail, grad_lags = lax.fori_loop(0, fold_piece.shape[0], advance, start_back)
    grad_lags = jnp.concatenate([grad_lags[:1] + lag_zero[None], grad_lags[1:]], axis=0)
    filter_grads = filter_back(grad_lags)[0]
    grad_own = grad_own + tail_pick * grad_tail[:, None]
    grad_masked = jnp.einsum(
        "fn,rdfw->rdnw",
        forward_table,
        grad_own,
        precision=HIGHEST,
        preferred_element_type=jnp.float32,
    )
    grad_inner = jnp.sum(doc_mask * grad_masked, axis=1) + conv_bias * grad_mixed
    grad_short = jnp.concatenate([grad_gate_part, grad_inner * value, grad_inner * mult], axis=-1)
    grad_taps = jnp.stack(
        [
            jnp.sum(grad_short * proj, axis=(0, 1)),
            jnp.sum(grad_short * prev_one * keep_one, axis=(0, 1)),
            jnp.sum(grad_short * prev_two * keep_two, axis=(0, 1)),
        ],
        axis=0,
    )
    grad_short_bias = jnp.sum(grad_short, axis=(0, 1))
    pass_one = grad_short * keep_one
    pass_two = grad_short * keep_two
    three_width = 3 * width
    grad_proj = (
        short_taps[0] * grad_short
        + short_taps[1]
        * jnp.concatenate([pass_one[:, 1:], jnp.zeros((rows, 1, three_width), jnp.float32)], axis=1)
        + short_taps[2]
        * jnp.concatenate([pass_two[:, 2:], jnp.zeros((rows, 2, three_width), jnp.float32)], axis=1)
    )
    to_previous = jnp.concatenate(
        [
            short_taps[2] * pass_two[:, :1],
            short_taps[1] * pass_one[:, :1] + short_taps[2] * pass_two[:, 1:2],
        ],
        axis=1,
    )
    incoming = from_behind(to_previous, "block", -1)
    grad_proj = grad_proj + jnp.concatenate(
        [jnp.zeros((rows, block_len - 2, three_width), jnp.float32), incoming], axis=1
    )
    grad_proj_low = grad_proj.reshape(tokens, three_width).astype(jnp.bfloat16)
    grad_in_weight = dot_first(normed_low, grad_proj_low)
    grad_b_in = jnp.sum(grad_proj_low.astype(jnp.float32), axis=0)
    grad_normed = dot_last(grad_proj_low, full_in)
    input_part, grad_gain_one, grad_bias_one = norm1_back(grad_normed)
    grad_input = (grad_resid + input_part).reshape(rows, block_len, width)
    summed = lax.psum(
        (
            grad_gain_one,
            grad_bias_one,
            grad_b_in,
            grad_taps,
            grad_short_bias,
            filter_grads[0],
            filter_grads[1],
            filter_grads[2],
            filter_grads[3],
            filter_grads[4],
            filter_grads[5],
            grad_conv_bias,
            grad_b_out,
            grad_gain_two,
            grad_bias_two,
            grad_b_up,
            grad_b_down,
        ),
        ("dp", "block"),
    )
    column_parts = (
        lax.psum_scatter(grad_in_weight, "dp", scatter_dimension=1, tiled=True),
        lax.psum_scatter(grad_out, "dp", scatter_dimension=1, tiled=True),
        lax.psum_scatter(grad_up, "dp", scatter_dimension=1, tiled=True),
        lax.psum_scatter(grad_down, "dp", scatter_dimension=1, tiled=True),
    )
    large = lax.psum((column_parts[0], column_parts[1], column_parts[2], column_parts[3]), "block")
    return (
        block_out,
        grad_input,
        summed[0],
        summed[1],
        large[0],
        summed[2],
        summed[3],
        summed[4],
        summed[5],
        summed[6],
        summed[7],
        summed[8],
        summed[9],
        summed[10],
        summed[11],
        large[1],
        summed[12],
        summed[13],
        summed[14],
        large[2],
        summed[15],
        large[3],
        summed[16],
    )


def solution(mesh):
    placed = (
        P("dp", "block", None),
        P("dp", None),
        P(),
        P(),
        P(None, "dp"),
        P(),
        P(),
        P(),
        P(),
        P(),
        P(),
        P(),
        P(),
        P(),
        P(),
        P(None, "dp"),
        P(),
        P(),
        P(),
        P(None, "dp"),
        P(),
        P(None, "dp"),
        P(),
        P("dp", "block", None),
    )
    return jax.shard_map(
        local,
        mesh=mesh,
        in_specs=placed,
        out_specs=(
            P("dp", "block", None),
            P("dp", "block", None),
            P(),
            P(),
            P(None, "dp"),
            P(),
            P(),
            P(),
            P(),
            P(),
            P(),
            P(),
            P(),
            P(),
            P(),
            P(None, "dp"),
            P(),
            P(),
            P(),
            P(None, "dp"),
            P(),
            P(None, "dp"),
            P(),
        ),
        check_vma=False,
    )
```

profile of v0, /device:TPU:1, one launch (start us, length us, event | category | flops | bytes accessed | tf_op | source)
XLA Modules:
  0.0 1914.3 jit_solution(4257959086279586007)
XLA Ops:
  17.9 93.8 %all-gather.9.cloned.1.call-done = bf16[1024,3072]{1,0:T(8,128)(2,1)} async-done(((bf16[1024,384]{1,0:T(8,128)(2,1)}), bf16[1024,3072]{1,0:T(8,128)(2,1)}) %all-gather.9.cloned.1.call-update) | async-done | bytes 6291472 | tf_op jit(solution)/shard_map/all_gather | solution.py:147
  124.9 12.9 multiply_reduce_fusion.1
  151.8 14.2 convolution_bitcast_fusion
  169.3 8.7 multiply_add_fusion.5
  178.0 8.7 copy.90
  197.1 41.4 %while.32 = (s32[]{:T(128)}, f32[1,512,1024]{2,1,0:T(8,128)}, s32[]{:T(128)}, s32[1,4]{1,0:T(1,128)S(1)}, s32[1]{0:T(128)}, /*index=5*/f32[4,1,512,1024]{3,2,1,0...) while((s32[]{:T(128)}, f32[1,512,1024]{2,1,0:T(8,128)}, ...), condition=%wide.region_5.6_spmd.clone.clone, body=%wide.region_4.5_spmd.clone.clone.sunk | while | flops 4982027 | bytes 16781540 | solution.py:241
  238.5 17.7 fusion.31
  265.2 108.1 %all-gather.13.cloned.1.call-done = bf16[1024,4096]{1,0:T(8,128)(2,1)} async-done(((bf16[1024,512]{1,0:T(8,128)(2,1)}), bf16[1024,4096]{1,0:T(8,128)(2,1)}) %all-gather.13.cloned.1.call-update) | async-done | bytes 8388624 | tf_op jit(solution)/shard_map/all_gather | solution.py:149
  373.3 16.7 multiply_convert_fusion
  390.0 108.8 %all-gather.15.cloned.1.call-done = bf16[4096,1024]{1,0:T(8,128)(2,1)} async-done(((bf16[4096,128]{1,0:T(8,128)(2,1)}), bf16[4096,1024]{1,0:T(8,128)(2,1)}) %all-gather.15.cloned.1.call-update) | async-done | bytes 8388624 | tf_op jit(solution)/shard_map/all_gather | solution.py:150
  498.8 10.4 convert_reduce_fusion
  518.6 13.3 multiply_reduce_fusion
  538.2 9.3 fusion.142
  559.1 11.5 add_bitcast_fusion.1
  570.6 18.8 all-gather.19.cloned.1.call-done
  593.8 90.3 %while.33 = (s32[]{:T(128)}, f32[1,512,1024]{2,1,0:T(8,128)}, f32[4,512,1024]{1,2,0:T(8,128)}, s32[]{:T(128)}, s32[1,4]{1,0:T(1,128)S(1)}, /*index=5*/s32[1]{0:T...) while((s32[]{:T(128)}, f32[1,512,1024]{2,1,0:T(8,128)}, ...), condition=%wide.region_13.14_spmd.clone.clone, body=%wide.region_12.13_spmd.clone.clone.sunk | while | flops 8389899 | bytes 44044540 | solution.py:313
  684.2 17.7 fusion.30
  740.9 9.1 fusion.19
  774.1 193.7 %reduce-scatter.9.cloned.1.call-done = f32[1024,512]{1,0:T(8,128)} async-done(((f32[1024,4096]{1,0:T(8,128)}), f32[1024,512]{1,0:T(8,128)}) %reduce-scatter.9.cloned.1.call-update) | async-done | bytes 2097168 | tf_op jit(solution)/shard_map/reduce_scatter | solution.py:387
  967.9 285.6 %reduce-scatter.11.cloned.1.call-done = f32[4096,128]{1,0:T(8,128)} async-done(((f32[4096,1024]{1,0:T(8,128)}), f32[4096,128]{1,0:T(8,128)}) %reduce-scatter.11.cloned.1.call-update) | async-done | bytes 2097168 | tf_op jit(solution)/shard_map/reduce_scatter | solution.py:388
  1253.4 210.1 %reduce-scatter.5.cloned.1.call-done = f32[1024,384]{1,0:T(8,128)} async-done(((f32[1024,3072]{1,0:T(8,128)}), f32[1024,384]{1,0:T(8,128)}) %reduce-scatter.5.cloned.1.call-update) | async-done | bytes 1572880 | tf_op jit(solution)/shard_map/reduce_scatter | solution.py:385
  1470.1 153.5 %all-reduce.14.cloned.1.call-done = (f32[1024]{0:T(1024)}, f32[1024]{0:T(1024)}, f32[3072]{0:T(1024)}, f32[3,3072]{1,0:T(4,128)}, f32[3072]{0:T(1024)}, /*index=...) async-done(((f32[1024]{0:T(1024)}, f32[1024]{0:T(1024)}, ...) | async-done | bytes 135952 | tf_op jit(solution)/shard_map/psum | solution.py:362
  1623.6 136.2 %all-reduce.12.cloned.1.call-done = f32[64,1024]{1,0:T(8,128)} async-done(((f32[64,1024]{1,0:T(8,128)}), f32[64,1024]{1,0:T(8,128)}) %all-reduce.12.cloned.1.call-update) | async-done | bytes 262160 | tf_op jit(solution)/shard_map/psum | solution.py:362
  1759.8 122.5 %all-reduce.16.cloned.1.call-done = (f32[1024,384]{1,0:T(8,128)}, f32[1024,128]{1,0:T(8,128)}, f32[1024,512]{1,0:T(8,128)}, f32[4096,128]{1,0:T(8,128)}) async-done(((f32[1024,384]{1,0:T(8,128)}, f32[1024,128]{1,0:T(8,128)}, f32[1024,512]{1,0:T(8,128)}, f32[4096,128]{1,0:T(8,128)}), (f32[1024,384]{1,0:T(8,128)}, f32[1024,128]{1,0:T(8,128)}, f32[1024,512]{1,0:T(8,128)}, ...) | async-done | bytes 6291472 | tf_op jit(solution)/shard_map/psum | solution.py:390
  (433 shorter events, 306.9 us)
Async XLA Ops:
  7.2 137.2 %copy-start = (f32[64,1024]{1,0:T(8,128)S(1)}, f32[64,1024]{1,0:T(8,128)}, u32[]{:S(2)}) copy-start(f32[64,1024]{1,0:T(8,128)} %param.40) | copy-start | bytes 786436
  7.2 104.5 %all-gather.9.cloned.1.call-start = ((), (), s32[]{:S(2)}) async-start(), calls=%async_computation.4 | async-start | bytes 7077888 | tf_op jit(solution)/shard_map/all_gather | solution.py:147
  7.9 189.1 %all-gather.17.cloned.1.call-start = ((), (), s32[]{:S(2)}) async-start(), calls=%async_computation.13 | async-start | bytes 10485760 | tf_op jit(solution)/shard_map/all_gather | solution.py:235
  10.8 141.0 %copy-start.36 = (f32[256,256]{1,0:T(8,128)}, f32[256,256]{1,0:T(8,128)S(1)}, u32[]{:S(2)}) copy-start(f32[256,256]{1,0:T(8,128)S(1)} %fusion.117) | copy-start | bytes 786436
  16.9 134.9 %copy-start.38 = (f32[256,256]{1,0:T(8,128)}, f32[256,256]{1,0:T(8,128)S(1)}, u32[]{:S(2)}) copy-start(f32[256,256]{1,0:T(8,128)S(1)} %get-tuple-element.659) | copy-start | bytes 786436
  116.5 5.1 collective-permute-start
  137.8 123.5 %all-gather.11.cloned.1.call-start = ((), (), s32[]{:S(2)}) async-start(), calls=%async_computation.5 | async-start | bytes 2359296 | tf_op jit(solution)/shard_map/all_gather | solution.py:148
  138.6 234.7 %all-gather.13.cloned.1.call-start = ((), (), s32[]{:S(2)}) async-start(), calls=%async_computation.6 | async-start | bytes 9437184 | tf_op jit(solution)/shard_map/all_gather | solution.py:149
  139.2 359.6 %all-gather.15.cloned.1.call-start = ((), (), s32[]{:S(2)}) async-start(), calls=%async_computation.7 | async-start | bytes 9437184 | tf_op jit(solution)/shard_map/all_gather | solution.py:150
  139.7 449.7 %all-gather.19.cloned.1.call-start = ((), (), s32[]{:S(2)}) async-start(), calls=%async_computation.14 | async-start | bytes 10485760 | tf_op jit(solution)/shard_map/all_gather | solution.py:307
  531.9 242.2 %reduce-scatter.7.cloned.1.call-start = ((), (), s32[]{:S(2)}) async-start(), calls=%async_computation.10 | async-start | bytes 4718592 | tf_op jit(solution)/shard_map/reduce_scatter | solution.py:386
  535.9 431.9 %reduce-scatter.9.cloned.1.call-start = ((), (), s32[]{:S(2)}) async-start(), calls=%async_computation.11 | async-start | bytes 18874368 | tf_op jit(solution)/shard_map/reduce_scatter | solution.py:387
  547.6 705.9 %reduce-scatter.11.cloned.1.call-start = ((), (), s32[]{:S(2)}) async-start(), calls=%async_computation.12 | async-start | bytes 18874368 | tf_op jit(solution)/shard_map/reduce_scatter | solution.py:388
  557.5 906.0 %reduce-scatter.5.cloned.1.call-start = ((), (), s32[]{:S(2)}) async-start(), calls=%async_computation.8 | async-start | bytes 14155776 | tf_op jit(solution)/shard_map/reduce_scatter | solution.py:385
  709.8 5.5 collective-permute-start.1
  725.7 898.0 %all-reduce.14.cloned.1.call-start = ((), (), s32[]{:S(2)}) async-start(), calls=%async_computation.15 | async-start | bytes 354304 | tf_op jit(solution)/shard_map/psum | solution.py:362
  768.4 991.4 %all-reduce.12.cloned.1.call-start = ((), (), s32[]{:S(2)}) async-start(), calls=%async_computation.9 | async-start | bytes 524288 | tf_op jit(solution)/shard_map/psum | solution.py:362
  774.0 689.6 %copy-start.19 = (f32[256,1024]{1,0:T(8,128)S(1)}, f32[256,1024]{1,0:T(8,128)}, u32[]{:S(2)}) copy-start(f32[256,1024]{1,0:T(8,128)} %copy-done.16) | copy-start | bytes 3145732
  774.0 689.6 %copy-start.45 = (bf16[256,4096]{1,0:T(8,128)(2,1)S(1)}, bf16[256,4096]{1,0:T(8,128)(2,1)}, u32[]{:S(2)}) copy-start(bf16[256,4096]{1,0:T(8,128)(2,1)} %get-tuple-element.619) | copy-start | bytes 6291460
  774.0 689.6 %copy-start.110 = (f32[1024]{0:T(1024)S(1)}, f32[1024]{0:T(1024)}, u32[]{:S(2)}) copy-start(f32[1024]{0:T(1024)} %param.50) | copy-start | bytes 12292
  774.0 1108.3 %all-reduce.16.cloned.1.call-start = ((), (), s32[]{:S(2)}) async-start(), calls=%async_computation.16 | async-start | bytes 12582912 | tf_op jit(solution)/shard_map/psum | solution.py:390
  1623.6 278.2 %copy-start.102 = (f32[1024]{0:T(1024)S(1)}, f32[1024]{0:T(1024)}, u32[]{:S(2)}) copy-start(f32[1024]{0:T(1024)} %get-tuple-element.891) | copy-start | bytes 12292
  1623.6 278.8 %copy-start.101 = (f32[1024]{0:T(1024)S(1)}, f32[1024]{0:T(1024)}, u32[]{:S(2)}) copy-start(f32[1024]{0:T(1024)} %get-tuple-element.892) | copy-start | bytes 12292
  1623.6 279.4 %copy-start.100 = (f32[1024]{0:T(1024)S(1)}, f32[1024]{0:T(1024)}, u32[]{:S(2)}) copy-start(f32[1024]{0:T(1024)} %get-tuple-element.893) | copy-start | bytes 12292
  (104 other events, 1876.7 us)
Sparse Core Ops, SparseCore 0:
  10.1 101.5 all-gather.8
  138.0 57.4 all-gather.16
  197.5 50.0 all-gather.10
  249.5 123.7 all-gather.12
  375.2 123.5 all-gather.14
  532.0 57.3 all-gather.18
  593.0 88.0 reduce-scatter.6
  685.5 282.3 reduce-scatter.8
  971.6 281.7 reduce-scatter.10
  1257.3 206.2 reduce-scatter.4
  1472.8 150.7 all-reduce.13
  1633.2 126.5 all-reduce.11
  1762.6 119.6 all-reduce.15
where the time goes:
time: 1920 us; the launch traced here: 1910 us
  waiting for transfers between devices  1440 us (75%)
  matrix products  188 us (10%)
  other arithmetic  140 us (7%)
  local copies, waits for them, and re-layouts  117 us (6%)
    psum x2, waiting for transfers between devices, local(): lax.psum((grad_gain_one, grad_bias_one, grad_b_in, grad_taps, grad_short_...  290 us
    reduce_scatter x1, waiting for transfers between devices, local(): lax.psum_scatter(grad_down, 'dp', scatter_dimension=1, tiled=True)  286 us
    reduce_scatter x1, waiting for transfers between devices, local(): lax.psum_scatter(grad_in_weight, 'dp', scatter_dimension=1, tiled=True)  210 us
    reduce_scatter x1, waiting for transfers between devices, local(): lax.psum_scatter(grad_up, 'dp', scatter_dimension=1, tiled=True)  194 us
    psum x1, waiting for transfers between devices, local(): lax.psum((column_parts[0], column_parts[1], column_parts[2], column_parts...  123 us
    all_gather x1, waiting for transfers between devices, local(): lax.all_gather(w_down, 'dp', axis=1, tiled=True)  109 us
    all_gather x1, waiting for transfers between devices, local(): lax.all_gather(w_up, 'dp', axis=1, tiled=True)  108 us
    all_gather x1, waiting for transfers between devices, local(): lax.all_gather(w_in, 'dp', axis=1, tiled=True)  93.8 us
  transfers between devices with their start and end apart: 15, of which 12 were waited for; matrix products, arithmetic and copies ran while one was open for 19% of the time, Pallas kernels for 0%

commit v1 on v0

v1 whole, which is shorter than its diff:
```python
import math

import jax
import jax.numpy as jnp
import numpy as np
from jax import lax
from jax.sharding import PartitionSpec as P

EPSILON = 1e-05
MOD_SHIFT = 0.05
HIGHEST = lax.Precision.HIGHEST
HIGH = lax.Precision.HIGH
LOW = jnp.bfloat16
WIDE = jnp.float32


def dot_high(left, right):
    return jnp.dot(left, right, precision=HIGHEST, preferred_element_type=WIDE)


def dot_near(left, right):
    return jnp.dot(left, right, precision=HIGH, preferred_element_type=WIDE)


def dot_plain(left, right):
    return jnp.dot(left, right, preferred_element_type=WIDE)


def dot_first(left, right):
    return lax.dot_general(left, right, (((0,), (0,)), ((), ())), preferred_element_type=WIDE)


def dot_last(left, right):
    return lax.dot_general(left, right, (((1,), (1,)), ((), ())), preferred_element_type=WIDE)


def layer_norm(values, gain, bias):
    mean = jnp.mean(values, axis=-1, keepdims=True)
    centered = values - mean
    variance = jnp.mean(centered * centered, axis=-1, keepdims=True)
    return centered * lax.rsqrt(variance + EPSILON) * gain + bias


def exact_gelu(values):
    return jax.nn.gelu(values, approximate=False)


def position_table(length, emb_dim):
    bands = (emb_dim - 1) // 2
    sample = np.arange(length, dtype=np.float32)
    times = sample / np.float32(length - 1)
    frequency = np.linspace(0.0001, bands - 1, bands).astype(np.float32)
    angle = np.float32(2.0 * math.pi) * sample[:, None] * frequency[None, :] / np.float32(length)
    table = np.concatenate([times[:, None], np.cos(angle), -np.sin(angle)], axis=1)
    return (table.astype(np.float32), times)


def transform_tables(block_len):
    span = 2 * block_len
    frequency = np.arange(block_len)
    sample = np.arange(block_len)
    is_zero = (frequency == 0)[:, None]
    angle = 2.0 * math.pi * (frequency[:, None] * sample[None, :] % span) / span
    alternate = np.where(sample % 2 == 0, 1.0, -1.0)
    real_rows = np.cos(angle)
    imag_rows = np.where(is_zero, alternate[None, :], -np.sin(angle))
    forward_table = np.concatenate([real_rows, imag_rows], axis=0)
    outputs = sample + block_len
    out_angle = 2.0 * math.pi * (outputs[:, None] * frequency[None, :] % span) / span
    out_alternate = np.where(outputs % 2 == 0, 1.0, -1.0)
    zero_col = (frequency == 0)[None, :]
    real_cols = np.where(zero_col, 1.0, 2.0) * np.cos(out_angle) / span
    imag_cols = np.where(zero_col, out_alternate[:, None] / span, -2.0 * np.sin(out_angle) / span)
    inverse_table = np.concatenate([real_cols, imag_cols], axis=1)
    parity = np.where(frequency % 2 == 0, 1.0, -1.0)
    sign = np.concatenate([parity, np.where(frequency == 0, 1.0, parity)])
    edge = (frequency == 0).astype(np.float32)[:, None]
    return tuple(item.astype(np.float32) for item in (forward_table, inverse_table, sign, edge))


def spectral_product(left, right, edge):
    half = left.shape[-2] // 2
    left_re, left_im = (left[..., :half, :], left[..., half:, :])
    right_re, right_im = (right[..., :half, :], right[..., half:, :])
    inside = 1.0 - edge
    out_re = left_re * right_re - inside * left_im * right_im
    out_im = inside * (left_re * right_im + left_im * right_re) + edge * left_im * right_im
    return jnp.concatenate([out_re, out_im], axis=-2)


def spectral_back(grad, other, edge):
    half = grad.shape[-2] // 2
    grad_re, grad_im = (grad[..., :half, :], grad[..., half:, :])
    other_re, other_im = (other[..., :half, :], other[..., half:, :])
    inside = 1.0 - edge
    back_re = grad_re * other_re + inside * grad_im * other_im
    back_im = inside * (grad_im * other_re - grad_re * other_im) + edge * grad_im * other_im
    return jnp.concatenate([back_re, back_im], axis=-2)


class Grid:
    def __init__(self, count_dp, count_block):
        self.count_dp = count_dp
        self.count_block = count_block
        self.row = lax.axis_index("dp")
        self.place = lax.axis_index("block")
        self.dp_steps = []
        bit = 1
        while bit < count_dp:
            self.dp_steps.append((bit | (bit >> 1) if bit == 4 else bit, 0))
            bit *= 2
        self.chip_steps = []
        bit = 2
        while bit < count_block:
            self.chip_steps.append((0, bit | (bit >> 1) if bit == 4 else bit))
            bit *= 2
        self.core_step = (0, 1)

    def swap(self, value, step):
        pairs = []
        for row in range(self.count_dp):
            for place in range(self.count_block):
                to = (row ^ step[0]) * self.count_block + (place ^ step[1])
                pairs.append((row * self.count_block + place, to))
        return lax.ppermute(value, ("dp", "block"), pairs)

    def gather(self, value, steps):
        held = value[None]
        for step in steps:
            held = jnp.concatenate([held, self.swap(held, step)], axis=0)
        return held

    def scatter(self, held, steps):
        for step in reversed(steps):
            half = held.shape[0] // 2
            arrived = self.swap(held[half:], step)
            held = (held[:half].astype(WIDE) + arrived.astype(WIDE)).astype(held.dtype)
        return held[0]


def offsets_of(steps):
    offsets = [(0, 0)]
    for step in steps:
        offsets = offsets + [(a ^ step[0], b ^ step[1]) for a, b in offsets]
    return offsets


def pick(held, places):
    return jnp.concatenate(
        [lax.dynamic_slice_in_dim(held, places[i], 1, 0) for i in range(len(places))], axis=0
    )


def places_of(steps, wanted):
    return wanted


def lookup(table, index):
    return lax.dynamic_index_in_dim(jnp.asarray(np.asarray(table, np.int32)), index, 0, keepdims=False)


def local(
    block_in,
    doc_starts,
    norm1_gain,
    norm1_bias,
    w_in,
    b_in,
    short_taps,
    short_bias,
    filter_w1,
    filter_b1,
    filter_w2,
    filter_b2,
    filter_w3,
    filter_decay,
    conv_bias,
    w_out,
    b_out,
    norm2_gain,
    norm2_bias,
    w_up,
    b_up,
    w_down,
    b_down,
    cotangent,
):
    count_dp, blocks = lax.axis_size("dp"), lax.axis_size("block")
    grid = Grid(count_dp, blocks)
    row, place = grid.row, grid.place
    chips, core, chip = blocks // 2, place % 2, place // 2
    _, block_len, width = block_in.shape
    length = block_len * blocks
    hidden_width = w_up.shape[1] * count_dp
    dp_steps, chip_steps, core_step = grid.dp_steps, grid.chip_steps, grid.core_step
    block_steps = chip_steps + [core_step]

    def dp_places(steps):
        code = {a: i for i, (a, _) in enumerate(offsets_of(steps))}
        return [lookup([code[k ^ r] for r in range(count_dp)], row) for k in range(count_dp)]

    def block_places(steps):
        code = {b: i for i, (_, b) in enumerate(offsets_of(steps))}
        return [lookup([code[k ^ r] for r in range(blocks)], place) for k in range(blocks)]

    def pair_places(steps):
        code = {pair: i for i, pair in enumerate(offsets_of(steps))}
        flat = row * chips + chip
        return [
            lookup(
                [code[(k ^ r, (x ^ c) * 2)] for r in range(count_dp) for c in range(chips)], flat
            )
            for k in range(count_dp)
            for x in range(chips)
        ]

    def inverse_places(steps, count, mine, part):
        return [mine ^ offset[part] for offset in offsets_of(steps)]

    def rotated(steps, turn):
        turn = turn % len(steps)
        return steps[turn:] + steps[:turn]

    shard_in = w_in.shape[1]
    group = math.gcd(width, shard_in)
    groups_here, share = shard_in // group, group // blocks
    channels = width // blocks

    def own(values, lead=()):
        total = values.shape[-1]
        split = values.reshape(*values.shape[:-1], total // group, blocks, share)
        kept = lax.dynamic_index_in_dim(split, place, split.ndim - 2, keepdims=False)
        return kept.reshape(*values.shape[:-1], total // blocks)

    in_turned = w_in.T.reshape(groups_here, blocks, share, width)
    in_own = lax.dynamic_index_in_dim(in_turned, place, 1, keepdims=False)
    in_orders = [rotated(dp_steps, i) for i in range(groups_here)]
    in_parts = [
        pick(grid.gather(in_own[i], in_orders[i]), dp_places(in_orders[i]))
        for i in range(groups_here)
    ]
    in_rows = jnp.stack(in_parts, axis=1).reshape(3 * channels, width)

    inputs = block_in.astype(WIDE).reshape(block_len, width)
    normed, norm1_back = jax.vjp(layer_norm, inputs, norm1_gain, norm1_bias)
    normed_low = normed.astype(LOW)
    normed_all = pick(grid.gather(normed_low, block_steps), block_places(block_steps)).reshape(
        length, width
    )

    out_order = dp_steps[::-1] + block_steps
    out_split = w_out.reshape(width // group, blocks, share, w_out.shape[1])
    out_own = lax.dynamic_index_in_dim(out_split, place, 1, keepdims=False).reshape(
        channels, w_out.shape[1]
    )
    out_held = grid.gather(out_own, out_order).reshape(blocks, count_dp, channels, w_out.shape[1])
    out_places = dp_places(dp_steps[::-1])
    full_out = jnp.concatenate(
        [lax.dynamic_slice_in_dim(out_held, p, 1, 1) for p in out_places], axis=1
    )
    full_out = full_out.transpose(0, 2, 1, 3).reshape(width, width)

    pair_steps = dp_steps + chip_steps
    piece = w_up.shape[1] // blocks
    up_own = lax.dynamic_slice_in_dim(w_up, place_column(core, chip, chips) * piece, piece, 1)
    up_own = up_own.reshape(2, width // 2, piece)
    down_own = w_down.reshape(count_dp, 2 * chips, piece, w_down.shape[1])
    down_own = lax.dynamic_index_in_dim(down_own, core * chips + chip, 1, keepdims=False)
    down_own = down_own.reshape(2, count_dp // 2 * piece, w_down.shape[1])
    ff_orders = [rotated(pair_steps, i) for i in range(4)]
    up_parts = [
        pick(grid.gather(up_own[i], ff_orders[i]), pair_places(ff_orders[i])) for i in range(2)
    ]
    down_parts = [
        pick(grid.gather(down_own[i], ff_orders[2 + i]), pair_places(ff_orders[2 + i]))
        for i in range(2)
    ]
    half_hidden = hidden_width // 2
    up_here = jnp.concatenate(
        [part.transpose(1, 0, 2).reshape(width // 2, half_hidden) for part in up_parts], axis=0
    )
    down_here = jnp.stack(
        [
            part.reshape(count_dp, chips, count_dp // 2, piece, w_down.shape[1]).transpose(
                2, 1, 3, 0, 4
            )
            for part in down_parts
        ],
        axis=0,
    ).reshape(half_hidden, width)
    b_up_here = lax.dynamic_index_in_dim(
        b_up.reshape(count_dp, 2, chips * piece), core, 1, keepdims=False
    ).reshape(half_hidden)
    cot_flat = cotangent.reshape(block_len, width)
    cot_pair = jnp.concatenate([cot_flat, grid.swap(cot_flat, core_step)], axis=0)

    forward_table, inverse_table, sign, edge = transform_tables(block_len)
    starts = doc_starts[0]
    positions = jnp.arange(length, dtype=jnp.int32)
    segment = jnp.sum((starts[None, :] <= positions[:, None]).astype(jnp.int32), axis=-1) - 1
    keep_one = jnp.concatenate([jnp.zeros((1,), WIDE), (segment[1:] == segment[:-1]).astype(WIDE)])
    keep_two = jnp.concatenate([jnp.zeros((2,), WIDE), (segment[2:] == segment[:-2]).astype(WIDE)])
    keep_one, keep_two = keep_one[:, None], keep_two[:, None]
    num_docs = doc_starts.shape[1]
    long_doc = jnp.sum((starts <= block_len).astype(jnp.int32)) - 1
    long_mask = (segment == long_doc).astype(WIDE)[:, None]
    first_segment, last_segment = segment[:block_len], segment[length - block_len :]
    short_early, short_masks = [], []
    for number in range(num_docs - 1):
        early = number < long_doc
        doc = jnp.where(early, number, number + 1)
        where = jnp.where(early, first_segment, last_segment)
        short_early.append(early.astype(WIDE))
        short_masks.append((where == doc).astype(WIDE)[:, None])

    def spread(values):
        masked = values * long_mask
        parts = [masked[i * block_len : (i + 1) * block_len] for i in range(blocks)]
        first, last = values[:block_len], values[length - block_len :]
        for early, mask in zip(short_early, short_masks):
            parts.append(mask * (early * first + (1.0 - early) * last))
        return jnp.concatenate(parts, axis=1)

    def collect(values):
        parts = [
            values[:, i * channels : (i + 1) * channels] for i in range(blocks + num_docs - 1)
        ]
        first, last = jnp.zeros_like(parts[0]), jnp.zeros_like(parts[0])
        for early, mask, part in zip(short_early, short_masks, parts[blocks:]):
            first = first + early * mask * part
            last = last + (1.0 - early) * mask * part
        joined = jnp.concatenate(parts[:blocks], axis=0) * long_mask
        middle = jnp.zeros((length - 2 * block_len, channels), WIDE)
        return joined + jnp.concatenate([first, middle, last], axis=0)

    def cut(values, count):
        return [values[:, i * channels : (i + 1) * channels] for i in range(count)]

    table, times = position_table(length, filter_w1.shape[0])

    def filter_spectra(params):
        first = jnp.sin(dot_high(table, params[0]) + params[1])
        second = jnp.sin(dot_high(first, params[2]) + params[3])
        kernel = dot_high(second, params[4]) * (
            jnp.exp(-times[:, None] * params[5][None, :]) + MOD_SHIFT
        )
        pieces = jnp.concatenate(
            [kernel[i * block_len : (i + 1) * block_len] for i in range(blocks)], axis=1
        )
        halves = dot_near(forward_table, pieces)
        earlier = jnp.concatenate(
            [jnp.zeros((2 * block_len, channels), WIDE), halves[:, : (blocks - 1) * channels]],
            axis=1,
        )
        return earlier + sign[:, None] * halves

    spectra_flat, filter_back = jax.vjp(
        filter_spectra,
        (filter_w1, filter_b1, filter_w2, filter_b2, own(filter_w3), own(filter_decay)),
    )
    spectra = cut(spectra_flat, blocks)

    proj = dot_last(normed_all, in_rows) + own(b_in)
    taps, short_shift = own(short_taps), own(short_bias)
    three = 3 * channels
    prev_one = jnp.concatenate([jnp.zeros((1, three), WIDE), proj[:-1]], axis=0) * keep_one
    prev_two = jnp.concatenate([jnp.zeros((2, three), WIDE), proj[:-2]], axis=0) * keep_two
    short = short_shift + taps[0] * proj + taps[1] * prev_one + taps[2] * prev_two
    gate_part, mult, value = cut(short, 3)
    inner = value * mult
    direct = own(conv_bias)

    entries = cut(dot_near(forward_table, spread(inner)), blocks + num_docs - 1)
    totals = []
    for i in range(blocks):
        total = spectral_product(entries[i], spectra[0], edge)
        for j in range(i):
            total = total + spectral_product(entries[j], spectra[i - j], edge)
        totals.append(total)
    for entry in entries[blocks:]:
        totals.append(spectral_product(entry, spectra[0], edge))
    mixed = collect(dot_near(inverse_table, jnp.concatenate(totals, axis=1))) + direct * inner
    gated_low = (gate_part * mixed).astype(LOW)

    block_offsets = [b for _, b in offsets_of(block_steps)]
    gated_parts = []
    for offset in block_offsets:
        part = lax.dynamic_slice_in_dim(gated_low, (place ^ offset) * block_len, block_len, 0)
        gated_parts.append(grid.swap(part, (0, offset)) if offset else part)
    gated_rows = jnp.concatenate(gated_parts, axis=1)
    resid = inputs + dot_plain(gated_rows, full_out) + b_out
    normed2, norm2_back = jax.vjp(layer_norm, resid, norm2_gain, norm2_bias)
    normed2_low = normed2.astype(LOW)

    pair = jnp.concatenate([normed2_low, grid.swap(normed2_low, core_step)], axis=0)
    hidden = dot_plain(pair, up_here) + b_up_here
    act, gelu_back = jax.vjp(exact_gelu, hidden)
    act_low = act.astype(LOW)
    grad_act = dot_last(cot_pair, down_here)
    grad_hidden = gelu_back(grad_act)[0].astype(LOW)
    grad_pair = dot_last(grad_hidden, up_here)
    grad_normed2 = grad_pair[:block_len] + grid.swap(
        grad_pair[block_len:].astype(LOW), core_step
    ).astype(WIDE)
    out_pair = dot_plain(act_low, down_here)
    output = (
        resid
        + out_pair[:block_len]
        + grid.swap(out_pair[block_len:].astype(LOW), core_step).astype(WIDE)
        + b_down
    )
    block_out = output.astype(LOW)[None]
    grad_down_here = dot_first(act_low, cot_pair).astype(LOW)
    grad_up_here = dot_first(pair, grad_hidden).astype(LOW)
    grad_b_up_here = jnp.sum(grad_hidden.astype(WIDE), axis=0)
    grad_b_down = jnp.sum(cot_flat.astype(WIDE), axis=0)

    def send_home(natural, order):
        wanted = [
            ((row ^ a) * chips + (chip ^ (b >> 1))) for a, b in offsets_of(order)
        ]
        return grid.scatter(pick(natural, wanted), order)

    up_grads = [
        send_home(
            grad_up_here[i * (width // 2) : (i + 1) * (width // 2)]
            .reshape(width // 2, count_dp * chips, piece)
            .transpose(1, 0, 2),
            ff_orders[i],
        )
        for i in range(2)
    ]
    down_split = grad_down_here.reshape(
        2, count_dp // 2, chips, piece, count_dp, w_down.shape[1]
    )
    down_grads = [
        send_home(
            down_split[i]
            .transpose(3, 1, 0, 2, 4)
            .reshape(count_dp * chips, count_dp // 2 * piece, w_down.shape[1]),
            ff_orders[2 + i],
        )
        for i in range(2)
    ]

    resid_part, grad_gain_two, grad_bias_two = norm2_back(grad_normed2)
    grad_resid = cot_flat.astype(WIDE) + resid_part
    grad_branch = grad_resid.astype(LOW)
    grad_b_out = jnp.sum(grad_branch.astype(WIDE), axis=0)
    grad_gated_rows = dot_last(grad_branch, full_out).astype(LOW)
    grad_out_here = dot_first(gated_rows, grad_branch).astype(LOW)
    grad_out_split = grad_out_here.reshape(blocks, channels, count_dp, w_out.shape[1]).transpose(
        0, 2, 1, 3
    )
    out_wanted = [row ^ a for a, _ in offsets_of(dp_steps[::-1])]
    grad_out_split = jnp.concatenate(
        [lax.dynamic_slice_in_dim(grad_out_split, p, 1, 1) for p in out_wanted], axis=1
    ).reshape(blocks * count_dp, channels, w_out.shape[1])
    out_grad = grid.scatter(grad_out_split, out_order)

    grad_parts = []
    for index, offset in enumerate(block_offsets):
        part = grad_gated_rows[:, index * channels : (index + 1) * channels]
        grad_parts.append((grid.swap(part, (0, offset)) if offset else part)[None])
    grad_gated = pick(jnp.concatenate(grad_parts, axis=0), block_places(block_steps))
    grad_gated = grad_gated.reshape(length, channels).astype(WIDE)

    grad_gate_part = grad_gated * mixed
    grad_mixed = grad_gated * gate_part
    grad_conv_bias = jnp.sum(grad_mixed * inner, axis=0)
    grad_totals = cut(
        lax.dot_general(
            inverse_table,
            spread(grad_mixed),
            (((0,), (0,)), ((), ())),
            precision=HIGH,
            preferred_element_type=WIDE,
        ),
        blocks + num_docs - 1,
    )
    grad_entries = []
    grad_lags = [None] * blocks
    for i in range(blocks + num_docs - 1):
        lag = spectral_back(grad_totals[i], entries[i], edge)
        grad_lags[0] = lag if grad_lags[0] is None else grad_lags[0] + lag
        grad_entries.append(spectral_back(grad_totals[i], spectra[0], edge))
    for j in range(blocks):
        for i in range(j + 1, blocks):
            grad_entries[j] = grad_entries[j] + spectral_back(
                grad_totals[i], spectra[i - j], edge
            )
            lag = spectral_back(grad_totals[i], entries[j], edge)
            grad_lags[i - j] = lag if grad_lags[i - j] is None else grad_lags[i - j] + lag
    filter_grads = filter_back(jnp.concatenate(grad_lags, axis=1))[0]
    grad_inner = (
        collect(
            lax.dot_general(
                forward_table,
                jnp.concatenate(grad_entries, axis=1),
                (((0,), (0,)), ((), ())),
                precision=HIGH,
                preferred_element_type=WIDE,
            )
        )
        + direct * grad_mixed
    )
    grad_short = jnp.concatenate([grad_gate_part, grad_inner * value, grad_inner * mult], axis=1)
    grad_taps = jnp.stack(
        [
            jnp.sum(grad_short * proj, axis=0),
            jnp.sum(grad_short * prev_one, axis=0),
            jnp.sum(grad_short * prev_two, axis=0),
        ],
        axis=0,
    )
    grad_short_bias = jnp.sum(grad_short, axis=0)
    pass_one = grad_short * keep_one
    pass_two = grad_short * keep_two
    grad_proj = (
        taps[0] * grad_short
        + taps[1] * jnp.concatenate([pass_one[1:], jnp.zeros((1, three), WIDE)], axis=0)
        + taps[2] * jnp.concatenate([pass_two[2:], jnp.zeros((2, three), WIDE)], axis=0)
    )
    grad_proj_low = grad_proj.astype(LOW)
    grad_b_in = jnp.sum(grad_proj_low.astype(WIDE), axis=0)
    grad_in_rows = dot_first(grad_proj_low, normed_all).astype(LOW)
    grad_in_split = grad_in_rows.reshape(count_dp, groups_here, share, width)
    in_grads = []
    for i in range(groups_here):
        wanted = [row ^ a for a, _ in offsets_of(in_orders[i])]
        in_grads.append(grid.scatter(pick(grad_in_split[:, i], wanted), in_orders[i]))
    grad_normed_part = dot_plain(grad_proj_low, in_rows).astype(LOW).reshape(
        blocks, block_len, width
    )
    grad_normed = grid.scatter(
        pick(grad_normed_part, [place ^ offset for offset in block_offsets]), block_steps
    ).astype(WIDE)
    input_part, grad_gain_one, grad_bias_one = norm1_back(grad_normed)
    grad_input = (grad_resid + input_part)[None]

    def all_places(value):
        return pick(grid.gather(value, block_steps), block_places(block_steps))

    in_whole = all_places(jnp.stack(in_grads, axis=0))
    in_whole = in_whole.transpose(1, 0, 2, 3).reshape(shard_in, width).T.astype(WIDE)
    out_whole = all_places(out_grad).reshape(blocks, width // group, share, w_out.shape[1])
    out_whole = out_whole.transpose(1, 0, 2, 3).reshape(width, w_out.shape[1]).astype(WIDE)
    core_major = [b for c in range(2) for b in range(c, blocks, 2)]
    up_whole = all_places(jnp.concatenate(up_grads, axis=0))
    up_whole = jnp.concatenate([up_whole[b] for b in core_major], axis=1).astype(WIDE)
    down_whole = all_places(jnp.concatenate(down_grads, axis=0))
    down_whole = jnp.stack([down_whole[b] for b in core_major], axis=0).reshape(
        2 * chips, count_dp, piece, w_down.shape[1]
    )
    down_whole = down_whole.transpose(1, 0, 2, 3).reshape(hidden_width, w_down.shape[1])
    down_whole = down_whole.astype(WIDE)

    shared = [
        grad_gain_one,
        grad_bias_one,
        grad_b_out,
        grad_gain_two,
        grad_bias_two,
        grad_b_down,
        filter_grads[0],
        filter_grads[1],
        filter_grads[2],
        filter_grads[3],
    ]
    up_home = jnp.zeros((2, half_hidden), WIDE)
    up_home = lax.dynamic_update_slice_in_dim(up_home, grad_b_up_here[None], core, 0)
    shared.append(up_home)
    flat = jnp.concatenate([item.reshape(-1) for item in shared])
    chunk = -(-flat.shape[0] // (blocks * 128)) * 128
    flat = jnp.pad(flat, (0, chunk * blocks - flat.shape[0])).reshape(blocks, chunk)
    shared_part = grid.scatter(
        pick(flat, [place ^ offset for offset in block_offsets]), block_steps
    )
    parted = [
        grad_b_in[None],
        grad_taps,
        grad_short_bias[None],
        filter_grads[4],
        filter_grads[5][None],
        grad_conv_bias[None],
    ]
    joined = jnp.concatenate([shared_part] + [item.reshape(-1) for item in parted])
    for step in dp_steps:
        joined = joined + grid.swap(joined, step)
    every = all_places(joined)
    whole_flat = every[:, :chunk].reshape(-1)
    shared_out, at = [], 0
    for item in shared:
        shared_out.append(whole_flat[at : at + item.size].reshape(item.shape))
        at += item.size
    parted_out, at = [], chunk
    for item in parted:
        lead, size = item.shape[0], item.size
        values = every[:, at : at + size].reshape(blocks, lead, item.shape[1] // share, share)
        parted_out.append(values.transpose(1, 2, 0, 3).reshape(lead, item.shape[1] * blocks))
        at += size
    grad_b_up = shared_out[10].reshape(2, count_dp, chips * piece)
    grad_b_up = grad_b_up.transpose(1, 0, 2).reshape(hidden_width)
    return (
        block_out,
        grad_input,
        shared_out[0],
        shared_out[1],
        in_whole,
        parted_out[0][0],
        parted_out[1],
        parted_out[2][0],
        shared_out[6],
        shared_out[7],
        shared_out[8],
        shared_out[9],
        parted_out[3],
        parted_out[4][0],
        parted_out[5][0],
        out_whole,
        shared_out[2],
        shared_out[3],
        shared_out[4],
        up_whole,
        grad_b_up,
        down_whole,
        shared_out[5],
    )


def place_column(core, chip, chips):
    return core * chips + chip


def solution(mesh):
    placed = (
        P("dp", "block", None),
        P("dp", None),
        P(),
        P(),
        P(None, "dp"),
        P(),
        P(),
        P(),
        P(),
        P(),
        P(),
        P(),
        P(),
        P(),
        P(),
        P(None, "dp"),
        P(),
        P(),
        P(),
        P(None, "dp"),
        P(),
        P(None, "dp"),
        P(),
        P("dp", "block", None),
    )
    return jax.shard_map(
        local,
        mesh=mesh,
        in_specs=placed,
        out_specs=(
            P("dp", "block", None),
            P("dp", "block", None),
            P(),
            P(),
            P(None, "dp"),
            P(),
            P(),
            P(),
            P(),
            P(),
            P(),
            P(),
            P(),
            P(),
            P(),
            P(None, "dp"),
            P(),
            P(),
            P(),
            P(None, "dp"),
            P(),
            P(None, "dp"),
            P(),
        ),
        check_vma=False,
    )
```

time: 1920 us -> 813 us (0.42)
  waiting for transfers between devices: 1440 us -> 101 us
  between operations: 15.3 us -> 194 us
  starting transfers between devices: 7.32 us -> 154 us
  matrix products: 188 us -> 66.6 us
  local copies, waits for them, and re-layouts: 117 us -> 223 us
  other arithmetic: 140 us -> 61.1 us
    reduce_scatter x4 -> x0, waiting for transfers between devices: 689 us -> none  [the longest x1 286 us: local(): lax.psum_scatter(grad_down, 'dp', scatter_dimension=1, tiled=True)]
    psum x3 -> x0, waiting for transfers between devices: 412 us -> none  [the longest x2 290 us: local(): lax.psum((grad_gain_one, grad_bias_one, grad_b_in, grad_taps, grad_short_...]
    all_gather x6 -> x0, waiting for transfers between devices: 329 us -> none  [the longest x1 109 us: local(): lax.all_gather(w_down, 'dp', axis=1, tiled=True)]
    ppermute x2 -> x89, starting transfers between devices: 6.44 us -> 154 us  [swap(): return lax.ppermute(value, ('dp', 'block'), pairs)]
    ppermute x2 -> x89, waiting for transfers between devices: 2.55 us -> 101 us  [swap(): return lax.ppermute(value, ('dp', 'block'), pairs)]
    dot_general x18, matrix products: 141 us -> 45.5 us  [the longest x4 18.5 us: dot_plain(): return jnp.dot(left, right, preferred_element_type=WIDE)]
    dynamic_slice x18 -> x117, local copies, waits for them, and re-layouts: 26 us -> 110 us  [the longest x100 107 us: lookup(): lax.dynamic_index_in_dim(jnp.asarray(np.asarray(table, np.int32)), index,...]
    add x13 -> x19, other arithmetic: 48.8 us -> 8.41 us  [the longest x1 2.44 us: filter_spectra(): return earlier + sign[:, None] * halves]
  transfers between devices with their start and end apart: 15 -> 89, of which waited for: 12 -> 29; matrix products, arithmetic and copies ran while one was open for 19% -> 39% of each run, Pallas kernels for 0% -> 0%
where the time goes in v1:
time: 813 us; the launch traced here: 800 us
  local copies, waits for them, and re-layouts  223 us (27%)
  between operations  194 us (24%)
  starting transfers between devices  154 us (19%)
  waiting for transfers between devices  101 us (12%)
  matrix products  66.6 us (8%)
  other arithmetic  61.1 us (8%)
    ppermute x89, starting transfers between devices, swap(): return lax.ppermute(value, ('dp', 'block'), pairs)  154 us
    dynamic_slice x100, local copies, waits for them, and re-layouts, lookup(): lax.dynamic_index_in_dim(jnp.asarray(np.asarray(table, np.int32)), index,...  107 us
    ppermute x89, waiting for transfers between devices, swap(): return lax.ppermute(value, ('dp', 'block'), pairs)  101 us
    unnamed x583, local copies, waits for them, and re-layouts  52 us
    dot_general x4, matrix products, dot_plain(): return jnp.dot(left, right, preferred_element_type=WIDE)  18.5 us
    another operation x4, local copies, waits for them, and re-layouts  17.9 us
  transfers between devices with their start and end apart: 89, of which 29 were waited for; matrix products, arithmetic and copies ran while one was open for 39% of the time, Pallas kernels for 0%

profile of v1, /device:TPU:1, one launch (start us, length us, event | category | flops | bytes accessed | tf_op | source)
XLA Modules:
  0.0 799.9 jit_solution(7259603435418489012)
XLA Ops:
  2.3 4.2 collective-permute-start.14
  356.5 5.4 collective-permute-start.37
  375.1 4.4 collective-permute-done.33
  384.7 6.5 collective-permute-start.10
  392.3 5.0 collective-permute-done.10
  398.5 4.4 collective-permute-done.7
  414.4 12.7 %collective-permute-start.1 = (bf16[2,256,1024]{2,1,0:T(8,128)(2,1)S(1)}, bf16[2,256,1024]{2,1,0:T(8,128)(2,1)S(1)}, u32[]{:S(2)}, u32[]{:S(2)}) collective-permute-start(bf16[2,256,1024]{2,1,0:T(8,128)(2,1)S(1)} %pad_maximum_fusion.8), channel_id=1, source_target_pairs={{0,1},{1,0},{2,3},{3,2},{4,5},{5,4},{6,7},{7,6},{8,9},{9,8},{10,11... | collective-permute-start | bytes 3145736 | tf_op jit(solution)/shard_map/ppermute | solution.py:125
  450.8 28.3 %collective-permute-done.31 = bf16[8,512,128]{2,1,0:T(8,128)(2,1)S(1)} collective-permute-done((bf16[8,512,128]{2,1,0:T(8,128)(2,1)S(1)}, bf16[8,512,128]{2,1,0:T(8,128)(2,1)S(1)}, u32[]{:S(2)}, u32[]{:S(2)}) %collective-permute-start.31) | collective-permute-done | bytes 1048608 | tf_op jit(solution)/shard_map/ppermute | solution.py:125
  484.2 4.0 copy.345
  495.0 12.3 %multiply_convert_fusion = (bf16[512,2048]{1,0:T(8,128)(2,1)S(1)}, f32[512,2048]{1,0:T(8,128)S(1)}, f32[512,2048]{1,0:T(8,128)}) fusion(f32[2048]{0:T(1024)S(1)} %bitcast.683, bf16[512,2048]{0,1:T(8,128)(2,1)S(1)} %bitcast.679, bf16[512,2048]{0,1:T(8,128)(2,1)S(1)} %bitcast.681, bf16[256,1024]{1,0:T(8,128)(2,1)S(1)} %collective-permute-done.19, ...), kind=kOutput, calls=%fused_computation.10 | convolution fusion | flops 2227175424 | bytes 15736832 | tf_op jit(solution)/shard_map/dot_general | solution.py:26
  507.3 3.7 fusion.3
  511.0 5.9 convert_reduce_fusion
  524.0 4.0 convolution_convert_fusion
  548.4 6.5 constant_dynamic-slice_fusion.12
  555.7 6.1 constant_dynamic-slice_fusion.28
  578.5 5.2 constant_dynamic-slice_fusion.40
  606.3 4.0 fusion.146
  635.9 6.3 collective-permute-start.57
  643.6 4.6 collective-permute-done.57
  666.1 8.3 %collective-permute-done.56 = bf16[1,32,1024]{2,1,0:T(8,128)(2,1)S(1)} collective-permute-done((bf16[1,32,1024]{2,1,0:T(8,128)(2,1)S(1)}, bf16[1,32,1024]{2,1,0:T(8,128)(2,1)S(1)}, u32[]{:S(2)}, u32[]{:S(2)}) %collective-permute-start.56) | collective-permute-done | bytes 65568 | tf_op jit(solution)/shard_map/ppermute | solution.py:125
  689.3 6.9 collective-permute-start.61
  714.0 4.3 collective-permute-start.76
  729.3 23.1 %collective-permute-start.44 = (f32[2,4224]{1,0:T(2,128)S(1)}, f32[2,4224]{1,0:T(2,128)S(1)}, u32[]{:S(2)}, u32[]{:S(2)}) collective-permute-start(f32[2,4224]{1,0:T(2,128)S(1)} %pad_maximum_fusion.62), channel_id=1, source_target_pairs={{0,1},{1,0},{2,3},{3,2},{4,5},{5,4},{6,7},{7,6},{8,9},{9,8},{10,11... | collective-permute-start | bytes 101384 | tf_op jit(solution)/shard_map/ppermute | solution.py:125
  772.4 5.5 collective-permute-start.78
  (1196 shorter events, 424.1 us)
Async XLA Ops:
  2.3 340.8 %collective-permute-start.14 = (bf16[1,256,128]{2,1,0:T(8,128)(2,1)}, bf16[1,256,128]{2,1,0:T(8,128)(2,1)}, u32[]{:S(2)}, u32[]{:S(2)}) collective-permute-start(bf16[1,256,128]{2,1,0:T(8,128)(2,1)} %bitcast.43), channel_id=1, source_target_pairs={{0,24},{1,25},{2,26},{3,27},{4,28},{5,29},{6,30},{7,31},{8,16},{9,... | collective-permute-start | bytes 196616 | tf_op jit(solution)/shard_map/ppermute | solution.py:125
  7.5 357.0 %collective-permute-start.24 = (bf16[1,512,128]{1,2,0:T(8,128)(2,1)S(1)}, bf16[1,512,128]{1,2,0:T(8,128)(2,1)S(1)}, u32[]{:S(2)}, u32[]{:S(2)}) collective-permute-start(bf16[1,512,128]{1,2,0:T(8,128)(2,1)S(1)} %bitcast.623), channel_id=1, source_target_pairs={{0,8},{1,9},{2,10},{3,11},{4,12},{5,13},{6,14},{7,15},{8,0},{9,1},... | collective-permute-start | bytes 393224 | tf_op jit(solution)/shard_map/ppermute | solution.py:125
  7.8 354.3 %collective-permute-start.20 = (bf16[1,512,128]{1,2,0:T(8,128)(2,1)S(1)}, bf16[1,512,128]{1,2,0:T(8,128)(2,1)}, u32[]{:S(2)}, u32[]{:S(2)}) collective-permute-start(bf16[1,512,128]{1,2,0:T(8,128)(2,1)S(1)} %bitcast.627), channel_id=1, source_target_pairs={{0,4},{1,5},{2,6},{3,7},{4,0},{5,1},{6,2},{7,3},{8,12},{9,13},{10,... | collective-permute-start | bytes 393224 | tf_op jit(solution)/shard_map/ppermute | solution.py:125
  10.1 351.8 %collective-permute-start.32 = (bf16[1,512,128]{2,1,0:T(8,128)(2,1)S(1)}, bf16[1,512,128]{2,1,0:T(8,128)(2,1)S(1)}, u32[]{:S(2)}, u32[]{:S(2)}) collective-permute-start(bf16[1,512,128]{2,1,0:T(8,128)(2,1)S(1)} %bitcast.613), channel_id=1, source_target_pairs={{0,2},{1,3},{2,0},{3,1},{4,6},{5,7},{6,4},{7,5},{8,10},{9,11},{10,... | collective-permute-start | bytes 393224 | tf_op jit(solution)/shard_map/ppermute | solution.py:125
  11.4 345.1 %collective-permute-start.28 = (bf16[1,512,128]{2,1,0:T(8,128)(2,1)S(1)}, bf16[1,512,128]{2,1,0:T(8,128)(2,1)S(1)}, u32[]{:S(2)}, u32[]{:S(2)}) collective-permute-start(bf16[1,512,128]{2,1,0:T(8,128)(2,1)S(1)} %bitcast.618), channel_id=1, source_target_pairs={{0,24},{1,25},{2,26},{3,27},{4,28},{5,29},{6,30},{7,31},{8,16},{9,... | collective-permute-start | bytes 393224 | tf_op jit(solution)/shard_map/ppermute | solution.py:125
  354.7 53.5 %collective-permute-start = (bf16[1,256,1024]{2,1,0:T(8,128)(2,1)S(1)}, bf16[1,256,1024]{2,1,0:T(8,128)(2,1)S(1)}, u32[]{:S(2)}, u32[]{:S(2)}) collective-permute-start(bf16[1,256,1024]{2,1,0:T(8,128)(2,1)S(1)} %fusion.64), channel_id=1, source_target_pairs={{0,2},{1,3},{2,0},{3,1},{4,6},{5,7},{6,4},{7,5},{8,10},{9,11},{10,... | collective-permute-start | bytes 1572872 | tf_op jit(solution)/shard_map/ppermute | solution.py:125
  356.5 154.5 %collective-permute-start.37 = (bf16[256,1024]{1,0:T(8,128)(2,1)}, bf16[256,1024]{1,0:T(8,128)(2,1)S(1)}, u32[]{:S(2)}, u32[]{:S(2)}) collective-permute-start(bf16[256,1024]{1,0:T(8,128)(2,1)} %bitcast.649), channel_id=1, source_target_pairs={{0,1},{1,0},{2,3},{3,2},{4,5},{5,4},{6,7},{7,6},{8,9},{9,8},{10,11... | collective-permute-start | bytes 1572872 | tf_op jit(solution)/shard_map/ppermute | solution.py:125
  428.3 54.1 %collective-permute-start.27 = (bf16[8,512,128]{1,2,0:T(8,128)(2,1)S(1)}, bf16[8,512,128]{1,2,0:T(8,128)(2,1)S(1)}, u32[]{:S(2)}, u32[]{:S(2)}) collective-permute-start(bf16[8,512,128]{1,2,0:T(8,128)(2,1)S(1)} %pad_maximum_fusion.11), channel_id=1, source_target_pairs={{0,4},{1,5},{2,6},{3,7},{4,0},{5,1},{6,2},{7,3},{8,12},{9,13},{10,... | collective-permute-start | bytes 3145736 | tf_op jit(solution)/shard_map/ppermute | solution.py:125
  429.4 54.6 %collective-permute-start.23 = (bf16[8,512,128]{1,2,0:T(8,128)(2,1)S(1)}, bf16[8,512,128]{1,2,0:T(8,128)(2,1)S(1)}, u32[]{:S(2)}, u32[]{:S(2)}) collective-permute-start(bf16[8,512,128]{1,2,0:T(8,128)(2,1)S(1)} %pad_maximum_fusion.10), channel_id=1, source_target_pairs={{0,2},{1,3},{2,0},{3,1},{4,6},{5,7},{6,4},{7,5},{8,10},{9,11},{10,... | collective-permute-start | bytes 3145736 | tf_op jit(solution)/shard_map/ppermute | solution.py:125
  429.8 50.6 %collective-permute-start.35 = (bf16[8,512,128]{2,1,0:T(8,128)(2,1)S(1)}, bf16[8,512,128]{2,1,0:T(8,128)(2,1)S(1)}, u32[]{:S(2)}, u32[]{:S(2)}) collective-permute-start(bf16[8,512,128]{2,1,0:T(8,128)(2,1)S(1)} %pad_maximum_fusion.13), channel_id=1, source_target_pairs={{0,24},{1,25},{2,26},{3,27},{4,28},{5,29},{6,30},{7,31},{8,16},{9,... | collective-permute-start | bytes 3145736 | tf_op jit(solution)/shard_map/ppermute | solution.py:125
  431.3 47.8 %collective-permute-start.31 = (bf16[8,512,128]{2,1,0:T(8,128)(2,1)S(1)}, bf16[8,512,128]{2,1,0:T(8,128)(2,1)S(1)}, u32[]{:S(2)}, u32[]{:S(2)}) collective-permute-start(bf16[8,512,128]{2,1,0:T(8,128)(2,1)S(1)} %pad_maximum_fusion.12), channel_id=1, source_target_pairs={{0,8},{1,9},{2,10},{3,11},{4,12},{5,13},{6,14},{7,15},{8,0},{9,1},... | collective-permute-start | bytes 3145736 | tf_op jit(solution)/shard_map/ppermute | solution.py:125
  523.4 47.5 %collective-permute-start.36 = (bf16[256,1024]{1,0:T(8,128)(2,1)S(1)}, bf16[256,1024]{1,0:T(8,128)(2,1)S(1)}, u32[]{:S(2)}, u32[]{:S(2)}) collective-permute-start(bf16[256,1024]{1,0:T(8,128)(2,1)S(1)} %slice.1520), channel_id=1, source_target_pairs={{0,1},{1,0},{2,3},{3,2},{4,5},{5,4},{6,7},{7,6},{8,9},{9,8},{10,11... | collective-permute-start | bytes 1572872 | tf_op jit(solution)/shard_map/ppermute | solution.py:125
  523.9 44.0 %collective-permute-start.38 = (bf16[256,1024]{1,0:T(8,128)(2,1)S(1)}, bf16[256,1024]{1,0:T(8,128)(2,1)S(1)}, u32[]{:S(2)}, u32[]{:S(2)}) collective-permute-start(bf16[256,1024]{1,0:T(8,128)(2,1)S(1)} %slice.1519), channel_id=1, source_target_pairs={{0,1},{1,0},{2,3},{3,2},{4,5},{5,4},{6,7},{7,6},{8,9},{9,8},{10,11... | collective-permute-start | bytes 1572872 | tf_op jit(solution)/shard_map/ppermute | solution.py:125
  536.6 113.1 %collective-permute-start.83 = (bf16[8,512,128]{2,1,0:T(8,128)(2,1)}, bf16[8,512,128]{2,1,0:T(8,128)(2,1)}, u32[]{:S(2)}, u32[]{:S(2)}) collective-permute-start(bf16[8,512,128]{2,1,0:T(8,128)(2,1)} %get-tuple-element.229), channel_id=1, source_target_pairs={{0,24},{1,25},{2,26},{3,27},{4,28},{5,29},{6,30},{7,31},{8,16},{9,... | collective-permute-start | bytes 3145736 | tf_op jit(solution)/shard_map/ppermute | solution.py:125
  544.2 107.3 %collective-permute-start.79 = (bf16[8,512,128]{2,1,0:T(8,128)(2,1)}, bf16[8,512,128]{2,1,0:T(8,128)(2,1)}, u32[]{:S(2)}, u32[]{:S(2)}) collective-permute-start(bf16[8,512,128]{2,1,0:T(8,128)(2,1)} %get-tuple-element.213), channel_id=1, source_target_pairs={{0,8},{1,9},{2,10},{3,11},{4,12},{5,13},{6,14},{7,15},{8,0},{9,1},... | collective-permute-start | bytes 3145736 | tf_op jit(solution)/shard_map/ppermute | solution.py:125
  587.1 67.4 %collective-permute-start.73 = (bf16[8,512,128]{2,1,0:T(8,128)(2,1)}, bf16[8,512,128]{2,1,0:T(8,128)(2,1)}, u32[]{:S(2)}, u32[]{:S(2)}) collective-permute-start(bf16[8,512,128]{2,1,0:T(8,128)(2,1)} %constant_dynamic-update-slice_fusion.174), channel_id=1, source_target_pairs={{0,4},{1,5},{2,6},{3,7},{4,0},{5,1},{6,2},{7,3},{8,12},{9,13},{10,... | collective-permute-start | bytes 3145736 | tf_op jit(solution)/shard_map/ppermute | solution.py:125
  642.3 38.0 %collective-permute-start.69 = (bf16[8,512,128]{2,1,0:T(8,128)(2,1)}, bf16[8,512,128]{2,1,0:T(8,128)(2,1)S(1)}, u32[]{:S(2)}, u32[]{:S(2)}) collective-permute-start(bf16[8,512,128]{2,1,0:T(8,128)(2,1)} %copy-done.113), channel_id=1, source_target_pairs={{0,2},{1,3},{2,0},{3,1},{4,6},{5,7},{6,4},{7,5},{8,10},{9,11},{10,... | collective-permute-start | bytes 3145736 | tf_op jit(solution)/shard_map/ppermute | solution.py:125
  648.2 52.7 %collective-permute-start.62 = (bf16[16,256,128]{2,1,0:T(8,128)(2,1)}, bf16[16,256,128]{2,1,0:T(8,128)(2,1)S(1)}, u32[]{:S(2)}, u32[]{:S(2)}) collective-permute-start(bf16[16,256,128]{2,1,0:T(8,128)(2,1)} %bitcast.191), channel_id=1, source_target_pairs={{0,1},{1,0},{2,3},{3,2},{4,5},{5,4},{6,7},{7,6},{8,9},{9,8},{10,11... | collective-permute-start | bytes 3145736 | tf_op jit(solution)/shard_map/ppermute | solution.py:125
  649.7 53.6 %collective-permute-start.42 = (bf16[2,256,1024]{2,1,0:T(8,128)(2,1)}, bf16[2,256,1024]{2,1,0:T(8,128)(2,1)S(1)}, u32[]{:S(2)}, u32[]{:S(2)}) collective-permute-start(bf16[2,256,1024]{2,1,0:T(8,128)(2,1)} %pad_maximum_fusion.15), channel_id=1, source_target_pairs={{0,1},{1,0},{2,3},{3,2},{4,5},{5,4},{6,7},{7,6},{8,9},{9,8},{10,11... | collective-permute-start | bytes 3145736 | tf_op jit(solution)/shard_map/ppermute | solution.py:125
  704.6 47.8 %collective-permute-start.63 = (bf16[8,256,128]{2,1,0:T(8,128)(2,1)}, bf16[8,256,128]{2,1,0:T(8,128)(2,1)}, u32[]{:S(2)}, u32[]{:S(2)}) collective-permute-start(bf16[8,256,128]{2,1,0:T(8,128)(2,1)} %slice.1065), channel_id=1, source_target_pairs={{0,2},{1,3},{2,0},{3,1},{4,6},{5,7},{6,4},{7,5},{8,10},{9,11},{10,... | collective-permute-start | bytes 1572872 | tf_op jit(solution)/shard_map/ppermute | solution.py:125
  723.7 32.2 %collective-permute-start.87 = (bf16[1,1024,128]{2,1,0:T(8,128)(2,1)S(1)}, bf16[1,1024,128]{2,1,0:T(8,128)(2,1)S(1)}, u32[]{:S(2)}, u32[]{:S(2)}) collective-permute-start(bf16[1,1024,128]{2,1,0:T(8,128)(2,1)S(1)} %maximum_bitcast_fusion.1), channel_id=1, source_target_pairs={{0,2},{1,3},{2,0},{3,1},{4,6},{5,7},{6,4},{7,5},{8,10},{9,11},{10,... | collective-permute-start | bytes 786440 | tf_op jit(solution)/shard_map/ppermute | solution.py:125
  727.0 45.3 %collective-permute-start.77 = (bf16[1,1024,128]{2,1,0:T(8,128)(2,1)S(1)}, bf16[1,1024,128]{2,1,0:T(8,128)(2,1)S(1)}, u32[]{:S(2)}, u32[]{:S(2)}) collective-permute-start(bf16[1,1024,128]{2,1,0:T(8,128)(2,1)S(1)} %maximum_bitcast_fusion), channel_id=1, source_target_pairs={{0,2},{1,3},{2,0},{3,1},{4,6},{5,7},{6,4},{7,5},{8,10},{9,11},{10,... | collective-permute-start | bytes 786440 | tf_op jit(solution)/shard_map/ppermute | solution.py:125
  729.3 25.6 %collective-permute-start.44 = (f32[2,4224]{1,0:T(2,128)S(1)}, f32[2,4224]{1,0:T(2,128)S(1)}, u32[]{:S(2)}, u32[]{:S(2)}) collective-permute-start(f32[2,4224]{1,0:T(2,128)S(1)} %pad_maximum_fusion.62), channel_id=1, source_target_pairs={{0,1},{1,0},{2,3},{3,2},{4,5},{5,4},{6,7},{7,6},{8,9},{9,8},{10,11... | collective-permute-start | bytes 101384 | tf_op jit(solution)/shard_map/ppermute | solution.py:125
  756.0 28.9 %collective-permute-start.88 = (bf16[2,1024,128]{2,1,0:T(8,128)(2,1)S(1)}, bf16[2,1024,128]{2,1,0:T(8,128)(2,1)S(1)}, u32[]{:S(2)}, u32[]{:S(2)}) collective-permute-start(bf16[2,1024,128]{2,1,0:T(8,128)(2,1)S(1)} %pad_maximum_fusion.36), channel_id=1, source_target_pairs={{0,1},{1,0},{2,3},{3,2},{4,5},{5,4},{6,7},{7,6},{8,9},{9,8},{10,11... | collective-permute-start | bytes 1572872 | tf_op jit(solution)/shard_map/ppermute | solution.py:125
  (263 other events, 11329.9 us)

commit v2 on v1

--- a/solution.py
+++ b/solution.py
@@ -151,12 +151,19 @@
     )
 
 
-def places_of(steps, wanted):
-    return wanted
-
-
-def lookup(table, index):
-    return lax.dynamic_index_in_dim(jnp.asarray(np.asarray(table, np.int32)), index, 0, keepdims=False)
+def place_in(codes, offset):
+    place = 0
+    for j, code in enumerate(codes):
+        place = place ^ (((offset >> j) & 1) * code)
+    return place
+
+
+def codes_of(offsets, count):
+    codes, bit = [], 1
+    while bit < count:
+        codes.append(offsets.index(bit))
+        bit *= 2
+    return codes
 
 
 def local(
@@ -196,26 +203,17 @@
     block_steps = chip_steps + [core_step]
 
     def dp_places(steps):
-        code = {a: i for i, (a, _) in enumerate(offsets_of(steps))}
-        return [lookup([code[k ^ r] for r in range(count_dp)], row) for k in range(count_dp)]
+        codes = codes_of([a for a, _ in offsets_of(steps)], count_dp)
+        return [place_in(codes, k ^ row) for k in range(count_dp)]
 
     def block_places(steps):
-        code = {b: i for i, (_, b) in enumerate(offsets_of(steps))}
-        return [lookup([code[k ^ r] for r in range(blocks)], place) for k in range(blocks)]
+        codes = codes_of([b for _, b in offsets_of(steps)], blocks)
+        return [place_in(codes, k ^ place) for k in range(blocks)]
 
     def pair_places(steps):
-        code = {pair: i for i, pair in enumerate(offsets_of(steps))}
+        codes = codes_of([a * chips + b // 2 for a, b in offsets_of(steps)], count_dp * chips)
         flat = row * chips + chip
-        return [
-            lookup(
-                [code[(k ^ r, (x ^ c) * 2)] for r in range(count_dp) for c in range(chips)], flat
-            )
-            for k in range(count_dp)
-            for x in range(chips)
-        ]
-
-    def inverse_places(steps, count, mine, part):
-        return [mine ^ offset[part] for offset in offsets_of(steps)]
+        return [place_in(codes, k ^ flat) for k in range(count_dp * chips)]
 
     def rotated(steps, turn):
         turn = turn % len(steps)

time: 813 us -> 515 us (0.63)
  between operations: 194 us -> 7.71 us
  local copies, waits for them, and re-layouts: 223 us -> 116 us
    dynamic_slice x100 -> x0, local copies, waits for them, and re-layouts: 107 us -> none  [lookup(): lax.dynamic_index_in_dim(jnp.asarray(np.asarray(table, np.int32)), index,...]
    unnamed x583 -> x521, local copies, waits for them, and re-layouts: 52 us -> 52.3 us
  transfers between devices with their start and end apart: 89 -> 89, of which waited for: 29 -> 30; matrix products, arithmetic and copies ran while one was open for 39% -> 40% of each run, Pallas kernels for 0% -> 0%
where the time goes in v2:
time: 515 us; the launch traced here: 505 us
  starting transfers between devices  156 us (30%)
  local copies, waits for them, and re-layouts  116 us (23%)
  waiting for transfers between devices  99.4 us (19%)
  matrix products  66.6 us (13%)
  other arithmetic  60 us (12%)
  between operations  7.71 us (1%)
    ppermute x89, starting transfers between devices, swap(): return lax.ppermute(value, ('dp', 'block'), pairs)  156 us
    ppermute x89, waiting for transfers between devices, swap(): return lax.ppermute(value, ('dp', 'block'), pairs)  99.4 us
    unnamed x521, local copies, waits for them, and re-layouts  52.3 us
    dot_general x4, matrix products, dot_plain(): return jnp.dot(left, right, preferred_element_type=WIDE)  18.6 us
    another operation x4, local copies, waits for them, and re-layouts  17.9 us
    dot_general x8, matrix products, dot_high(): return jnp.dot(left, right, precision=HIGHEST, preferred_element_type=WIDE)  15.6 us
    dot_general x4, matrix products, dot_last(): lax.dot_general(left, right, (((1,), (1,)), ((), ())), preferred_element_...  12.2 us
    convert_element_type x27, other arithmetic, scatter(): held = (held[:half].astype(WIDE) + arrived.astype(WIDE)).astype(held.dtype)  11.2 us
  transfers between devices with their start and end apart: 89, of which 30 were waited for; matrix products, arithmetic and copies ran while one was open for 40% of the time, Pallas kernels for 0%

profile of v2, /device:TPU:1, one launch (start us, length us, event | category | flops | bytes accessed | tf_op | source)
XLA Modules:
  0.0 505.0 jit_solution(16704539103499426601)
XLA Ops:
  2.2 4.2 collective-permute-start.14
  62.0 5.4 %collective-permute-start.37 = (bf16[256,1024]{1,0:T(8,128)(2,1)}, bf16[256,1024]{1,0:T(8,128)(2,1)S(1)}, u32[]{:S(2)}, u32[]{:S(2)}) collective-permute-start(bf16[256,1024]{1,0:T(8,128)(2,1)} %bitcast.549), channel_id=1, source_target_pairs={{0,1},{1,0},{2,3},{3,2},{4,5},{5,4},{6,7},{7,6},{8,9},{9,8},{10,11... | collective-permute-start | bytes 1572872 | tf_op jit(solution)/shard_map/ppermute | solution.py:125
  80.6 4.4 collective-permute-done.33
  90.2 6.5 %collective-permute-start.10 = (bf16[4,32,1024]{2,1,0:T(8,128)(2,1)S(1)}, bf16[4,32,1024]{2,1,0:T(8,128)(2,1)S(1)}, u32[]{:S(2)}, u32[]{:S(2)}) collective-permute-start(bf16[4,32,1024]{2,1,0:T(8,128)(2,1)S(1)} %pad_maximum_fusion.42), channel_id=1, source_target_pairs={{0,8},{1,9},{2,10},{3,11},{4,12},{5,13},{6,14},{7,15},{8,0},{9,1},... | collective-permute-start | bytes 786440 | tf_op jit(solution)/shard_map/ppermute | solution.py:125
  97.8 5.0 collective-permute-done.10
  104.0 4.4 collective-permute-done.7
  120.4 12.3 %collective-permute-start.1 = (bf16[2,256,1024]{2,1,0:T(8,128)(2,1)S(1)}, bf16[2,256,1024]{2,1,0:T(8,128)(2,1)S(1)}, u32[]{:S(2)}, u32[]{:S(2)}) collective-permute-start(bf16[2,256,1024]{2,1,0:T(8,128)(2,1)S(1)} %pad_maximum_fusion.8), channel_id=1, source_target_pairs={{0,1},{1,0},{2,3},{3,2},{4,5},{5,4},{6,7},{7,6},{8,9},{9,8},{10,11... | collective-permute-start | bytes 3145736 | tf_op jit(solution)/shard_map/ppermute | solution.py:125
  136.8 3.7 collective-permute-start.31
  156.6 28.0 %collective-permute-done.31 = bf16[8,512,128]{2,1,0:T(8,128)(2,1)S(1)} collective-permute-done((bf16[8,512,128]{2,1,0:T(8,128)(2,1)S(1)}, bf16[8,512,128]{2,1,0:T(8,128)(2,1)S(1)}, u32[]{:S(2)}, u32[]{:S(2)}) %collective-permute-start.31) | collective-permute-done | bytes 1048608 | tf_op jit(solution)/shard_map/ppermute | solution.py:125
  189.6 3.7 copy.221
  200.2 12.3 %multiply_convert_fusion = (bf16[512,2048]{1,0:T(8,128)(2,1)S(1)}, f32[512,2048]{1,0:T(8,128)S(1)}, f32[512,2048]{1,0:T(8,128)}) fusion(f32[2048]{0:T(1024)S(1)} %bitcast.583, bf16[512,2048]{0,1:T(8,128)(2,1)S(1)} %bitcast.579, bf16[512,2048]{0,1:T(8,128)(2,1)S(1)} %bitcast.581, bf16[256,1024]{1,0:T(8,128)(2,1)S(1)} %collective-permute-done.19, ...), kind=kOutput, calls=%fused_computation.10 | convolution fusion | flops 2227175424 | bytes 15736832 | tf_op jit(solution)/shard_map/dot_general | solution.py:26
  216.2 6.0 %convert_reduce_fusion = (f32[2048]{0:T(1024)S(1)}, bf16[512,2048]{1,0:T(8,128)(2,1)S(1)}) fusion(f32[512,2048]{1,0:T(8,128)S(1)} %get-tuple-element.115, bf16[256,8,8,128]{3,2,1,0:T(8,128)(2,1)S(1)} %bitcast.512, bf16[256,1024]{1,0:T(8,128)(2,1)S(1)} %collective-permute-done.37, bf16[256,1024]{1,0:T(8,128)(2,1)S(1)} %bitcast.550, ...), kind=kOutput, calls=%fused_computation.8 | convolution fusion | flops 2167404544 | bytes 15745024 | tf_op jit(solution)/shard_map/dot_general | solution.py:34
  229.3 4.0 convolution_convert_fusion
  253.8 6.6 %constant_dynamic-slice_fusion.16 = (bf16[512,1,128]{2,1,0:T(2,128)(2,1)S(1)}, bf16[512,1,128]{2,1,0:T(2,128)(2,1)S(1)}, bf16[512,1,128]{2,1,0:T(2,128)(2,1)S(1)...) fusion(bf16[512,16,128]{2,1,0:T(8,128)(2,1)S(1)} %bitcast.488, ...), kind=kLoop, calls=%fused_computation.678 | loop fusion | bytes 4194368 | tf_op jit(solution)/shard_map/dynamic-slice.55
  261.0 6.1 %constant_dynamic-slice_fusion.32 = (bf16[512,1,128]{2,1,0:T(2,128)(2,1)S(1)}, bf16[512,1,128]{2,1,0:T(2,128)(2,1)S(1)}, bf16[512,1,128]{2,1,0:T(2,128)(2,1)S(1)...) fusion(bf16[512,16,128]{2,1,0:T(8,128)(2,1)S(1)} %bitcast.487, ...), kind=kLoop, calls=%fused_computation.694 | loop fusion | bytes 4194368 | tf_op jit(solution)/shard_map/dynamic-slice.39
  283.8 5.2 %constant_dynamic-slice_fusion.44 = (bf16[4,256,1,128]{3,2,1,0:T(2,128)(2,1)S(1)}, bf16[4,256,1,128]{3,2,1,0:T(2,128)(2,1)S(1)}, bf16[4,256,1,128]{3,2,1,0:T(2,1...) fusion(bf16[4,256,8,128]{3,2,1,0:T(8,128)(2,1)S(1)} %bitcast.48, ...), kind=kLoop, calls=%fused_computation.706 | loop fusion | bytes 4194336 | tf_op jit(solution)/shard_map/dynamic-slice.31
  311.6 4.0 fusion.146
  341.2 6.3 %collective-permute-start.57 = (bf16[4,32,1024]{2,1,0:T(8,128)(2,1)}, bf16[4,32,1024]{2,1,0:T(8,128)(2,1)S(1)}, u32[]{:S(2)}, u32[]{:S(2)}) collective-permute-start(bf16[4,32,1024]{2,1,0:T(8,128)(2,1)} %pad_maximum_fusion.50), channel_id=1, source_target_pairs={{0,8},{1,9},{2,10},{3,11},{4,12},{5,13},{6,14},{7,15},{8,0},{9,1},... | collective-permute-start | bytes 786440 | tf_op jit(solution)/shard_map/ppermute | solution.py:125
  348.9 4.5 collective-permute-done.57
  371.1 8.2 %collective-permute-done.56 = bf16[1,32,1024]{2,1,0:T(8,128)(2,1)S(1)} collective-permute-done((bf16[1,32,1024]{2,1,0:T(8,128)(2,1)S(1)}, bf16[1,32,1024]{2,1,0:T(8,128)(2,1)S(1)}, u32[]{:S(2)}, u32[]{:S(2)}) %collective-permute-start.56) | collective-permute-done | bytes 65568 | tf_op jit(solution)/shard_map/ppermute | solution.py:125
  394.1 7.4 %collective-permute-start.61 = (bf16[2,3,32,1024]{3,2,1,0:T(8,128)(2,1)S(1)}, bf16[2,3,32,1024]{3,2,1,0:T(8,128)(2,1)S(1)}, u32[]{:S(2)}, u32[]{:S(2)}) collective-permute-start(bf16[2,3,32,1024]{3,2,1,0:T(8,128)(2,1)S(1)} %pad_maximum_fusion.39), channel_id=1, source_target_pairs={{0,1},{1,0},{2,3},{3,2},{4,5},{5,4},{6,7},{7,6},{8,9},{9,8},{10,11... | collective-permute-start | bytes 1179656 | tf_op jit(solution)/shard_map/ppermute | solution.py:125
  418.9 4.6 collective-permute-start.76
  434.5 23.0 %collective-permute-start.44 = (f32[2,4224]{1,0:T(2,128)S(1)}, f32[2,4224]{1,0:T(2,128)S(1)}, u32[]{:S(2)}, u32[]{:S(2)}) collective-permute-start(f32[2,4224]{1,0:T(2,128)S(1)} %pad_maximum_fusion.62), channel_id=1, source_target_pairs={{0,1},{1,0},{2,3},{3,2},{4,5},{5,4},{6,7},{7,6},{8,9},{9,8},{10,11... | collective-permute-start | bytes 101384 | tf_op jit(solution)/shard_map/ppermute | solution.py:125
  477.6 5.4 %collective-permute-start.78 = (bf16[2,1024,128]{2,1,0:T(8,128)(2,1)S(1)}, bf16[2,1024,128]{2,1,0:T(8,128)(2,1)S(1)}, u32[]{:S(2)}, u32[]{:S(2)}) collective-permute-start(bf16[2,1024,128]{2,1,0:T(8,128)(2,1)S(1)} %pad_maximum_fusion.35), channel_id=1, source_target_pairs={{0,1},{1,0},{2,3},{3,2},{4,5},{5,4},{6,7},{7,6},{8,9},{9,8},{10,11... | collective-permute-start | bytes 1572872 | tf_op jit(solution)/shard_map/ppermute | solution.py:125
  (1034 shorter events, 316.1 us)
Async XLA Ops:
  2.2 46.3 %collective-permute-start.14 = (bf16[1,256,128]{2,1,0:T(8,128)(2,1)}, bf16[1,256,128]{2,1,0:T(8,128)(2,1)}, u32[]{:S(2)}, u32[]{:S(2)}) collective-permute-start(bf16[1,256,128]{2,1,0:T(8,128)(2,1)} %bitcast.15), channel_id=1, source_target_pairs={{0,24},{1,25},{2,26},{3,27},{4,28},{5,29},{6,30},{7,31},{8,16},{9,... | collective-permute-start | bytes 196616 | tf_op jit(solution)/shard_map/ppermute | solution.py:125
  7.5 62.5 %collective-permute-start.24 = (bf16[1,512,128]{1,2,0:T(8,128)(2,1)S(1)}, bf16[1,512,128]{1,2,0:T(8,128)(2,1)S(1)}, u32[]{:S(2)}, u32[]{:S(2)}) collective-permute-start(bf16[1,512,128]{1,2,0:T(8,128)(2,1)S(1)} %bitcast.523), channel_id=1, source_target_pairs={{0,8},{1,9},{2,10},{3,11},{4,12},{5,13},{6,14},{7,15},{8,0},{9,1},... | collective-permute-start | bytes 393224 | tf_op jit(solution)/shard_map/ppermute | solution.py:125
  7.7 59.8 %collective-permute-start.20 = (bf16[1,512,128]{1,2,0:T(8,128)(2,1)S(1)}, bf16[1,512,128]{1,2,0:T(8,128)(2,1)}, u32[]{:S(2)}, u32[]{:S(2)}) collective-permute-start(bf16[1,512,128]{1,2,0:T(8,128)(2,1)S(1)} %bitcast.527), channel_id=1, source_target_pairs={{0,4},{1,5},{2,6},{3,7},{4,0},{5,1},{6,2},{7,3},{8,12},{9,13},{10,... | collective-permute-start | bytes 393224 | tf_op jit(solution)/shard_map/ppermute | solution.py:125
  10.0 57.4 %collective-permute-start.32 = (bf16[1,512,128]{2,1,0:T(8,128)(2,1)S(1)}, bf16[1,512,128]{2,1,0:T(8,128)(2,1)S(1)}, u32[]{:S(2)}, u32[]{:S(2)}) collective-permute-start(bf16[1,512,128]{2,1,0:T(8,128)(2,1)S(1)} %bitcast.513), channel_id=1, source_target_pairs={{0,2},{1,3},{2,0},{3,1},{4,6},{5,7},{6,4},{7,5},{8,10},{9,11},{10,... | collective-permute-start | bytes 393224 | tf_op jit(solution)/shard_map/ppermute | solution.py:125
  11.3 50.7 %collective-permute-start.28 = (bf16[1,512,128]{2,1,0:T(8,128)(2,1)S(1)}, bf16[1,512,128]{2,1,0:T(8,128)(2,1)S(1)}, u32[]{:S(2)}, u32[]{:S(2)}) collective-permute-start(bf16[1,512,128]{2,1,0:T(8,128)(2,1)S(1)} %bitcast.518), channel_id=1, source_target_pairs={{0,24},{1,25},{2,26},{3,27},{4,28},{5,29},{6,30},{7,31},{8,16},{9,... | collective-permute-start | bytes 393224 | tf_op jit(solution)/shard_map/ppermute | solution.py:125
  60.2 53.9 %collective-permute-start = (bf16[1,256,1024]{2,1,0:T(8,128)(2,1)S(1)}, bf16[1,256,1024]{2,1,0:T(8,128)(2,1)S(1)}, u32[]{:S(2)}, u32[]{:S(2)}) collective-permute-start(bf16[1,256,1024]{2,1,0:T(8,128)(2,1)S(1)} %fusion.64), channel_id=1, source_target_pairs={{0,2},{1,3},{2,0},{3,1},{4,6},{5,7},{6,4},{7,5},{8,10},{9,11},{10,... | collective-permute-start | bytes 1572872 | tf_op jit(solution)/shard_map/ppermute | solution.py:125
  62.0 154.2 %collective-permute-start.37 = (bf16[256,1024]{1,0:T(8,128)(2,1)}, bf16[256,1024]{1,0:T(8,128)(2,1)S(1)}, u32[]{:S(2)}, u32[]{:S(2)}) collective-permute-start(bf16[256,1024]{1,0:T(8,128)(2,1)} %bitcast.549), channel_id=1, source_target_pairs={{0,1},{1,0},{2,3},{3,2},{4,5},{5,4},{6,7},{7,6},{8,9},{9,8},{10,11... | collective-permute-start | bytes 1572872 | tf_op jit(solution)/shard_map/ppermute | solution.py:125
  86.5 26.0 %collective-permute-start.16 = (bf16[4,256,128]{2,1,0:T(8,128)(2,1)S(1)}, bf16[4,256,128]{2,1,0:T(8,128)(2,1)S(1)}, u32[]{:S(2)}, u32[]{:S(2)}) collective-permute-start(bf16[4,256,128]{2,1,0:T(8,128)(2,1)S(1)} %pad_maximum_fusion.43), channel_id=1, source_target_pairs={{0,4},{1,5},{2,6},{3,7},{4,0},{5,1},{6,2},{7,3},{8,12},{9,13},{10,... | collective-permute-start | bytes 786440 | tf_op jit(solution)/shard_map/ppermute | solution.py:125
  133.8 53.8 %collective-permute-start.27 = (bf16[8,512,128]{1,2,0:T(8,128)(2,1)S(1)}, bf16[8,512,128]{1,2,0:T(8,128)(2,1)S(1)}, u32[]{:S(2)}, u32[]{:S(2)}) collective-permute-start(bf16[8,512,128]{1,2,0:T(8,128)(2,1)S(1)} %pad_maximum_fusion.11), channel_id=1, source_target_pairs={{0,4},{1,5},{2,6},{3,7},{4,0},{5,1},{6,2},{7,3},{8,12},{9,13},{10,... | collective-permute-start | bytes 3145736 | tf_op jit(solution)/shard_map/ppermute | solution.py:125
  134.6 54.6 %collective-permute-start.23 = (bf16[8,512,128]{1,2,0:T(8,128)(2,1)S(1)}, bf16[8,512,128]{1,2,0:T(8,128)(2,1)S(1)}, u32[]{:S(2)}, u32[]{:S(2)}) collective-permute-start(bf16[8,512,128]{1,2,0:T(8,128)(2,1)S(1)} %pad_maximum_fusion.10), channel_id=1, source_target_pairs={{0,2},{1,3},{2,0},{3,1},{4,6},{5,7},{6,4},{7,5},{8,10},{9,11},{10,... | collective-permute-start | bytes 3145736 | tf_op jit(solution)/shard_map/ppermute | solution.py:125
  135.2 50.6 %collective-permute-start.35 = (bf16[8,512,128]{2,1,0:T(8,128)(2,1)S(1)}, bf16[8,512,128]{2,1,0:T(8,128)(2,1)S(1)}, u32[]{:S(2)}, u32[]{:S(2)}) collective-permute-start(bf16[8,512,128]{2,1,0:T(8,128)(2,1)S(1)} %pad_maximum_fusion.13), channel_id=1, source_target_pairs={{0,24},{1,25},{2,26},{3,27},{4,28},{5,29},{6,30},{7,31},{8,16},{9,... | collective-permute-start | bytes 3145736 | tf_op jit(solution)/shard_map/ppermute | solution.py:125
  136.8 47.8 %collective-permute-start.31 = (bf16[8,512,128]{2,1,0:T(8,128)(2,1)S(1)}, bf16[8,512,128]{2,1,0:T(8,128)(2,1)S(1)}, u32[]{:S(2)}, u32[]{:S(2)}) collective-permute-start(bf16[8,512,128]{2,1,0:T(8,128)(2,1)S(1)} %pad_maximum_fusion.12), channel_id=1, source_target_pairs={{0,8},{1,9},{2,10},{3,11},{4,12},{5,13},{6,14},{7,15},{8,0},{9,1},... | collective-permute-start | bytes 3145736 | tf_op jit(solution)/shard_map/ppermute | solution.py:125
  228.7 47.6 %collective-permute-start.36 = (bf16[256,1024]{1,0:T(8,128)(2,1)S(1)}, bf16[256,1024]{1,0:T(8,128)(2,1)S(1)}, u32[]{:S(2)}, u32[]{:S(2)}) collective-permute-start(bf16[256,1024]{1,0:T(8,128)(2,1)S(1)} %slice.1520), channel_id=1, source_target_pairs={{0,1},{1,0},{2,3},{3,2},{4,5},{5,4},{6,7},{7,6},{8,9},{9,8},{10,11... | collective-permute-start | bytes 1572872 | tf_op jit(solution)/shard_map/ppermute | solution.py:125
  229.1 44.2 %collective-permute-start.38 = (bf16[256,1024]{1,0:T(8,128)(2,1)S(1)}, bf16[256,1024]{1,0:T(8,128)(2,1)S(1)}, u32[]{:S(2)}, u32[]{:S(2)}) collective-permute-start(bf16[256,1024]{1,0:T(8,128)(2,1)S(1)} %slice.1519), channel_id=1, source_target_pairs={{0,1},{1,0},{2,3},{3,2},{4,5},{5,4},{6,7},{7,6},{8,9},{9,8},{10,11... | collective-permute-start | bytes 1572872 | tf_op jit(solution)/shard_map/ppermute | solution.py:125
  241.9 113.1 %collective-permute-start.83 = (bf16[8,512,128]{2,1,0:T(8,128)(2,1)}, bf16[8,512,128]{2,1,0:T(8,128)(2,1)}, u32[]{:S(2)}, u32[]{:S(2)}) collective-permute-start(bf16[8,512,128]{2,1,0:T(8,128)(2,1)} %get-tuple-element.229), channel_id=1, source_target_pairs={{0,24},{1,25},{2,26},{3,27},{4,28},{5,29},{6,30},{7,31},{8,16},{9,... | collective-permute-start | bytes 3145736 | tf_op jit(solution)/shard_map/ppermute | solution.py:125
  249.5 107.2 %collective-permute-start.79 = (bf16[8,512,128]{2,1,0:T(8,128)(2,1)}, bf16[8,512,128]{2,1,0:T(8,128)(2,1)}, u32[]{:S(2)}, u32[]{:S(2)}) collective-permute-start(bf16[8,512,128]{2,1,0:T(8,128)(2,1)} %get-tuple-element.213), channel_id=1, source_target_pairs={{0,8},{1,9},{2,10},{3,11},{4,12},{5,13},{6,14},{7,15},{8,0},{9,1},... | collective-permute-start | bytes 3145736 | tf_op jit(solution)/shard_map/ppermute | solution.py:125
  292.3 67.4 %collective-permute-start.73 = (bf16[8,512,128]{2,1,0:T(8,128)(2,1)}, bf16[8,512,128]{2,1,0:T(8,128)(2,1)}, u32[]{:S(2)}, u32[]{:S(2)}) collective-permute-start(bf16[8,512,128]{2,1,0:T(8,128)(2,1)} %constant_dynamic-update-slice_fusion.174), channel_id=1, source_target_pairs={{0,4},{1,5},{2,6},{3,7},{4,0},{5,1},{6,2},{7,3},{8,12},{9,13},{10,... | collective-permute-start | bytes 3145736 | tf_op jit(solution)/shard_map/ppermute | solution.py:125
  347.5 37.9 %collective-permute-start.69 = (bf16[8,512,128]{2,1,0:T(8,128)(2,1)}, bf16[8,512,128]{2,1,0:T(8,128)(2,1)S(1)}, u32[]{:S(2)}, u32[]{:S(2)}) collective-permute-start(bf16[8,512,128]{2,1,0:T(8,128)(2,1)} %copy-done.113), channel_id=1, source_target_pairs={{0,2},{1,3},{2,0},{3,1},{4,6},{5,7},{6,4},{7,5},{8,10},{9,11},{10,... | collective-permute-start | bytes 3145736 | tf_op jit(solution)/shard_map/ppermute | solution.py:125
  353.4 52.5 %collective-permute-start.62 = (bf16[16,256,128]{2,1,0:T(8,128)(2,1)}, bf16[16,256,128]{2,1,0:T(8,128)(2,1)S(1)}, u32[]{:S(2)}, u32[]{:S(2)}) collective-permute-start(bf16[16,256,128]{2,1,0:T(8,128)(2,1)} %bitcast.91), channel_id=1, source_target_pairs={{0,1},{1,0},{2,3},{3,2},{4,5},{5,4},{6,7},{7,6},{8,9},{9,8},{10,11... | collective-permute-start | bytes 3145736 | tf_op jit(solution)/shard_map/ppermute | solution.py:125
  355.0 53.5 %collective-permute-start.42 = (bf16[2,256,1024]{2,1,0:T(8,128)(2,1)}, bf16[2,256,1024]{2,1,0:T(8,128)(2,1)S(1)}, u32[]{:S(2)}, u32[]{:S(2)}) collective-permute-start(bf16[2,256,1024]{2,1,0:T(8,128)(2,1)} %pad_maximum_fusion.15), channel_id=1, source_target_pairs={{0,1},{1,0},{2,3},{3,2},{4,5},{5,4},{6,7},{7,6},{8,9},{9,8},{10,11... | collective-permute-start | bytes 3145736 | tf_op jit(solution)/shard_map/ppermute | solution.py:125
  409.7 47.8 %collective-permute-start.63 = (bf16[8,256,128]{2,1,0:T(8,128)(2,1)}, bf16[8,256,128]{2,1,0:T(8,128)(2,1)}, u32[]{:S(2)}, u32[]{:S(2)}) collective-permute-start(bf16[8,256,128]{2,1,0:T(8,128)(2,1)} %slice.1065), channel_id=1, source_target_pairs={{0,2},{1,3},{2,0},{3,1},{4,6},{5,7},{6,4},{7,5},{8,10},{9,11},{10,... | collective-permute-start | bytes 1572872 | tf_op jit(solution)/shard_map/ppermute | solution.py:125
  428.8 32.2 %collective-permute-start.87 = (bf16[1,1024,128]{2,1,0:T(8,128)(2,1)S(1)}, bf16[1,1024,128]{2,1,0:T(8,128)(2,1)S(1)}, u32[]{:S(2)}, u32[]{:S(2)}) collective-permute-start(bf16[1,1024,128]{2,1,0:T(8,128)(2,1)S(1)} %maximum_bitcast_fusion.1), channel_id=1, source_target_pairs={{0,2},{1,3},{2,0},{3,1},{4,6},{5,7},{6,4},{7,5},{8,10},{9,11},{10,... | collective-permute-start | bytes 786440 | tf_op jit(solution)/shard_map/ppermute | solution.py:125
  432.1 45.4 %collective-permute-start.77 = (bf16[1,1024,128]{2,1,0:T(8,128)(2,1)S(1)}, bf16[1,1024,128]{2,1,0:T(8,128)(2,1)S(1)}, u32[]{:S(2)}, u32[]{:S(2)}) collective-permute-start(bf16[1,1024,128]{2,1,0:T(8,128)(2,1)S(1)} %maximum_bitcast_fusion), channel_id=1, source_target_pairs={{0,2},{1,3},{2,0},{3,1},{4,6},{5,7},{6,4},{7,5},{8,10},{9,11},{10,... | collective-permute-start | bytes 786440 | tf_op jit(solution)/shard_map/ppermute | solution.py:125
  461.0 28.9 %collective-permute-start.88 = (bf16[2,1024,128]{2,1,0:T(8,128)(2,1)S(1)}, bf16[2,1024,128]{2,1,0:T(8,128)(2,1)S(1)}, u32[]{:S(2)}, u32[]{:S(2)}) collective-permute-start(bf16[2,1024,128]{2,1,0:T(8,128)(2,1)S(1)} %pad_maximum_fusion.36), channel_id=1, source_target_pairs={{0,1},{1,0},{2,3},{3,2},{4,5},{5,4},{6,7},{7,6},{8,9},{9,8},{10,11... | collective-permute-start | bytes 1572872 | tf_op jit(solution)/shard_map/ppermute | solution.py:125
  (232 other events, 2200.8 us)

commit v3 on v2

v3 whole, which is shorter than its diff:
```python
import math

import jax
import jax.numpy as jnp
import ml_dtypes
import numpy as np
from jax import lax
from jax.experimental import pallas as pl
from jax.experimental.pallas import tpu as pltpu
from jax.sharding import PartitionSpec as P

EPSILON = 1e-05
MOD_SHIFT = 0.05
HIGHEST = lax.Precision.HIGHEST
HIGH = lax.Precision.HIGH
LOW = jnp.bfloat16
WIDE = jnp.float32


def dot_high(left, right):
    return jnp.dot(left, right, precision=HIGHEST, preferred_element_type=WIDE)


def dot_near(left, right):
    return jnp.dot(left, right, precision=HIGH, preferred_element_type=WIDE)


def dot_plain(left, right):
    return jnp.dot(left, right, preferred_element_type=WIDE)


def dot_first(left, right):
    return lax.dot_general(left, right, (((0,), (0,)), ((), ())), preferred_element_type=WIDE)


def dot_last(left, right):
    return lax.dot_general(left, right, (((1,), (1,)), ((), ())), preferred_element_type=WIDE)


def layer_norm(values, gain, bias):
    mean = jnp.mean(values, axis=-1, keepdims=True)
    centered = values - mean
    variance = jnp.mean(centered * centered, axis=-1, keepdims=True)
    return centered * lax.rsqrt(variance + EPSILON) * gain + bias


def exact_gelu(values):
    return jax.nn.gelu(values, approximate=False)


def position_table(length, emb_dim):
    bands = (emb_dim - 1) // 2
    sample = np.arange(length, dtype=np.float32)
    times = sample / np.float32(length - 1)
    frequency = np.linspace(0.0001, bands - 1, bands).astype(np.float32)
    angle = np.float32(2.0 * math.pi) * sample[:, None] * frequency[None, :] / np.float32(length)
    table = np.concatenate([times[:, None], np.cos(angle), -np.sin(angle)], axis=1)
    return (table.astype(np.float32), times)


def transform_tables(block_len):
    span = 2 * block_len
    frequency = np.arange(block_len)
    sample = np.arange(block_len)
    is_zero = (frequency == 0)[:, None]
    angle = 2.0 * math.pi * (frequency[:, None] * sample[None, :] % span) / span
    alternate = np.where(sample % 2 == 0, 1.0, -1.0)
    real_rows = np.cos(angle)
    imag_rows = np.where(is_zero, alternate[None, :], -np.sin(angle))
    forward_table = np.concatenate([real_rows, imag_rows], axis=0)
    outputs = sample + block_len
    out_angle = 2.0 * math.pi * (outputs[:, None] * frequency[None, :] % span) / span
    out_alternate = np.where(outputs % 2 == 0, 1.0, -1.0)
    zero_col = (frequency == 0)[None, :]
    real_cols = np.where(zero_col, 1.0, 2.0) * np.cos(out_angle) / span
    imag_cols = np.where(zero_col, out_alternate[:, None] / span, -2.0 * np.sin(out_angle) / span)
    inverse_table = np.concatenate([real_cols, imag_cols], axis=1)
    parity = np.where(frequency % 2 == 0, 1.0, -1.0)
    sign = np.concatenate([parity, np.where(frequency == 0, 1.0, parity)])
    edge = (frequency == 0).astype(np.float32)[:, None]
    return tuple(item.astype(np.float32) for item in (forward_table, inverse_table, sign, edge))


def spectral_product(left, right, edge):
    half = left.shape[-2] // 2
    left_re, left_im = (left[..., :half, :], left[..., half:, :])
    right_re, right_im = (right[..., :half, :], right[..., half:, :])
    inside = 1.0 - edge
    out_re = left_re * right_re - inside * left_im * right_im
    out_im = inside * (left_re * right_im + left_im * right_re) + edge * left_im * right_im
    return jnp.concatenate([out_re, out_im], axis=-2)


def spectral_back(grad, other, edge):
    half = grad.shape[-2] // 2
    grad_re, grad_im = (grad[..., :half, :], grad[..., half:, :])
    other_re, other_im = (other[..., :half, :], other[..., half:, :])
    inside = 1.0 - edge
    back_re = grad_re * other_re + inside * grad_im * other_im
    back_im = inside * (grad_im * other_re - grad_re * other_im) + edge * grad_im * other_im
    return jnp.concatenate([back_re, back_im], axis=-2)


class Grid:
    def __init__(self, count_dp, count_block):
        self.count_dp = count_dp
        self.count_block = count_block
        self.row = lax.axis_index("dp")
        self.place = lax.axis_index("block")
        self.dp_steps = []
        bit = 1
        while bit < count_dp:
            self.dp_steps.append((bit | (bit >> 1) if bit == 4 else bit, 0))
            bit *= 2
        self.chip_steps = []
        bit = 2
        while bit < count_block:
            self.chip_steps.append((0, bit | (bit >> 1) if bit == 4 else bit))
            bit *= 2
        self.core_step = (0, 1)

    def swap(self, value, step):
        pairs = []
        for row in range(self.count_dp):
            for place in range(self.count_block):
                to = (row ^ step[0]) * self.count_block + (place ^ step[1])
                pairs.append((row * self.count_block + place, to))
        return lax.ppermute(value, ("dp", "block"), pairs)

    def gather(self, value, steps):
        held = value[None]
        pieces = [held]
        for number, step in enumerate(steps):
            pieces.append(self.swap(held, step))
            if number + 1 < len(steps):
                held = jnp.concatenate(pieces, axis=0)
        return pieces

    def scatter(self, kept, sent, steps):
        for step in reversed(steps):
            arrived = self.swap(sent, step)
            half = kept.shape[0] // 2
            if half:
                sent = add_low(kept[half:], arrived[half:])
                kept = add_low(kept[:half], arrived[:half])
            else:
                kept = add_low(kept, arrived)
        return kept[0]


def add_low(left, right):
    return (left.astype(WIDE) + right.astype(WIDE)).astype(left.dtype)


def offsets_of(steps):
    offsets = [(0, 0)]
    for step in steps:
        offsets = offsets + [(a ^ step[0], b ^ step[1]) for a, b in offsets]
    return offsets


def arrange(pieces, mine, offsets):
    shape = pieces[0].shape[1:]
    if shape[-2] % 32 or shape[-1] % 128:
        held = jnp.concatenate(pieces, axis=0)
        codes = codes_of(offsets, len(offsets))
        return jnp.concatenate(
            [
                lax.dynamic_slice_in_dim(held, place_in(codes, k ^ mine), 1, 0)
                for k in range(len(offsets))
            ],
            axis=0,
        )
    count = len(pieces)

    def kernel(mine_ref, *refs):
        source, target = refs[:count], refs[count]
        at = 0
        for ref in source:
            for i in range(ref.shape[0]):
                target[mine_ref[0] ^ offsets[at]] = ref[i]
                at += 1

    return pl.pallas_call(
        kernel,
        out_shape=jax.ShapeDtypeStruct((len(offsets), *shape), pieces[0].dtype),
        in_specs=[pl.BlockSpec(memory_space=pltpu.SMEM)]
        + [pl.BlockSpec(memory_space=pltpu.VMEM)] * count,
        out_specs=pl.BlockSpec(memory_space=pltpu.VMEM),
    )(jnp.reshape(mine, (1,)).astype(jnp.int32), *pieces)


def deal(natural, mine, offsets):
    half = len(offsets) // 2
    shape = natural.shape[1:]
    if shape[-2] % 32 or shape[-1] % 128:
        dealt = [lax.dynamic_slice_in_dim(natural, mine ^ offset, 1, 0) for offset in offsets]
        return jnp.concatenate(dealt[:half], axis=0), jnp.concatenate(dealt[half:], axis=0)

    def kernel(mine_ref, source, kept, sent):
        for at, offset in enumerate(offsets):
            if at < half:
                kept[at] = source[mine_ref[0] ^ offset]
            else:
                sent[at - half] = source[mine_ref[0] ^ offset]

    out = jax.ShapeDtypeStruct((half, *shape), natural.dtype)
    vmem = pl.BlockSpec(memory_space=pltpu.VMEM)
    return pl.pallas_call(
        kernel,
        out_shape=(out, out),
        in_specs=[pl.BlockSpec(memory_space=pltpu.SMEM), vmem],
        out_specs=(vmem, vmem),
    )(jnp.reshape(mine, (1,)).astype(jnp.int32), natural)


def place_in(codes, offset):
    place = 0
    for j, code in enumerate(codes):
        place = place ^ (((offset >> j) & 1) * code)
    return place


def codes_of(offsets, count):
    codes, bit = [], 1
    while bit < count:
        codes.append(offsets.index(bit))
        bit *= 2
    return codes


def split_low(values):
    high = values.astype(LOW)
    return high, (values - high.astype(WIDE)).astype(LOW)


def triple(table):
    high = table.astype(ml_dtypes.bfloat16)
    low = (table - high.astype(np.float32)).astype(ml_dtypes.bfloat16)
    return np.concatenate([high, high, low], axis=1)


def store_triple(target, columns, values):
    high, low = split_low(values)
    size = values.shape[0]
    target[0:size, columns] = high
    target[size : 2 * size, columns] = low
    target[2 * size : 3 * size, columns] = high


def long_range(starts, count, block_len, length):
    begin, end, before = starts[0], jnp.int32(length), jnp.int32(-1)
    for d in range(count):
        begin = jnp.where(starts[d] <= block_len, starts[d], begin)
        before = before + jnp.where(starts[d] <= block_len, 1, 0)
    for d in reversed(range(count)):
        end = jnp.where(starts[d] > block_len, starts[d], end)
    return begin, end, before


def short_range(starts, count, number, before, block_len, length):
    early = number < before
    bounds = [starts[d] for d in range(count)] + [jnp.int32(length)]
    begin = jnp.where(early, bounds[number], bounds[number + 1])
    end = jnp.where(early, bounds[number + 1], bounds[number + 2])
    return begin, end, jnp.where(early, 0, length - block_len)


def rows_from(base, size, lanes):
    return lax.broadcasted_iota(jnp.int32, (size, lanes), 0) + base


def inside_mask(base, size, lanes, begin, end):
    rows = rows_from(base, size, lanes)
    return (rows >= begin) & (rows < end)


def keep_masks(starts, count, base, size, lanes):
    rows = rows_from(base, size, lanes)
    one = rows != starts[0]
    for d in range(1, count):
        one = one & (rows != starts[d])
    two = one
    for d in range(count):
        two = two & (rows != starts[d] + 1)
    return one, two


VMEM_SPACE = pl.BlockSpec(memory_space=pltpu.VMEM)
ANY_SPACE = pl.BlockSpec(memory_space=pl.ANY)
SMEM_SPACE = pl.BlockSpec(memory_space=pltpu.SMEM)
LIMIT = 56 * 1024 * 1024


class Copies:
    def __init__(self, sems):
        self.sems, self.used = sems, 0

    def start(self, source, target):
        copy = pltpu.make_async_copy(source, target, self.sems.at[self.used])
        self.used += 1
        copy.start()
        return copy


def filter_kernel(block_len, blocks, table_ref, w1, w2, vec, third_at, f3_ref, spectra):
    length = block_len * blocks
    channels = vec.shape[1]
    one_row = jnp.where(lax.broadcasted_iota(jnp.int32, (8, length), 0) == 0, 1.0, 0.0)

    def turned(left, right):
        return lax.dot_general(
            left, right, (((0,), (0,)), ((), ())), precision=HIGHEST, preferred_element_type=WIDE
        )

    first = jnp.sin(turned(w1[...], table_ref[...]))
    second = jnp.sin(turned(w2[...], jnp.concatenate([first, one_row], axis=0)))
    decay = vec[third_at - 2 : third_at - 1, :]
    third_w = vec[third_at : third_at + second.shape[0], :]
    before = None
    half_rows = lax.broadcasted_iota(jnp.int32, (2 * block_len, channels), 0)
    parity = jnp.where(half_rows % 2 == 0, 1.0, -1.0)
    sign = jnp.where(half_rows == block_len, 1.0, parity)
    for i in range(blocks):
        part = turned(second[:, i * block_len : (i + 1) * block_len], third_w)
        times = rows_from(i * block_len, block_len, channels).astype(WIDE) / (length - 1)
        part = part * (jnp.exp(-times * decay) + MOD_SHIFT)
        high, low = split_low(part)
        stacked = jnp.concatenate([high, low, high], axis=0)
        half = jnp.dot(f3_ref[...], stacked, preferred_element_type=WIDE)
        spectra[i] = sign * half if before is None else before + sign * half
        before = half


def with_bias(weights, bias):
    rows = weights.shape[0]
    return jnp.pad(jnp.concatenate([weights, bias[None]], axis=0), ((0, -(rows + 1) % 8), (0, 0)))


def turned_table(table):
    length, count = table.shape
    rows = [table.T, np.ones((1, length), np.float32)]
    rows.append(np.zeros((-(count + 1) % 8, length), np.float32))
    return np.concatenate(rows, axis=0)


def filter_call(block_len, blocks, table, f3, w1, w2, vec, third_at):
    channels = vec.shape[1]

    def body(table_ref, w1_ref, w2_ref, vec_ref, f3_ref, spectra):
        filter_kernel(
            block_len, blocks, table_ref, w1_ref, w2_ref, vec_ref, third_at, f3_ref, spectra
        )

    return pl.pallas_call(
        body,
        out_shape=jax.ShapeDtypeStruct((blocks, 2 * block_len, channels), WIDE),
        in_specs=[VMEM_SPACE] * 5,
        out_specs=VMEM_SPACE,
        compiler_params=pltpu.CompilerParams(vmem_limit_bytes=LIMIT),
    )(table, w1, w2, vec, f3)


def gather_in(copies, pieces, mine, offsets, target):
    started, at = [], 0
    for ref in pieces:
        for i in range(ref.shape[0]):
            started.append(copies.start(ref.at[i], target.at[mine ^ offsets[at]]))
            at += 1
    return started


def conv_call(
    block_len, blocks, places, starts, normed_pieces, in_pieces, in_offsets, block_offsets, vec, spectra, f3, i3
):
    length = block_len * blocks
    channels = vec.shape[1]
    docs = starts.shape[0]
    entries = blocks + docs - 1
    width = normed_pieces[0].shape[-1]
    groups = len(in_pieces)
    share = in_pieces[0][0].shape[1]
    count_dp = len(in_offsets[0])
    flat_in = [piece for pieces in in_pieces for piece in pieces]
    n_norm, n_in, n_out = len(normed_pieces), len(flat_in), blocks
    step = 16

    def body(place_ref, starts_ref, vec_ref, f3_ref, i3_ref, spectra_ref, *refs):
        norm_refs, in_refs = refs[:n_norm], refs[n_norm : n_norm + n_in]
        refs = refs[n_norm + n_in :]
        gated_refs, (proj_out, entry_out, mixed_out, rows_out, norm_out) = refs[:n_out], refs[n_out : n_out + 5]
        norm, rows, proj, inner, gate, xs, ent, ys, mixed, spec, sems = refs[n_out + 5 :]
        row, place = place_ref[0], place_ref[1]
        copies = Copies(sems)
        waiting = gather_in(copies, norm_refs, place, block_offsets, norm)
        at = 0
        for g in range(groups):
            count = len(in_pieces[g])
            index = 0
            for ref in in_refs[at : at + count]:
                for i in range(ref.shape[0]):
                    to = row ^ in_offsets[g][index]
                    waiting.append(copies.start(ref.at[i], rows.at[to, g]))
                    index += 1
            at += count
        spec_copy = copies.start(spectra_ref, spec)
        for copy in waiting:
            copy.wait()
        leaving = [copies.start(norm, norm_out), copies.start(rows, rows_out)]

        flat_rows = rows[...].reshape(3 * channels, width)
        for role in range(3):
            weights = flat_rows[role * channels : (role + 1) * channels]
            bias = vec_ref[role : role + 1, :]
            for b in range(blocks):
                proj[b * block_len : (b + 1) * block_len, role * channels : (role + 1) * channels] = (
                    lax.dot_general(
                        norm[b],
                        weights,
                        (((1,), (1,)), ((), ())),
                        preferred_element_type=WIDE,
                    )
                    + bias
                )
        leaving.append(copies.start(proj, proj_out))
        for b in range(blocks):
            base = b * block_len
            one, two = keep_masks(starts_ref, docs, base, block_len, channels)
            parts = []
            for role in range(3):
                lanes = slice(role * channels, (role + 1) * channels)
                here = proj[base : base + block_len, lanes]
                if b:
                    back = proj[base - 8 : base + block_len, lanes]
                    prev_one = pltpu.roll(back, 1, 0)[8:]
                    prev_two = pltpu.roll(back, 2, 0)[8:]
                else:
                    prev_one, prev_two = pltpu.roll(here, 1, 0), pltpu.roll(here, 2, 0)
                tap = [vec_ref[3 + 3 * j + role : 4 + 3 * j + role, :] for j in range(3)]
                short = (
                    vec_ref[12 + role : 13 + role, :]
                    + tap[0] * here
                    + tap[1] * jnp.where(one, prev_one, 0.0)
                    + tap[2] * jnp.where(two, prev_two, 0.0)
                )
                parts.append(short)
            gate[base : base + block_len] = parts[0]
            inner[base : base + block_len] = parts[1] * parts[2]
        begin, end, before = long_range(starts_ref, docs, block_len, length)
        for b in range(blocks):
            mask = inside_mask(b * block_len, block_len, channels, begin, end)
            part = jnp.where(mask, inner[b * block_len : (b + 1) * block_len], 0.0)
            store_triple(xs, slice(b * channels, (b + 1) * channels), part)
        for m in range(docs - 1):
            first, last, base = short_range(starts_ref, docs, m, before, block_len, length)
            base = pl.multiple_of(base, block_len)
            mask = inside_mask(base, block_len, channels, first, last)
            part = jnp.where(mask, inner[pl.ds(base, block_len)], 0.0)
            store_triple(xs, slice((blocks + m) * channels, (blocks + m + 1) * channels), part)
        for e in range(entries):
            ent[e] = jnp.dot(
                f3_ref[...], xs[:, e * channels : (e + 1) * channels], preferred_element_type=WIDE
            )
        leaving.append(copies.start(ent, entry_out))
        spec_copy.wait()

        @pl.loop(0, block_len // step)
        def _(number):
            at_re = pl.multiple_of(number * step, step)
            at_im = pl.multiple_of(number * step + block_len, step)
            edge = jnp.where(rows_from(at_re, step, channels) == 0, 1.0, 0.0)
            inside = 1.0 - edge
            keys = [(spec[k, pl.ds(at_re, step)], spec[k, pl.ds(at_im, step)]) for k in range(blocks)]
            held = [(ent[k, pl.ds(at_re, step)], ent[k, pl.ds(at_im, step)]) for k in range(blocks)]
            for e in range(entries):
                pairs = (
                    [(held[j], keys[e - j]) for j in range(e + 1)]
                    if e < blocks
                    else [((ent[e, pl.ds(at_re, step)], ent[e, pl.ds(at_im, step)]), keys[0])]
                )
                rr = ii = ri = None
                for (a, b), (c, d) in pairs:
                    rr = a * c if rr is None else rr + a * c
                    ii = b * d if ii is None else ii + b * d
                    ri = a * d + b * c if ri is None else ri + (a * d + b * c)
                lanes = slice(e * channels, (e + 1) * channels)
                out_re = rr - inside * ii
                out_im = inside * ri + edge * ii
                for part, at in ((out_re, at_re), (out_im, at_im)):
                    high, low = split_low(part)
                    ys[pl.ds(at, step), lanes] = high
                    ys[pl.ds(at + 2 * block_len, step), lanes] = low
                    ys[pl.ds(at + 4 * block_len, step), lanes] = high

        direct = vec_ref[16:17, :]
        for b in range(blocks):
            back = jnp.dot(
                i3_ref[...], ys[:, b * channels : (b + 1) * channels], preferred_element_type=WIDE
            )
            rows_here = slice(b * block_len, (b + 1) * block_len)
            mask = inside_mask(b * block_len, block_len, channels, begin, end)
            mixed[rows_here] = jnp.where(mask, back, 0.0) + direct * inner[rows_here]
        for m in range(docs - 1):
            lanes = slice((blocks + m) * channels, (blocks + m + 1) * channels)
            back = jnp.dot(i3_ref[...], ys[:, lanes], preferred_element_type=WIDE)
            first, last, base = short_range(starts_ref, docs, m, before, block_len, length)
            base = pl.multiple_of(base, block_len)
            mask = inside_mask(base, block_len, channels, first, last)
            where = pl.ds(base, block_len)
            mixed[where] = mixed[where] + jnp.where(mask, back, 0.0)
        leaving.append(copies.start(mixed, mixed_out))
        for index, offset in enumerate(block_offsets):
            where = pl.ds(pl.multiple_of((place ^ offset) * block_len, block_len), block_len)
            gated_refs[index][...] = (gate[where] * mixed[where]).astype(LOW)
        for copy in leaving:
            copy.wait()

    shape = jax.ShapeDtypeStruct
    sem_count = blocks + groups * count_dp + 6
    return pl.pallas_call(
        body,
        out_shape=[shape((block_len, channels), LOW)] * blocks
        + [
            shape((length, 3 * channels), WIDE),
            shape((entries, 2 * block_len, channels), WIDE),
            shape((length, channels), WIDE),
            shape((count_dp, groups, share, width), LOW),
            shape((blocks, block_len, width), LOW),
        ],
        in_specs=[SMEM_SPACE, SMEM_SPACE, VMEM_SPACE, VMEM_SPACE, VMEM_SPACE, ANY_SPACE]
        + [ANY_SPACE] * (n_norm + n_in),
        out_specs=[VMEM_SPACE] * blocks + [ANY_SPACE] * 5,
        scratch_shapes=[
            pltpu.VMEM((blocks, block_len, width), LOW),
            pltpu.VMEM((count_dp, groups, share, width), LOW),
            pltpu.VMEM((length, 3 * channels), WIDE),
            pltpu.VMEM((length, channels), WIDE),
            pltpu.VMEM((length, channels), WIDE),
            pltpu.VMEM((3 * block_len, entries * channels), LOW),
            pltpu.VMEM((entries, 2 * block_len, channels), WIDE),
            pltpu.VMEM((6 * block_len, entries * channels), LOW),
            pltpu.VMEM((length, channels), WIDE),
            pltpu.VMEM((blocks, 2 * block_len, channels), WIDE),
            pltpu.SemaphoreType.DMA((sem_count,)),
        ],
        compiler_params=pltpu.CompilerParams(vmem_limit_bytes=LIMIT),
    )(places, starts, vec, f3, i3, spectra, *normed_pieces, *flat_in)


def back_call(
    block_len,
    blocks,
    places,
    starts,
    grad_pieces,
    in_offsets,
    block_offsets,
    vec,
    norm1,
    spectra,
    proj,
    entries,
    mixed,
    in_rows,
    normed,
    it3,
    ft3,
):
    length = block_len * blocks
    channels = vec.shape[1]
    docs = starts.shape[0]
    count = entries.shape[0]
    count_dp, groups, share, width = in_rows.shape
    three = 3 * channels
    step = 16
    half_dp, half_block = count_dp // 2, blocks // 2

    def body(place_ref, starts_ref, vec_ref, norm1_ref, it3_ref, ft3_ref, *refs):
        grad_refs, refs = refs[:blocks], refs[blocks:]
        spectra_ref, proj_ref, entry_ref, mixed_ref, rows_ref, norm_ref = refs[:6]
        refs = refs[6:]
        dealt_refs = [(refs[2 * g], refs[2 * g + 1]) for g in range(groups)]
        refs = refs[2 * groups :]
        gn_kept, gn_sent, lags, sums, norm_sums = refs[:5]
        spec, proj, ent, mixed, rows, norm, gg, short, gs, gm, xs, gt, ys, gi, gp, gr, sems = refs[5:]
        row, place = place_ref[0], place_ref[1]
        copies = Copies(sems)
        proj_copy = copies.start(proj_ref, proj)
        mixed_copy = copies.start(mixed_ref, mixed)
        spec_copy = copies.start(spectra_ref, spec)
        entry_copy = copies.start(entry_ref, ent)
        rows_copy = copies.start(rows_ref, rows)
        norm_copy = copies.start(norm_ref, norm)
        for index, offset in enumerate(block_offsets):
            where = pl.ds(pl.multiple_of((place ^ offset) * block_len, block_len), block_len)
            gg[where] = grad_refs[index][...]
        proj_copy.wait()
        mixed_copy.wait()
        direct = vec_ref[16:17, :]
        direct_sum = jnp.zeros((1, channels), WIDE)
        for b in range(blocks):
            base = b * block_len
            here = slice(base, base + block_len)
            one, two = keep_masks(starts_ref, docs, base, block_len, channels)
            parts = []
            for role in range(3):
                lanes = slice(role * channels, (role + 1) * channels)
                now = proj[here, lanes]
                if b:
                    back = proj[base - 8 : base + block_len, lanes]
                    prev_one, prev_two = pltpu.roll(back, 1, 0)[8:], pltpu.roll(back, 2, 0)[8:]
                else:
                    prev_one, prev_two = pltpu.roll(now, 1, 0), pltpu.roll(now, 2, 0)
                tap = [vec_ref[3 + 3 * j + role : 4 + 3 * j + role, :] for j in range(3)]
                parts.append(
                    vec_ref[12 + role : 13 + role, :]
                    + tap[0] * now
                    + tap[1] * jnp.where(one, prev_one, 0.0)
                    + tap[2] * jnp.where(two, prev_two, 0.0)
                )
            grad = gg[here].astype(WIDE)
            gs[here, :channels] = grad * mixed[here]
            grad = grad * parts[0]
            gm[here] = grad
            short[here, :channels] = parts[1]
            short[here, channels:] = parts[2]
            direct_sum = direct_sum + jnp.sum(
                grad * (parts[1] * parts[2]), axis=0, keepdims=True
            )
        gs[length:, :] = jnp.zeros((8, three), WIDE)
        sums[15:16, :] = direct_sum
        begin, end, before = long_range(starts_ref, docs, block_len, length)
        ranges = []
        for m in range(docs - 1):
            first, last, base = short_range(starts_ref, docs, m, before, block_len, length)
            base = pl.multiple_of(base, block_len)
            ranges.append((base, inside_mask(base, block_len, channels, first, last)))
        for b in range(blocks):
            mask = inside_mask(b * block_len, block_len, channels, begin, end)
            part = jnp.where(mask, gm[b * block_len : (b + 1) * block_len], 0.0)
            store_triple(xs, slice(b * channels, (b + 1) * channels), part)
        for m, (base, mask) in enumerate(ranges):
            part = jnp.where(mask, gm[pl.ds(base, block_len)], 0.0)
            store_triple(xs, slice((blocks + m) * channels, (blocks + m + 1) * channels), part)
        for e in range(count):
            gt[e] = jnp.dot(
                it3_ref[...], xs[:, e * channels : (e + 1) * channels], preferred_element_type=WIDE
            )
        spec_copy.wait()
        entry_copy.wait()

        @pl.loop(0, block_len // step)
        def _(number):
            at_re = pl.multiple_of(number * step, step)
            at_im = pl.multiple_of(number * step + block_len, step)
            edge = jnp.where(rows_from(at_re, step, channels) == 0, 1.0, 0.0)
            inside = 1.0 - edge

            def load(ref, k):
                return ref[k, pl.ds(at_re, step)], ref[k, pl.ds(at_im, step)]

            def combine(pairs):
                rr = ii = ri = None
                for (a, b), (c, d) in pairs:
                    rr = a * c if rr is None else rr + a * c
                    ii = b * d if ii is None else ii + b * d
                    ri = b * c - a * d if ri is None else ri + (b * c - a * d)
                return rr + inside * ii, inside * ri + edge * ii

            for e in range(count):
                if e < blocks:
                    pairs = [(load(gt, i), load(spec, i - e)) for i in range(e, blocks)]
                else:
                    pairs = [(load(gt, e), load(spec, 0))]
                lanes = slice(e * channels, (e + 1) * channels)
                for part, at in zip(combine(pairs), (at_re, at_im)):
                    high, low = split_low(part)
                    ys[pl.ds(at, step), lanes] = high
                    ys[pl.ds(at + 2 * block_len, step), lanes] = low
                    ys[pl.ds(at + 4 * block_len, step), lanes] = high
            for k in range(blocks):
                pairs = [(load(gt, j + k), load(ent, j)) for j in range(blocks - k)]
                if k == 0:
                    pairs += [(load(gt, e), load(ent, e)) for e in range(blocks, count)]
                out_re, out_im = combine(pairs)
                lags[k, pl.ds(at_re, step)] = out_re
                lags[k, pl.ds(at_im, step)] = out_im

        for b in range(blocks):
            here = slice(b * block_len, (b + 1) * block_len)
            back = jnp.dot(
                ft3_ref[...], ys[:, b * channels : (b + 1) * channels], preferred_element_type=WIDE
            )
            mask = inside_mask(b * block_len, block_len, channels, begin, end)
            gi[here] = jnp.where(mask, back, 0.0) + direct * gm[here]
        for m, (base, mask) in enumerate(ranges):
            lanes = slice((blocks + m) * channels, (blocks + m + 1) * channels)
            back = jnp.dot(ft3_ref[...], ys[:, lanes], preferred_element_type=WIDE)
            where = pl.ds(base, block_len)
            gi[where] = gi[where] + jnp.where(mask, back, 0.0)
        for b in range(blocks):
            here = slice(b * block_len, (b + 1) * block_len)
            gs[here, channels : 2 * channels] = gi[here] * short[here, channels:]
            gs[here, 2 * channels :] = gi[here] * short[here, :channels]
        for role in range(3):
            lanes = slice(role * channels, (role + 1) * channels)
            tap = [vec_ref[3 + 3 * j + role : 4 + 3 * j + role, :] for j in range(3)]
            totals = [jnp.zeros((1, channels), WIDE) for _ in range(5)]
            for b in range(blocks):
                base = b * block_len
                here = slice(base, base + block_len)
                one, two = keep_masks(starts_ref, docs, base, block_len + 8, channels)
                grad = gs[base : base + block_len + 8, lanes]
                pass_one, pass_two = jnp.where(one, grad, 0.0), jnp.where(two, grad, 0.0)
                size = block_len + 8
                result = (
                    tap[0] * grad[:block_len]
                    + tap[1] * pltpu.roll(pass_one, size - 1, 0)[:block_len]
                    + tap[2] * pltpu.roll(pass_two, size - 2, 0)[:block_len]
                ).astype(LOW)
                gp[here, lanes] = result
                now = proj[here, lanes]
                if b:
                    back = proj[base - 8 : base + block_len, lanes]
                    prev_one, prev_two = pltpu.roll(back, 1, 0)[8:], pltpu.roll(back, 2, 0)[8:]
                else:
                    prev_one, prev_two = pltpu.roll(now, 1, 0), pltpu.roll(now, 2, 0)
                terms = [
                    result.astype(WIDE),
                    grad[:block_len] * now,
                    pass_one[:block_len] * prev_one,
                    pass_two[:block_len] * prev_two,
                    grad[:block_len],
                ]
                totals = [
                    total + jnp.sum(term, axis=0, keepdims=True)
                    for total, term in zip(totals, terms)
                ]
            sums[role : role + 1, :] = totals[0]
            for j in range(3):
                sums[3 + 3 * j + role : 4 + 3 * j + role, :] = totals[1 + j]
            sums[12 + role : 13 + role, :] = totals[4]
        rows_copy.wait()
        norm_copy.wait()
        weights = rows[...].reshape(three, width)
        shift_sum = jnp.zeros((1, width), WIDE)
        scale_sum = jnp.zeros((1, width), WIDE)
        for index, offset in enumerate(block_offsets):
            other = place ^ offset
            where = pl.ds(pl.multiple_of(other * block_len, block_len), block_len)
            part = jnp.dot(gp[where], weights, preferred_element_type=WIDE)
            shift_sum = shift_sum + jnp.sum(part, axis=0, keepdims=True)
            scale_sum = scale_sum + jnp.sum(
                part * norm[other].astype(WIDE), axis=0, keepdims=True
            )
            if index < half_block:
                gn_kept[index] = part.astype(LOW)
            else:
                gn_sent[index - half_block] = part.astype(LOW)
        norm_sums[0:1, :] = (scale_sum - norm1_ref[1:2, :] * shift_sum) / norm1_ref[0:1, :]
        norm_sums[1:2, :] = shift_sum
        for c in range(3):
            lanes = slice(c * channels, (c + 1) * channels)
            total = lax.dot_general(
                gp[:, lanes],
                norm[...].reshape(length, width),
                (((0,), (0,)), ((), ())),
                preferred_element_type=WIDE,
            )
            gr[lanes] = total.astype(LOW)
        dealt = gr.reshape(count_dp, groups, share, width)
        leaving = []
        for g in range(groups):
            for index, offset in enumerate(in_offsets[g]):
                target = dealt_refs[g][index // half_dp].at[index % half_dp]
                leaving.append(copies.start(dealt.at[row ^ offset, g], target))
        for copy in leaving:
            copy.wait()

    shape = jax.ShapeDtypeStruct
    half_in = shape((half_dp, share, width), LOW)
    return pl.pallas_call(
        body,
        out_shape=[half_in] * (2 * groups)
        + [
            shape((half_block, block_len, width), LOW),
            shape((half_block, block_len, width), LOW),
            shape((blocks, 2 * block_len, channels), WIDE),
            shape((16, channels), WIDE),
            shape((2, width), WIDE),
        ],
        in_specs=[SMEM_SPACE] * 2 + [VMEM_SPACE] * (4 + blocks) + [ANY_SPACE] * 6,
        out_specs=[ANY_SPACE] * (2 * groups) + [VMEM_SPACE] * 5,
        scratch_shapes=[
            pltpu.VMEM((blocks, 2 * block_len, channels), WIDE),
            pltpu.VMEM((length, three), WIDE),
            pltpu.VMEM((count, 2 * block_len, channels), WIDE),
            pltpu.VMEM((length, channels), WIDE),
            pltpu.VMEM((count_dp, groups, share, width), LOW),
            pltpu.VMEM((blocks, block_len, width), LOW),
            pltpu.VMEM((length, channels), LOW),
            pltpu.VMEM((length, 2 * channels), WIDE),
            pltpu.VMEM((length + 8, three), WIDE),
            pltpu.VMEM((length, channels), WIDE),
            pltpu.VMEM((3 * block_len, count * channels), LOW),
            pltpu.VMEM((count, 2 * block_len, channels), WIDE),
            pltpu.VMEM((6 * block_len, count * channels), LOW),
            pltpu.VMEM((length, channels), WIDE),
            pltpu.VMEM((length, three), LOW),
            pltpu.VMEM((three, width), LOW),
            pltpu.SemaphoreType.DMA((6 + groups * count_dp,)),
        ],
        compiler_params=pltpu.CompilerParams(vmem_limit_bytes=LIMIT),
    )(
        places,
        starts,
        vec,
        norm1,
        it3,
        ft3,
        *grad_pieces,
        spectra,
        proj,
        entries,
        mixed,
        in_rows,
        normed,
    )


def filter_back_call(block_len, blocks, table, ft3, w1, w2, vec, third_at, lags):
    length = block_len * blocks
    channels = vec.shape[1]
    units = w2.shape[1]

    def body(table_ref, w1_ref, w2_ref, vec_ref, ft3_ref, lags_ref, g1, g2, g3, gd):
        one_row = jnp.where(lax.broadcasted_iota(jnp.int32, (8, length), 0) == 0, 1.0, 0.0)

        def product(left, right, dims):
            return lax.dot_general(
                left, right, (dims, ((), ())), precision=HIGHEST, preferred_element_type=WIDE
            )

        z1 = product(w1_ref[...], table_ref[...], ((0,), (0,)))
        first = jnp.concatenate([jnp.sin(z1), one_row], axis=0)
        z2 = product(w2_ref[...], first, ((0,), (0,)))
        second = jnp.sin(z2)
        decay = vec_ref[third_at - 2 : third_at - 1, :]
        third_w = vec_ref[third_at : third_at + units, :]
        half_rows = lax.broadcasted_iota(jnp.int32, (2 * block_len, channels), 0)
        parity = jnp.where(half_rows % 2 == 0, 1.0, -1.0)
        sign = jnp.where(half_rows == block_len, 1.0, parity)
        third_sum = jnp.zeros((units, channels), WIDE)
        decay_sum = jnp.zeros((1, channels), WIDE)
        back = []
        for i in range(blocks):
            grad = sign * lags_ref[i]
            if i + 1 < blocks:
                grad = grad + lags_ref[i + 1]
            high, low = split_low(grad)
            stacked = jnp.concatenate([high, low, high], axis=0)
            grad = jnp.dot(ft3_ref[...], stacked, preferred_element_type=WIDE)
            here = second[:, i * block_len : (i + 1) * block_len]
            third = product(here, third_w, ((0,), (0,)))
            times = rows_from(i * block_len, block_len, channels).astype(WIDE) / (length - 1)
            fall = jnp.exp(-times * decay)
            decay_sum = decay_sum - jnp.sum(grad * third * fall * times, axis=0, keepdims=True)
            grad = grad * (fall + MOD_SHIFT)
            third_sum = third_sum + product(here, grad, ((1,), (0,)))
            back.append(product(third_w, grad, ((1,), (1,))))
        gz2 = jnp.concatenate(back, axis=1) * jnp.cos(z2)
        g2[...] = product(first, gz2, ((1,), (1,)))
        gz1 = product(w2_ref[:units, :], gz2, ((1,), (0,))) * jnp.cos(z1)
        g1[...] = product(table_ref[...], gz1, ((1,), (1,)))
        g3[...] = third_sum
        gd[...] = decay_sum

    shape = jax.ShapeDtypeStruct
    return pl.pallas_call(
        body,
        out_shape=[
            shape(w1.shape, WIDE),
            shape(w2.shape, WIDE),
            shape((units, channels), WIDE),
            shape((1, channels), WIDE),
        ],
        in_specs=[VMEM_SPACE] * 6,
        out_specs=[VMEM_SPACE] * 4,
        compiler_params=pltpu.CompilerParams(vmem_limit_bytes=LIMIT),
    )(table, w1, w2, vec, ft3, lags)


def local(
    block_in,
    doc_starts,
    norm1_gain,
    norm1_bias,
    w_in,
    b_in,
    short_taps,
    short_bias,
    filter_w1,
    filter_b1,
    filter_w2,
    filter_b2,
    filter_w3,
    filter_decay,
    conv_bias,
    w_out,
    b_out,
    norm2_gain,
    norm2_bias,
    w_up,
    b_up,
    w_down,
    b_down,
    cotangent,
):
    count_dp, blocks = lax.axis_size("dp"), lax.axis_size("block")
    grid = Grid(count_dp, blocks)
    row, place = grid.row, grid.place
    _, block_len, width = block_in.shape
    length = block_len * blocks
    hidden_width = w_up.shape[1] * count_dp
    hidden_here = hidden_width // blocks
    dp_steps = grid.dp_steps
    block_steps = grid.chip_steps + [grid.core_step]
    block_offsets = [b for _, b in offsets_of(block_steps)]

    def rotated(turn):
        turn = turn % len(dp_steps)
        return dp_steps[turn:] + dp_steps[:turn]

    def dp_offsets(steps):
        return [a for a, _ in offsets_of(steps)]

    shard_in, shard_out = w_in.shape[1], w_out.shape[1]
    group = math.gcd(width, shard_in)
    groups_here, share = shard_in // group, group // blocks
    channels = width // blocks
    bands = width // group
    vectors = jnp.concatenate(
        [
            b_in.reshape(3, width),
            short_taps.reshape(9, width),
            short_bias.reshape(3, width),
            filter_decay[None],
            conv_bias[None],
            filter_w3,
        ],
        axis=0,
    )
    vectors = lax.dynamic_index_in_dim(
        vectors.reshape(vectors.shape[0], bands, blocks, share), place, 2, keepdims=False
    ).reshape(vectors.shape[0], channels)
    b_in_here = vectors[:3].reshape(-1)
    taps = vectors[3:12].reshape(3, 3 * channels)
    short_shift = vectors[12:15].reshape(-1)
    decay_here, direct, third_here = vectors[15], vectors[16], vectors[17:]

    in_turned = w_in.T.reshape(groups_here, blocks, share, width)
    in_own = lax.dynamic_index_in_dim(in_turned, place, 1, keepdims=False)
    in_orders = [rotated(i) for i in range(groups_here)]
    in_offsets = [dp_offsets(order) for order in in_orders]
    in_pieces = [grid.gather(in_own[i], in_orders[i]) for i in range(groups_here)]
    kernels = channels % 128 == 0 and share % 32 == 0 and groups_here == 3

    inputs = block_in.astype(WIDE).reshape(block_len, width)
    normed, norm1_back = jax.vjp(layer_norm, inputs, norm1_gain, norm1_bias)
    normed_low = normed.astype(LOW)
    normed_pieces = grid.gather(normed_low, block_steps)

    up_order, down_order, out_dp_order = rotated(1), rotated(2), rotated(0)
    piece = w_up.shape[1] // blocks
    up_own = lax.dynamic_slice_in_dim(w_up, place * piece, piece, 1).T
    up_rows = arrange(grid.gather(up_own, up_order), row, dp_offsets(up_order)).reshape(
        hidden_here, width
    )
    b_up_here = lax.dynamic_index_in_dim(
        b_up.reshape(count_dp, blocks, piece), place, 1, keepdims=False
    ).reshape(hidden_here)
    down_own = w_down.reshape(count_dp, blocks, piece, w_down.shape[1])
    down_own = lax.dynamic_index_in_dim(down_own, place, 1, keepdims=False)
    down_own = down_own.reshape(hidden_here, w_down.shape[1]).T
    down_rows = arrange(grid.gather(down_own, down_order), row, dp_offsets(down_order)).reshape(
        width, hidden_here
    )

    out_own = w_out.reshape(bands, blocks, share, shard_out)
    out_own = lax.dynamic_index_in_dim(out_own, place, 1, keepdims=False)
    out_own = out_own.reshape(channels, shard_out).T
    out_dealt = arrange(grid.gather(out_own, out_dp_order), row, dp_offsets(out_dp_order))
    out_rows = jnp.concatenate(grid.gather(out_dealt.reshape(width, channels), block_steps), axis=0)
    cot_flat = cotangent.reshape(block_len, width)
    cot_all = jnp.concatenate(grid.gather(cot_flat, block_steps), axis=0).reshape(length, width)

    forward_table, inverse_table, sign, edge = transform_tables(block_len)
    starts = doc_starts[0]
    positions = jnp.arange(length, dtype=jnp.int32)
    segment = jnp.sum((starts[None, :] <= positions[:, None]).astype(jnp.int32), axis=-1) - 1
    keep_one = jnp.concatenate([jnp.zeros((1,), WIDE), (segment[1:] == segment[:-1]).astype(WIDE)])
    keep_two = jnp.concatenate([jnp.zeros((2,), WIDE), (segment[2:] == segment[:-2]).astype(WIDE)])
    keep_one, keep_two = keep_one[:, None], keep_two[:, None]
    num_docs = doc_starts.shape[1]
    long_doc = jnp.sum((starts <= block_len).astype(jnp.int32)) - 1
    long_mask = (segment == long_doc).astype(WIDE)[:, None]
    first_segment, last_segment = segment[:block_len], segment[length - block_len :]
    short_early, short_masks = [], []
    for number in range(num_docs - 1):
        early = number < long_doc
        doc = jnp.where(early, number, number + 1)
        where = jnp.where(early, first_segment, last_segment)
        short_early.append(early.astype(WIDE))
        short_masks.append((where == doc).astype(WIDE)[:, None])

    def spread(values):
        masked = values * long_mask
        parts = [masked[i * block_len : (i + 1) * block_len] for i in range(blocks)]
        first, last = values[:block_len], values[length - block_len :]
        for early, mask in zip(short_early, short_masks):
            parts.append(mask * (early * first + (1.0 - early) * last))
        return jnp.concatenate(parts, axis=1)

    def collect(values):
        parts = [
            values[:, i * channels : (i + 1) * channels] for i in range(blocks + num_docs - 1)
        ]
        first, last = jnp.zeros_like(parts[0]), jnp.zeros_like(parts[0])
        for early, mask, part in zip(short_early, short_masks, parts[blocks:]):
            first = first + early * mask * part
            last = last + (1.0 - early) * mask * part
        joined = jnp.concatenate(parts[:blocks], axis=0) * long_mask
        middle = jnp.zeros((length - 2 * block_len, channels), WIDE)
        return joined + jnp.concatenate([first, middle, last], axis=0)

    def cut(values, count):
        return [values[:, i * channels : (i + 1) * channels] for i in range(count)]

    forward_three, inverse_three = triple(forward_table), triple(inverse_table)
    table, times = position_table(length, filter_w1.shape[0])

    if kernels:
        spectra_held = filter_call(
            block_len,
            blocks,
            turned_table(table),
            forward_three,
            with_bias(filter_w1, filter_b1),
            with_bias(filter_w2, filter_b2),
            vectors,
            17,
        )
        made = conv_call(
            block_len,
            blocks,
            jnp.stack([row, place]).astype(jnp.int32),
            starts,
            normed_pieces,
            in_pieces,
            in_offsets,
            block_offsets,
            vectors,
            spectra_held,
            forward_three,
            inverse_three,
        )
        gated_own, (proj, entries_held, mixed, in_rows, normed_all) = made[:blocks], made[blocks:]
    else:
        def filter_spectra(params):
            first = jnp.sin(dot_high(table, params[0]) + params[1])
            second = jnp.sin(dot_high(first, params[2]) + params[3])
            kernel = dot_high(second, params[4]) * (
                jnp.exp(-times[:, None] * params[5][None, :]) + MOD_SHIFT
            )
            pieces = jnp.concatenate(
                [kernel[i * block_len : (i + 1) * block_len] for i in range(blocks)], axis=1
            )
            halves = dot_near(forward_table, pieces)
            earlier = jnp.concatenate(
                [jnp.zeros((2 * block_len, channels), WIDE), halves[:, : (blocks - 1) * channels]],
                axis=1,
            )
            return earlier + sign[:, None] * halves

        spectra_flat, filter_back = jax.vjp(
            filter_spectra,
            (filter_w1, filter_b1, filter_w2, filter_b2, third_here, decay_here),
        )
        normed_all = arrange(normed_pieces, place, block_offsets).reshape(length, width)
        in_rows = jnp.stack(
            [arrange(in_pieces[i], row, in_offsets[i]) for i in range(groups_here)], axis=1
        ).reshape(3 * channels, width)
        spectra = cut(spectra_flat, blocks)
        proj = dot_last(normed_all, in_rows) + b_in_here
    three = 3 * channels
    prev_one = jnp.concatenate([jnp.zeros((1, three), WIDE), proj[:-1]], axis=0) * keep_one
    prev_two = jnp.concatenate([jnp.zeros((2, three), WIDE), proj[:-2]], axis=0) * keep_two
    short = short_shift + taps[0] * proj + taps[1] * prev_one + taps[2] * prev_two
    gate_part, mult, value = cut(short, 3)
    inner = value * mult

    if not kernels:
        entries = cut(dot_near(forward_table, spread(inner)), blocks + num_docs - 1)
        totals = []
        for i in range(blocks):
            total = spectral_product(entries[i], spectra[0], edge)
            for j in range(i):
                total = total + spectral_product(entries[j], spectra[i - j], edge)
            totals.append(total)
        for entry in entries[blocks:]:
            totals.append(spectral_product(entry, spectra[0], edge))
        mixed = collect(dot_near(inverse_table, jnp.concatenate(totals, axis=1))) + direct * inner
        gated_low = (gate_part * mixed).astype(LOW)

        gated_own = [
            lax.dynamic_slice_in_dim(gated_low, (place ^ offset) * block_len, block_len, 0)
            for offset in block_offsets
        ]

    gated_parts = [
        grid.swap(part, (0, offset)) if offset else part
        for part, offset in zip(gated_own, block_offsets)
    ]
    branch = b_out
    for part, rows in zip(gated_parts, out_rows):
        branch = branch + dot_last(part, rows)
    resid = inputs + branch
    normed2, norm2_back = jax.vjp(layer_norm, resid, norm2_gain, norm2_bias)
    normed2_low = normed2.astype(LOW)

    normed2_all = jnp.concatenate(grid.gather(normed2_low, block_steps), axis=0)
    normed2_all = normed2_all.reshape(length, width)
    hidden = dot_last(normed2_all, up_rows) + b_up_here
    act, gelu_back = jax.vjp(exact_gelu, hidden)
    act_low = act.astype(LOW)
    grad_act = dot_plain(cot_all, down_rows)
    grad_hidden = gelu_back(grad_act)[0].astype(LOW)

    def to_tokens(partial):
        split = partial.astype(LOW).reshape(blocks, block_len, width)
        return grid.scatter(split[: blocks // 2], split[blocks // 2 :], block_steps).astype(WIDE)

    grad_normed2 = to_tokens(dot_plain(grad_hidden, up_rows))
    output = resid + to_tokens(dot_last(act_low, down_rows)) + b_down
    block_out = output.astype(LOW)[None]
    grad_b_up_here = jnp.sum(grad_hidden.astype(WIDE), axis=0)
    grad_b_down = jnp.sum(cot_flat.astype(WIDE), axis=0)

    def send_home(natural, order):
        natural = natural.astype(LOW).reshape(count_dp, -1, natural.shape[-1])
        return grid.scatter(*deal(natural, row, dp_offsets(order)), order)

    up_grad = send_home(dot_first(grad_hidden, normed2_all), up_order)
    down_grad = send_home(dot_first(cot_all, act_low), down_order)

    resid_part, grad_gain_two, grad_bias_two = norm2_back(grad_normed2)
    grad_resid = cot_flat.astype(WIDE) + resid_part
    grad_branch = grad_resid.astype(LOW)
    grad_b_out = jnp.sum(grad_branch.astype(WIDE), axis=0)
    grad_parts = []
    for index, offset in enumerate(block_offsets):
        part = dot_plain(grad_branch, out_rows[index]).astype(LOW)
        grad_parts.append((grid.swap(part, (0, offset)) if offset else part)[None])
    out_sums = jnp.stack([dot_first(grad_branch, part).astype(LOW) for part in gated_parts], axis=0)
    out_sums = grid.scatter(out_sums[: blocks // 2], out_sums[blocks // 2 :], block_steps)
    out_grad = send_home(out_sums, out_dp_order)

    if kernels:
        made = back_call(
            block_len,
            blocks,
            jnp.stack([row, place]).astype(jnp.int32),
            starts,
            [part[0] for part in grad_parts],
            in_offsets,
            block_offsets,
            vectors,
            jnp.stack([norm1_gain, norm1_bias]),
            spectra_held,
            proj,
            entries_held,
            mixed,
            in_rows,
            normed_all,
            triple(inverse_table.T),
            triple(forward_table.T),
        )
        in_dealt = [(made[2 * i], made[2 * i + 1]) for i in range(groups_here)]
        made = made[2 * groups_here :]
        normed_dealt, (grad_lags, sums, norm_sums) = made[:2], made[2:]
        grad_b_in, grad_taps, grad_short_bias = sums[:3], sums[3:12], sums[12:15]
        grad_conv_bias = sums[15]
        filter_grads = filter_back_call(
            block_len,
            blocks,
            turned_table(table),
            triple(forward_table.T),
            with_bias(filter_w1, filter_b1),
            with_bias(filter_w2, filter_b2),
            vectors,
            17,
            grad_lags,
        )
        rows_one, rows_two = filter_w1.shape[0], filter_w2.shape[0]
        filter_grads = (
            filter_grads[0][:rows_one],
            filter_grads[0][rows_one],
            filter_grads[1][:rows_two],
            filter_grads[1][rows_two],
            filter_grads[2],
            filter_grads[3][0],
        )
    else:
        grad_gated = arrange(grad_parts, place, block_offsets)
        grad_gated = grad_gated.reshape(length, channels).astype(WIDE)
        grad_gate_part = grad_gated * mixed
        grad_mixed = grad_gated * gate_part
        grad_conv_bias = jnp.sum(grad_mixed * inner, axis=0)
        grad_totals = cut(
            lax.dot_general(
                inverse_table,
                spread(grad_mixed),
                (((0,), (0,)), ((), ())),
                precision=HIGH,
                preferred_element_type=WIDE,
            ),
            blocks + num_docs - 1,
        )
        grad_entries = []
        grad_lags = [None] * blocks
        for i in range(blocks + num_docs - 1):
            lag = spectral_back(grad_totals[i], entries[i], edge)
            grad_lags[0] = lag if grad_lags[0] is None else grad_lags[0] + lag
            grad_entries.append(spectral_back(grad_totals[i], spectra[0], edge))
        for j in range(blocks):
            for i in range(j + 1, blocks):
                grad_entries[j] = grad_entries[j] + spectral_back(
                    grad_totals[i], spectra[i - j], edge
                )
                lag = spectral_back(grad_totals[i], entries[j], edge)
                grad_lags[i - j] = lag if grad_lags[i - j] is None else grad_lags[i - j] + lag
        filter_grads = filter_back(jnp.concatenate(grad_lags, axis=1))[0]
        grad_inner = (
            collect(
                lax.dot_general(
                    forward_table,
                    jnp.concatenate(grad_entries, axis=1),
                    (((0,), (0,)), ((), ())),
                    precision=HIGH,
                    preferred_element_type=WIDE,
                )
            )
            + direct * grad_mixed
        )
        grad_short = jnp.concatenate([grad_gate_part, grad_inner * value, grad_inner * mult], axis=1)
        grad_taps = jnp.stack(
            [
                jnp.sum(grad_short * proj, axis=0),
                jnp.sum(grad_short * prev_one, axis=0),
                jnp.sum(grad_short * prev_two, axis=0),
            ],
            axis=0,
        )
        grad_short_bias = jnp.sum(grad_short, axis=0)
        pass_one = grad_short * keep_one
        pass_two = grad_short * keep_two
        grad_proj = (
            taps[0] * grad_short
            + taps[1] * jnp.concatenate([pass_one[1:], jnp.zeros((1, three), WIDE)], axis=0)
            + taps[2] * jnp.concatenate([pass_two[2:], jnp.zeros((2, three), WIDE)], axis=0)
        )
        grad_proj_low = grad_proj.astype(LOW)
        grad_b_in = jnp.sum(grad_proj_low.astype(WIDE), axis=0)
        grad_in_rows = dot_first(grad_proj_low, normed_all)
        grad_in_split = grad_in_rows.reshape(count_dp, groups_here, share, width)
        in_dealt = [
            deal(grad_in_split[:, i].astype(LOW), row, in_offsets[i]) for i in range(groups_here)
        ]
        grad_normed_part = dot_plain(grad_proj_low, in_rows).astype(LOW)
        normed_dealt = deal(
            grad_normed_part.reshape(blocks, block_len, width), place, block_offsets
        )
    in_grads = [grid.scatter(*in_dealt[i], in_orders[i]) for i in range(groups_here)]
    grad_normed = grid.scatter(*normed_dealt, block_steps).astype(WIDE)
    input_part, grad_gain_one, grad_bias_one = norm1_back(grad_normed)
    if kernels:
        grad_gain_one, grad_bias_one = norm_sums[0], norm_sums[1]
    grad_input = (grad_resid + input_part)[None]

    def all_places(value):
        return arrange(grid.gather(value, block_steps), place, block_offsets)

    in_whole = all_places(jnp.concatenate(in_grads, axis=0))
    in_whole = in_whole.reshape(blocks, groups_here, share, width)
    in_whole = in_whole.transpose(3, 1, 0, 2).reshape(width, shard_in).astype(WIDE)
    if up_grad.shape[1] == down_grad.shape[1]:
        ff_whole = all_places(jnp.concatenate([up_grad, down_grad], axis=0))
        up_whole, down_whole = ff_whole[:, :piece], ff_whole[:, piece:]
    else:
        up_whole, down_whole = all_places(up_grad), all_places(down_grad)
    up_whole = up_whole.reshape(blocks * piece, width).T.astype(WIDE)
    down_whole = down_whole.reshape(blocks, w_down.shape[1], count_dp, piece)
    down_whole = down_whole.transpose(2, 0, 3, 1).reshape(hidden_width, w_down.shape[1])
    down_whole = down_whole.astype(WIDE)
    out_whole = all_places(out_grad).reshape(blocks, shard_out, bands, share)
    out_whole = out_whole.transpose(2, 0, 3, 1).reshape(width, shard_out).astype(WIDE)

    shared = [
        grad_gain_one,
        grad_bias_one,
        grad_b_out,
        grad_gain_two,
        grad_bias_two,
        grad_b_down,
        filter_grads[0],
        filter_grads[1],
        filter_grads[2],
        filter_grads[3],
    ]
    flat = jnp.concatenate([item.reshape(-1) for item in shared])
    unit = blocks * channels
    chunk = -(-flat.shape[0] // unit)
    flat = jnp.pad(flat, (0, chunk * unit - flat.shape[0])).reshape(blocks, chunk, channels)
    dealt = [lax.dynamic_slice_in_dim(flat, place ^ offset, 1, 0) for offset in block_offsets]
    half = blocks // 2
    shared_part = grid.scatter(
        jnp.concatenate(dealt[:half], axis=0), jnp.concatenate(dealt[half:], axis=0), block_steps
    )
    joined = jnp.concatenate(
        [
            shared_part,
            jnp.pad(grad_b_up_here, (0, -hidden_here % channels)).reshape(-1, channels),
            grad_b_in.reshape(3, channels),
            grad_taps.reshape(9, channels),
            grad_short_bias.reshape(3, channels),
            filter_grads[5][None],
            grad_conv_bias[None],
            filter_grads[4],
        ],
        axis=0,
    )
    for step in dp_steps:
        joined = joined + grid.swap(joined, step)
    every = all_places(joined)
    whole_flat = every[:, :chunk].reshape(-1)
    shared_out, at = [], 0
    for item in shared:
        shared_out.append(whole_flat[at : at + item.size].reshape(item.shape))
        at += item.size
    at = chunk + -(-hidden_here // channels)
    grad_b_up = every[:, chunk:at].reshape(blocks, -1)[:, :hidden_here]
    grad_b_up = grad_b_up.reshape(blocks, count_dp, piece)
    grad_b_up = grad_b_up.transpose(1, 0, 2).reshape(hidden_width)
    rest = every[:, at:].reshape(blocks, -1, bands, share).transpose(1, 2, 0, 3)
    rest = rest.reshape(-1, width)
    return (
        block_out,
        grad_input,
        shared_out[0],
        shared_out[1],
        in_whole,
        rest[:3].reshape(3 * width),
        rest[3:12].reshape(3, 3 * width),
        rest[12:15].reshape(3 * width),
        shared_out[6],
        shared_out[7],
        shared_out[8],
        shared_out[9],
        rest[17:],
        rest[15],
        rest[16],
        out_whole,
        shared_out[2],
        shared_out[3],
        shared_out[4],
        up_whole,
        grad_b_up,
        down_whole,
        shared_out[5],
    )


def solution(mesh):
    placed = (
        P("dp", "block", None),
        P("dp", None),
        P(),
        P(),
        P(None, "dp"),
        P(),
        P(),
        P(),
        P(),
        P(),
        P(),
        P(),
        P(),
        P(),
        P(),
        P(None, "dp"),
        P(),
        P(),
        P(),
        P(None, "dp"),
        P(),
        P(None, "dp"),
        P(),
        P("dp", "block", None),
    )
    return jax.shard_map(
        local,
        mesh=mesh,
        in_specs=placed,
        out_specs=(
            P("dp", "block", None),
            P("dp", "block", None),
            P(),
            P(),
            P(None, "dp"),
            P(),
            P(),
            P(),
            P(),
            P(),
            P(),
            P(),
            P(),
            P(),
            P(),
            P(None, "dp"),
            P(),
            P(),
            P(),
            P(None, "dp"),
            P(),
            P(None, "dp"),
            P(),
        ),
        check_vma=False,
    )
```

time: 515 us -> 427 us (0.83)
  Pallas kernels: 0 us -> 75.7 us
  starting transfers between devices: 156 us -> 107 us
  local copies, waits for them, and re-layouts: 116 us -> 68.2 us
  waiting for transfers between devices: 99.4 us -> 56 us
  matrix products: 66.6 us -> 45.7 us
  other arithmetic: 60 us -> 66.8 us
  between operations: 7.71 us -> 2.48 us
    pallas_call x0 -> x13, Pallas kernels: none -> 75.7 us  [the longest x1 22.8 us: back_call(): pl.pallas_call(body, out_shape=[half_in] * (2 * groups) + [shape((half_bl...]
    ppermute x89 -> x71, starting transfers between devices: 156 us -> 107 us  [swap(): return lax.ppermute(value, ('dp', 'block'), pairs)]
    ppermute x89 -> x71, waiting for transfers between devices: 99.4 us -> 56 us  [swap(): return lax.ppermute(value, ('dp', 'block'), pairs)]
    unnamed x521 -> x197, local copies, waits for them, and re-layouts: 52.3 us -> 10.7 us
    dot_general x14 -> x0, matrix products: 26.9 us -> none  [the longest x8 15.6 us: dot_high(): return jnp.dot(left, right, precision=HIGHEST, preferred_element_type=WIDE)]
    another operation x14 -> x2, local copies, waits for them, and re-layouts: 24.5 us -> 0.62 us  [local(): grad_b_up = grad_b_up.reshape(blocks, count_dp, piece)]
    concatenate x52 -> x27, other arithmetic: 12.5 us -> 24.4 us  [the longest x20 17.1 us: gather(): held = jnp.concatenate(pieces, axis=0)]
    add x23 -> x1, other arithmetic: 9.82 us -> 0.01 us  [add_low(): return (left.astype(WIDE) + right.astype(WIDE)).astype(left.dtype)]
  transfers between devices with their start and end apart: 89 -> 71, of which waited for: 30 -> 23; matrix products, arithmetic and copies ran while one was open for 40% -> 35% of each run, Pallas kernels for 0% -> 17%
where the time goes in v3:
time: 427 us; the launch traced here: 422 us
  starting transfers between devices  107 us (25%)
  Pallas kernels  75.7 us (18%)
  local copies, waits for them, and re-layouts  68.2 us (16%)
  other arithmetic  66.8 us (16%)
  waiting for transfers between devices  56 us (13%)
  matrix products  45.7 us (11%)
    ppermute x71, starting transfers between devices, swap(): return lax.ppermute(value, ('dp', 'block'), pairs)  107 us
    ppermute x71, waiting for transfers between devices, swap(): return lax.ppermute(value, ('dp', 'block'), pairs)  56 us
    pallas_call x1, Pallas kernels, back_call(): pl.pallas_call(body, out_shape=[half_in] * (2 * groups) + [shape((half_bl...  22.8 us
    dot_general x6, matrix products, dot_plain(): return jnp.dot(left, right, preferred_element_type=WIDE)  21.4 us
    concatenate x20, other arithmetic, gather(): held = jnp.concatenate(pieces, axis=0)  17.1 us
    pallas_call x6, Pallas kernels, arrange(): pl.pallas_call(kernel, out_shape=jax.ShapeDtypeStruct((len(offsets), *sha...  14.8 us
    pallas_call x1, Pallas kernels, conv_call(): pl.pallas_call(body, out_shape=[shape((block_len, channels), LOW)] * bloc...  14.1 us
    dot_general x6, matrix products, dot_first(): lax.dot_general(left, right, (((0,), (0,)), ((), ())), preferred_element_...  13.8 us
  transfers between devices with their start and end apart: 71, of which 23 were waited for; matrix products, arithmetic and copies ran while one was open for 35% of the time, Pallas kernels for 17%

profile of v3, /device:TPU:1, one launch (start us, length us, event | category | flops | bytes accessed | tf_op | source)
XLA Modules:
  0.0 421.6 jit_solution(8436905447131483499)
XLA Ops:
  2.3 4.2 %collective-permute-start.8 = (bf16[1,32,1024]{2,1,0:T(8,128)(2,1)S(1)}, bf16[1,32,1024]{2,1,0:T(8,128)(2,1)S(1)}, u32[]{:S(2)}, u32[]{:S(2)}) collective-permute-start(bf16[1,32,1024]{2,1,0:T(8,128)(2,1)S(1)} %get-tuple-element.149.refs_11_), channel_id=1, source_target_pairs={{0,24},{1,25},{2,26},{3,27},{4,28},{5,29},{6,30},{7,31},{8,16},{9,... | collective-permute-start | bytes 196616 | tf_op jit(solution)/shard_map/ppermute | solution.py:128
  28.6 4.9 %collective-permute-start.3 = (bf16[2,32,1024]{2,1,0:T(8,128)(2,1)S(1)}, bf16[2,32,1024]{2,1,0:T(8,128)(2,1)S(1)}, u32[]{:S(2)}, u32[]{:S(2)}) collective-permute-start(bf16[2,32,1024]{2,1,0:T(8,128)(2,1)S(1)} %pad_maximum_fusion.20), channel_id=1, source_target_pairs={{0,8},{1,9},{2,10},{3,11},{4,12},{5,13},{6,14},{7,15},{8,0},{9,1},... | collective-permute-start | bytes 393224 | tf_op jit(solution)/shard_map/ppermute | solution.py:128
  61.5 7.0 %shard_map.470.spectra_ref.refs_4_ = f32[4,512,256]{2,1,0:T(8,128)} custom-call(f32[40,1024]{1,0:T(8,128)} %constant.131.clone.table_ref, f32[40,64]{1,0:T(8,128)} %select_maximum_fusion.1.w1_ref, f32[72,64]{1,0:T(8,128)} %select_maximum_fusion.w2_ref, f32[81,256]{1,0:T(8,128)} %copy.100.vec_ref, bf16[512,768]{1,0:T(8,128)(2,1)} %constant.132.clone.f3_ref), custom_call_target="tpu_custom_call" | custom-call | tf_op jit(solution)/shard_map/pallas_call | solution.py:355
  69.7 14.1 %shard_map.471 = (bf16[256,256]{1,0:T(8,128)(2,1)}, bf16[256,256]{1,0:T(8,128)(2,1)}, bf16[256,256]{1,0:T(8,128)(2,1)}, bf16[256,256]{1,0:T(8,128)(2,1)}, f32[10...) custom-call(s32[2]{0:T(128)} %pad_add_fusion.place_ref, ...), custom_call_target="tpu_custom_call" | custom-call | tf_op jit(solution)/shard_map/pallas_call | solution.py:520
  94.6 3.5 collective-permute-done.18
  106.4 4.1 collective-permute-start.26
  110.5 3.9 collective-permute-done.19
  120.0 9.2 %collective-permute-done.23.refs_3_ = bf16[4,128,1024]{2,1,0:T(8,128)(2,1)} collective-permute-done((bf16[4,128,1024]{2,1,0:T(8,128)(2,1)}, bf16[4,128,1024]{2,1,0:T(8,128)(2,1)}, u32[]{:S(2)}, u32[]{:S(2)}) %collective-permute-start.23) | collective-permute-done | bytes 1048608 | tf_op jit(solution)/shard_map/ppermute | solution.py:128
  139.6 13.7 %convert_reduce_fusion = (f32[1024]{0:T(1024)S(1)}, bf16[1024,1024]{1,0:T(8,128)(2,1)S(1)}, f32[1024,1024]{1,0:T(8,128)}) fusion(f32[1024,1024]{1,0:T(8,128)S(1)} %fusion.77, f32[1024]{0:T(1024)S(1)} %bitcast.305, bf16[1024,1024]{1,0:T(8,128)(2,1)S(1)} %bitcast.281, bf16[1024,1024]{1,0:T(8,128)(2,1)S(1)} %bitcast.284), kind=kOutput, calls=%fused_computation.2 | convolution fusion | flops 2226125824 | bytes 14688256 | tf_op jit(solution)/shard_map/dot_general | solution.py:29
  153.3 3.8 convolution_convert_fusion.1
  157.2 3.7 convolution_convert_fusion.2
  164.8 4.7 %multiply_convert_fusion = bf16[1024,1024]{1,0:T(8,128)(2,1)S(1)} fusion(f32[1024,1024]{1,0:T(8,128)} %get-tuple-element.133, f32[1024,1024]{1,0:T(8,128)} %copy-done.9, f32[1024]{0:T(1024)S(1)} %bitcast.306), kind=kLoop, calls=%fused_computation.4 | loop fusion | flops 4194304 | bytes 10489856 | tf_op jit(solution)/shard_map/convert_element_type | solution.py:1135
  169.6 3.7 convolution_convert_fusion
  179.9 4.3 %collective-permute-start.31 = (bf16[2,256,1024]{2,1,0:T(8,128)(2,1)}, bf16[2,256,1024]{2,1,0:T(8,128)(2,1)}, u32[]{:S(2)}, u32[]{:S(2)}) collective-permute-start(bf16[2,256,1024]{2,1,0:T(8,128)(2,1)} %bitcast.44), channel_id=1, source_target_pairs={{0,1},{1,0},{2,3},{3,2},{4,5},{5,4},{6,7},{7,6},{8,9},{9,8},{10,11... | collective-permute-start | bytes 3145736 | tf_op jit(solution)/shard_map/ppermute | solution.py:128
  184.3 4.6 %convolution_convert_fusion.3 = bf16[1024,1024]{1,0:T(8,128)(2,1)S(1)} fusion(bf16[1024,1024]{1,0:T(8,128)(2,1)} %copy-done.17, bf16[1024,1024]{1,0:T(8,128)(2,1)} %bitcast.283), kind=kOutput, calls=%fused_computation.24 | convolution fusion | flops 2148532224 | bytes 6291456 | tf_op jit(solution)/shard_map/dot_general | solution.py:37
  204.3 6.6 %collective-permute-done.64 = bf16[2,128,1024]{2,1,0:T(8,128)(2,1)S(1)} collective-permute-done((bf16[2,128,1024]{2,1,0:T(8,128)(2,1)S(1)}, bf16[2,128,1024]{2,1,0:T(8,128)(2,1)S(1)}, u32[]{:S(2)}, u32[]{:S(2)}) %collective-permute-start.64) | collective-permute-done | bytes 524320 | tf_op jit(solution)/shard_map/ppermute | solution.py:128
  211.7 7.9 %collective-permute-start.65 = (bf16[1,128,1024]{2,1,0:T(8,128)(2,1)}, bf16[1,128,1024]{2,1,0:T(8,128)(2,1)}, u32[]{:S(2)}, u32[]{:S(2)}) collective-permute-start(bf16[1,128,1024]{2,1,0:T(8,128)(2,1)} %add_convert_fusion.15), channel_id=1, source_target_pairs={{0,8},{1,9},{2,10},{3,11},{4,12},{5,13},{6,14},{7,15},{8,0},{9,1},... | collective-permute-start | bytes 786440 | tf_op jit(solution)/shard_map/ppermute | solution.py:128
  229.9 3.5 collective-permute-start.35
  240.4 22.8 %shard_map.475 = (bf16[4,32,1024]{2,1,0:T(8,128)(2,1)}, bf16[4,32,1024]{2,1,0:T(8,128)(2,1)}, bf16[4,32,1024]{2,1,0:T(8,128)(2,1)}, bf16[4,32,1024]{2,1,0:T(8,12...) custom-call(s32[2]{0:T(128)} %pad_add_fusion.place_ref, ...), custom_call_target="tpu_custom_call" | custom-call | tf_op jit(solution)/shard_map/pallas_call | solution.py:782
  263.2 9.1 %shard_map.476 = (f32[40,64]{1,0:T(8,128)}, f32[72,64]{1,0:T(8,128)}, f32[64,256]{1,0:T(8,128)}, f32[1,256]{1,0:T(1,128)}) custom-call(f32[40,1024]{1,0:T(8,128)} %constant.131.clone.table_ref, f32[40,64]{1,0:T(8,128)} %select_maximum_fusion.1.w1_ref, f32[72,64]{1,0:T(8,128)} %select_maximum_fusion.w2_ref, f32[81,256]{1,0:T(8,128)} %copy.100.vec_ref, ...), custom_call_target="tpu_custom_call" | custom-call | tf_op jit(solution)/shard_map/pallas_call | solution.py:879
  294.2 4.0 collective-permute-done.41
  322.0 3.9 collective-permute-start.44
  387.0 5.2 %collective-permute-done.58 = bf16[4,128,256]{2,1,0:T(8,128)(2,1)S(1)} collective-permute-done((bf16[4,128,256]{2,1,0:T(8,128)(2,1)}, bf16[4,128,256]{2,1,0:T(8,128)(2,1)S(1)}, u32[]{:S(2)}, u32[]{:S(2)}) %collective-permute-start.58) | collective-permute-done | bytes 262176 | tf_op jit(solution)/shard_map/ppermute | solution.py:128
  407.0 3.6 collective-permute-start.62
  (495 shorter events, 263.0 us)
Async XLA Ops:
  2.3 22.4 %collective-permute-start.8 = (bf16[1,32,1024]{2,1,0:T(8,128)(2,1)S(1)}, bf16[1,32,1024]{2,1,0:T(8,128)(2,1)S(1)}, u32[]{:S(2)}, u32[]{:S(2)}) collective-permute-start(bf16[1,32,1024]{2,1,0:T(8,128)(2,1)S(1)} %get-tuple-element.149.refs_11_), channel_id=1, source_target_pairs={{0,24},{1,25},{2,26},{3,27},{4,28},{5,29},{6,30},{7,31},{8,16},{9,... | collective-permute-start | bytes 196616 | tf_op jit(solution)/shard_map/ppermute | solution.py:128
  6.5 22.1 %collective-permute-start.2 = (bf16[1,32,1024]{2,1,0:T(8,128)(2,1)S(1)}, bf16[1,32,1024]{2,1,0:T(8,128)(2,1)S(1)}, u32[]{:S(2)}, u32[]{:S(2)}) collective-permute-start(bf16[1,32,1024]{2,1,0:T(8,128)(2,1)S(1)} %get-tuple-element.151.refs_3_), channel_id=1, source_target_pairs={{0,4},{1,5},{2,6},{3,7},{4,0},{5,1},{6,2},{7,3},{8,12},{9,13},{10,... | collective-permute-start | bytes 196616 | tf_op jit(solution)/shard_map/ppermute | solution.py:128
  7.8 30.8 %collective-permute-start.5 = (bf16[1,32,1024]{2,1,0:T(8,128)(2,1)S(1)}, bf16[1,32,1024]{2,1,0:T(8,128)(2,1)}, u32[]{:S(2)}, u32[]{:S(2)}) collective-permute-start(bf16[1,32,1024]{2,1,0:T(8,128)(2,1)S(1)} %get-tuple-element.150.refs_7_), channel_id=1, source_target_pairs={{0,8},{1,9},{2,10},{3,11},{4,12},{5,13},{6,14},{7,15},{8,0},{9,1},... | collective-permute-start | bytes 196616 | tf_op jit(solution)/shard_map/ppermute | solution.py:128
  35.6 33.7 %collective-permute-start.1 = (bf16[2,256,1024]{2,1,0:T(8,128)(2,1)}, bf16[2,256,1024]{2,1,0:T(8,128)(2,1)}, u32[]{:S(2)}, u32[]{:S(2)}) collective-permute-start(bf16[2,256,1024]{2,1,0:T(8,128)(2,1)} %pad_maximum_fusion.2), channel_id=1, source_target_pairs={{0,1},{1,0},{2,3},{3,2},{4,5},{5,4},{6,7},{7,6},{8,9},{9,8},{10,11... | collective-permute-start | bytes 3145736 | tf_op jit(solution)/shard_map/ppermute | solution.py:128
  46.0 47.2 %collective-permute-start.17 = (bf16[2,1024,256]{2,1,0:T(8,128)(2,1)}, bf16[2,1024,256]{2,1,0:T(8,128)(2,1)}, u32[]{:S(2)}, u32[]{:S(2)}) collective-permute-start(bf16[2,1024,256]{2,1,0:T(8,128)(2,1)} %pad_maximum_fusion.3), channel_id=1, source_target_pairs={{0,1},{1,0},{2,3},{3,2},{4,5},{5,4},{6,7},{7,6},{8,9},{9,8},{10,11... | collective-permute-start | bytes 3145736 | tf_op jit(solution)/shard_map/ppermute | solution.py:128
  47.7 37.2 %collective-permute-start.21 = (bf16[1,128,1024]{2,1,0:T(8,128)(2,1)S(1)}, bf16[1,128,1024]{2,1,0:T(8,128)(2,1)S(1)}, u32[]{:S(2)}, u32[]{:S(2)}) collective-permute-start(bf16[1,128,1024]{2,1,0:T(8,128)(2,1)S(1)} %bitcast.267), channel_id=1, source_target_pairs={{0,8},{1,9},{2,10},{3,11},{4,12},{5,13},{6,14},{7,15},{8,0},{9,1},... | collective-permute-start | bytes 786440 | tf_op jit(solution)/shard_map/ppermute | solution.py:128
  58.5 28.8 %collective-permute-start.24 = (bf16[1,128,1024]{2,1,0:T(8,128)(2,1)S(1)}, bf16[1,128,1024]{2,1,0:T(8,128)(2,1)S(1)}, u32[]{:S(2)}, u32[]{:S(2)}) collective-permute-start(bf16[1,128,1024]{2,1,0:T(8,128)(2,1)S(1)} %bitcast.271), channel_id=1, source_target_pairs={{0,24},{1,25},{2,26},{3,27},{4,28},{5,29},{6,30},{7,31},{8,16},{9,... | collective-permute-start | bytes 786440 | tf_op jit(solution)/shard_map/ppermute | solution.py:128
  69.0 32.6 %collective-permute-start.29 = (bf16[1,256,1024]{2,1,0:T(8,128)(2,1)S(1)}, bf16[1,256,1024]{2,1,0:T(8,128)(2,1)S(1)}, u32[]{:S(2)}, u32[]{:S(2)}) collective-permute-start(bf16[1,256,1024]{2,1,0:T(8,128)(2,1)S(1)} %copy-done.3), channel_id=1, source_target_pairs={{0,2},{1,3},{2,0},{3,1},{4,6},{5,7},{6,4},{7,5},{8,10},{9,11},{10,... | collective-permute-start | bytes 1572872 | tf_op jit(solution)/shard_map/ppermute | solution.py:128
  104.3 24.9 %collective-permute-start.23 = (bf16[4,128,1024]{2,1,0:T(8,128)(2,1)}, bf16[4,128,1024]{2,1,0:T(8,128)(2,1)}, u32[]{:S(2)}, u32[]{:S(2)}) collective-permute-start(bf16[4,128,1024]{2,1,0:T(8,128)(2,1)} %pad_maximum_fusion.5), channel_id=1, source_target_pairs={{0,4},{1,5},{2,6},{3,7},{4,0},{5,1},{6,2},{7,3},{8,12},{9,13},{10,... | collective-permute-start | bytes 3145736 | tf_op jit(solution)/shard_map/ppermute | solution.py:128
  106.4 25.8 %collective-permute-start.26 = (bf16[4,128,1024]{2,1,0:T(8,128)(2,1)}, bf16[4,128,1024]{2,1,0:T(8,128)(2,1)}, u32[]{:S(2)}, u32[]{:S(2)}) collective-permute-start(bf16[4,128,1024]{2,1,0:T(8,128)(2,1)} %pad_maximum_fusion.6), channel_id=1, source_target_pairs={{0,8},{1,9},{2,10},{3,11},{4,12},{5,13},{6,14},{7,15},{8,0},{9,1},... | collective-permute-start | bytes 3145736 | tf_op jit(solution)/shard_map/ppermute | solution.py:128
  163.9 28.8 %collective-permute-start.63 = (bf16[4,128,1024]{2,1,0:T(8,128)(2,1)}, bf16[4,128,1024]{2,1,0:T(8,128)(2,1)}, u32[]{:S(2)}, u32[]{:S(2)}) collective-permute-start(bf16[4,128,1024]{2,1,0:T(8,128)(2,1)} %get-tuple-element.80), channel_id=1, source_target_pairs={{0,4},{1,5},{2,6},{3,7},{4,0},{5,1},{6,2},{7,3},{8,12},{9,13},{10,... | collective-permute-start | bytes 3145736 | tf_op jit(solution)/shard_map/ppermute | solution.py:128
  176.4 21.4 %collective-permute-start.66 = (bf16[4,128,1024]{2,1,0:T(8,128)(2,1)}, bf16[4,128,1024]{2,1,0:T(8,128)(2,1)}, u32[]{:S(2)}, u32[]{:S(2)}) collective-permute-start(bf16[4,128,1024]{2,1,0:T(8,128)(2,1)} %get-tuple-element.82), channel_id=1, source_target_pairs={{0,8},{1,9},{2,10},{3,11},{4,12},{5,13},{6,14},{7,15},{8,0},{9,1},... | collective-permute-start | bytes 3145736 | tf_op jit(solution)/shard_map/ppermute | solution.py:128
  201.4 21.3 %collective-permute-start.32 = (bf16[1,256,1024]{2,1,0:T(8,128)(2,1)S(1)}, bf16[1,256,1024]{2,1,0:T(8,128)(2,1)S(1)}, u32[]{:S(2)}, u32[]{:S(2)}) collective-permute-start(bf16[1,256,1024]{2,1,0:T(8,128)(2,1)S(1)} %fusion.41), channel_id=1, source_target_pairs={{0,2},{1,3},{2,0},{3,1},{4,6},{5,7},{6,4},{7,5},{8,10},{9,11},{10,... | collective-permute-start | bytes 1572872 | tf_op jit(solution)/shard_map/ppermute | solution.py:128
  204.1 20.7 %collective-permute-start.28 = (bf16[1,256,1024]{2,1,0:T(8,128)(2,1)S(1)}, bf16[1,256,1024]{2,1,0:T(8,128)(2,1)S(1)}, u32[]{:S(2)}, u32[]{:S(2)}) collective-permute-start(bf16[1,256,1024]{2,1,0:T(8,128)(2,1)S(1)} %fusion.45), channel_id=1, source_target_pairs={{0,2},{1,3},{2,0},{3,1},{4,6},{5,7},{6,4},{7,5},{8,10},{9,11},{10,... | collective-permute-start | bytes 1572872 | tf_op jit(solution)/shard_map/ppermute | solution.py:128
  211.7 74.8 %collective-permute-start.65 = (bf16[1,128,1024]{2,1,0:T(8,128)(2,1)}, bf16[1,128,1024]{2,1,0:T(8,128)(2,1)}, u32[]{:S(2)}, u32[]{:S(2)}) collective-permute-start(bf16[1,128,1024]{2,1,0:T(8,128)(2,1)} %add_convert_fusion.15), channel_id=1, source_target_pairs={{0,8},{1,9},{2,10},{3,11},{4,12},{5,13},{6,14},{7,15},{8,0},{9,1},... | collective-permute-start | bytes 786440 | tf_op jit(solution)/shard_map/ppermute | solution.py:128
  220.5 67.5 %collective-permute-start.68 = (bf16[1,128,1024]{2,1,0:T(8,128)(2,1)}, bf16[1,128,1024]{2,1,0:T(8,128)(2,1)}, u32[]{:S(2)}, u32[]{:S(2)}) collective-permute-start(bf16[1,128,1024]{2,1,0:T(8,128)(2,1)} %add_convert_fusion.12), channel_id=1, source_target_pairs={{0,24},{1,25},{2,26},{3,27},{4,28},{5,29},{6,30},{7,31},{8,16},{9,... | collective-permute-start | bytes 786440 | tf_op jit(solution)/shard_map/ppermute | solution.py:128
  280.1 64.0 %collective-permute-start.56 = (bf16[2,1024,256]{2,1,0:T(8,128)(2,1)}, bf16[2,1024,256]{2,1,0:T(8,128)(2,1)}, u32[]{:S(2)}, u32[]{:S(2)}) collective-permute-start(bf16[2,1024,256]{2,1,0:T(8,128)(2,1)} %pad_maximum_fusion.8), channel_id=1, source_target_pairs={{0,1},{1,0},{2,3},{3,2},{4,5},{5,4},{6,7},{7,6},{8,9},{9,8},{10,11... | collective-permute-start | bytes 3145736 | tf_op jit(solution)/shard_map/ppermute | solution.py:128
  298.3 53.9 %collective-permute-start.36 = (bf16[2,256,1024]{2,1,0:T(8,128)(2,1)}, bf16[2,256,1024]{2,1,0:T(8,128)(2,1)}, u32[]{:S(2)}, u32[]{:S(2)}) collective-permute-start(bf16[2,256,1024]{2,1,0:T(8,128)(2,1)} %get-tuple-element.63), channel_id=1, source_target_pairs={{0,1},{1,0},{2,3},{3,2},{4,5},{5,4},{6,7},{7,6},{8,9},{9,8},{10,11... | collective-permute-start | bytes 3145736 | tf_op jit(solution)/shard_map/ppermute | solution.py:128
  299.5 68.4 %collective-permute-start.69 = (bf16[1,256,1024]{2,1,0:T(8,128)(2,1)}, bf16[1,256,1024]{2,1,0:T(8,128)(2,1)}, u32[]{:S(2)}, u32[]{:S(2)}) collective-permute-start(bf16[1,256,1024]{2,1,0:T(8,128)(2,1)} %maximum_bitcast_fusion.refs_0_), channel_id=1, source_target_pairs={{0,2},{1,3},{2,0},{3,1},{4,6},{5,7},{6,4},{7,5},{8,10},{9,11},{10,... | collective-permute-start | bytes 1572872 | tf_op jit(solution)/shard_map/ppermute | solution.py:128
  326.1 21.0 %collective-permute-start.54 = (bf16[1,96,1024]{2,1,0:T(8,128)(2,1)S(1)}, bf16[1,96,1024]{2,1,0:T(8,128)(2,1)}, u32[]{:S(2)}, u32[]{:S(2)}) collective-permute-start(bf16[1,96,1024]{2,1,0:T(8,128)(2,1)S(1)} %maximum_bitcast_fusion.1.refs_0_), channel_id=1, source_target_pairs={{0,2},{1,3},{2,0},{3,1},{4,6},{5,7},{6,4},{7,5},{8,10},{9,11},{10,... | collective-permute-start | bytes 589832 | tf_op jit(solution)/shard_map/ppermute | solution.py:128
  346.5 31.8 %collective-permute-start.57 = (bf16[1,1024,256]{2,1,0:T(8,128)(2,1)}, bf16[1,1024,256]{2,1,0:T(8,128)(2,1)}, u32[]{:S(2)}, u32[]{:S(2)}) collective-permute-start(bf16[1,1024,256]{2,1,0:T(8,128)(2,1)} %fusion.30), channel_id=1, source_target_pairs={{0,2},{1,3},{2,0},{3,1},{4,6},{5,7},{6,4},{7,5},{8,10},{9,11},{10,... | collective-permute-start | bytes 1572872 | tf_op jit(solution)/shard_map/ppermute | solution.py:128
  348.7 21.8 %collective-permute-start.55 = (bf16[2,96,1024]{2,1,0:T(8,128)(2,1)}, bf16[2,96,1024]{2,1,0:T(8,128)(2,1)}, u32[]{:S(2)}, u32[]{:S(2)}) collective-permute-start(bf16[2,96,1024]{2,1,0:T(8,128)(2,1)} %pad_maximum_fusion.14), channel_id=1, source_target_pairs={{0,1},{1,0},{2,3},{3,2},{4,5},{5,4},{6,7},{7,6},{8,9},{9,8},{10,11... | collective-permute-start | bytes 1179656 | tf_op jit(solution)/shard_map/ppermute | solution.py:128
  354.2 30.5 %collective-permute-start.37 = (bf16[1,256,1024]{2,1,0:T(8,128)(2,1)}, bf16[1,256,1024]{2,1,0:T(8,128)(2,1)}, u32[]{:S(2)}, u32[]{:S(2)}) collective-permute-start(bf16[1,256,1024]{2,1,0:T(8,128)(2,1)} %add_convert_fusion.6), channel_id=1, source_target_pairs={{0,2},{1,3},{2,0},{3,1},{4,6},{5,7},{6,4},{7,5},{8,10},{9,11},{10,... | collective-permute-start | bytes 1572872 | tf_op jit(solution)/shard_map/ppermute | solution.py:128
  370.3 27.2 %collective-permute-start.70 = (bf16[2,256,1024]{2,1,0:T(8,128)(2,1)}, bf16[2,256,1024]{2,1,0:T(8,128)(2,1)}, u32[]{:S(2)}, u32[]{:S(2)}) collective-permute-start(bf16[2,256,1024]{2,1,0:T(8,128)(2,1)} %pad_maximum_fusion.9), channel_id=1, source_target_pairs={{0,1},{1,0},{2,3},{3,2},{4,5},{5,4},{6,7},{7,6},{8,9},{9,8},{10,11... | collective-permute-start | bytes 3145736 | tf_op jit(solution)/shard_map/ppermute | solution.py:128
  (143 other events, 1896.2 us)
